TPU v7x, 32 devices: a whole 2x2x4 slice. The times are simulated.
32 devices in a mesh: section: 2 (over y), tensor: 4 (over x, core), dp: 4 (over z).
Axes of the slice: x: 2, y: 2, z: 4, core: 2. Of those that a mesh axis runs over, the one named last changes fastest.
Arguments:
- inputs: bfloat16 [8, 1024, 1024], P('dp', 'tensor'), may hold values from -6 to 6
- out_grad: bfloat16 [8, 1024, 1024], P('dp', 'tensor'), may hold values from -6 to 6
- lang_ids: int32 [8], P('dp'), may hold values from 0 to 45
- lang_weights: int32 [46], replicated, may hold values from 1 to 64
- ln1_gain: float32 [2, 1024], P('section'), may hold values from 0.5 to 1.5
- ln1_bias: float32 [2, 1024], P('section'), may hold values from -1.2 to 1.2
- w_qkv: bfloat16 [2, 1024, 3, 1024], P('section', 'dp', None, 'tensor'), may hold values from -0.1875 to 0.1875
- b_qv: float32 [2, 2, 1024], P('section', None, 'tensor'), may hold values from -1.2 to 1.2
- w_out: bfloat16 [2, 1024, 1024], P('section', 'tensor', 'dp'), may hold values from -0.75 to 0.75
- b_out: float32 [2, 1024], P('section'), may hold values from -1.2 to 1.2
- ln2_gain: float32 [2, 1024], P('section'), may hold values from 0.5 to 1.5
- ln2_bias: float32 [2, 1024], P('section'), may hold values from -1.2 to 1.2
- w_up: bfloat16 [2, 1024, 4096], P('section', 'dp', 'tensor'), may hold values from -0.1875 to 0.1875
- b_up: float32 [2, 4096], P('section', 'tensor'), may hold values from -1.2 to 1.2
- w_down: bfloat16 [2, 4096, 1024], P('section', 'tensor', 'dp'), may hold values from -0.125 to 0.125
- b_down: float32 [2, 1024], P('section'), may hold values from -1.2 to 1.2
Outputs:
- acts: bfloat16 [2, 8, 1024, 1024], P('section', 'dp', 'tensor')
- in_grads: float32 [2, 8, 1024, 1024], P('section', 'dp', 'tensor')
- grad_ln1_gain: float32 [2, 1024], P('section', ('tensor', 'dp'))
- grad_ln1_bias: float32 [2, 1024], P('section', ('tensor', 'dp'))
- grad_w_qkv: float32 [2, 1024, 3, 1024], P('section', 'dp', None, 'tensor')
- grad_b_qv: float32 [2, 2, 1024], P('section', None, ('tensor', 'dp'))
- grad_w_out: float32 [2, 1024, 1024], P('section', 'tensor', 'dp')
- grad_b_out: float32 [2, 1024], P('section', ('tensor', 'dp'))
- grad_ln2_gain: float32 [2, 1024], P('section', ('tensor', 'dp'))
- grad_ln2_bias: float32 [2, 1024], P('section', ('tensor', 'dp'))
- grad_w_up: float32 [2, 1024, 4096], P('section', 'dp', 'tensor')
- grad_b_up: float32 [2, 4096], P('section', ('tensor', 'dp'))
- grad_w_down: float32 [2, 4096, 1024], P('section', 'tensor', 'dp')
- grad_b_down: float32 [2, 1024], P('section', ('tensor', 'dp'))
Inputs may be any that keep to these rules, and one draw needn't show every extreme that they name: `lang_ids`: each row's language.
All inputs are finite; a program needn't handle non-finite values.
Results may differ from a plain program's by a relative error of at most 0.024.
Values may be sent and summed in bfloat16 or wider, within the bound.
A program may use at most 256 MiB of HBM per device.

v0:
```python
from functools import reduce

import jax
import jax.numpy as jnp
from jax import lax
from jax.sharding import PartitionSpec as P

HEADS = 16
HEAD = 64


EPSILON = 1e-05
GELU_SCALE = 0.7978845608028654


def passed_along(value, axis, steps):
    count = lax.axis_size(axis)
    initial, last = (max(0, -steps), min(count, count - steps))
    return lax.ppermute(value, axis, [(source, source + steps) for source in range(initial, last)])


def layer_norm(values, gain, shift):
    center = values - jnp.mean(values, axis=-1, keepdims=True)
    spread = jnp.mean(center * center, axis=-1, keepdims=True)
    return center * lax.rsqrt(spread + EPSILON) * gain + shift


def gelu_tanh(values):
    return (
        0.5 * values * (1.0 + jnp.tanh(GELU_SCALE * (values + 0.044715 * values * values * values)))
    )


def add_trees(left, right):
    return jax.tree.map(jnp.add, left, right)


def per_device(
    inputs,
    out_grad,
    lang_ids,
    lang_weights,
    ln1_gain,
    ln1_bias,
    w_qkv,
    b_qv,
    w_out,
    b_out,
    ln2_gain,
    ln2_bias,
    w_up,
    b_up,
    w_down,
    b_down,
):
    section_index = lax.axis_index("section")
    tensor_count = lax.axis_size("tensor")
    micro_count, seg_rows, width = inputs.shape
    length = seg_rows * tensor_count
    query_block = min(512, length // 2)
    block_count = length // query_block
    local_width = w_qkv.shape[3]
    local_heads = local_width // HEAD
    head_ids = lax.axis_index("tensor") * local_heads + jnp.arange(local_heads, dtype=jnp.int32)
    slopes = jnp.exp2(-8.0 * (head_ids.astype(jnp.float32) + 1.0) / HEADS)
    qkv_full, up_full, out_full, down_full = (
        lax.all_gather(w_qkv[0], "dp", axis=0, tiled=True),
        lax.all_gather(w_up[0], "dp", axis=0, tiled=True),
        lax.all_gather(w_out[0], "dp", axis=1, tiled=True),
        lax.all_gather(w_down[0], "dp", axis=1, tiled=True),
    )
    first_gain = ln1_gain[0]
    first_shift = ln1_bias[0]
    second_gain = ln2_gain[0]
    second_shift = ln2_bias[0]
    bias_rows = jnp.stack([b_qv[0, 0], jnp.zeros_like(b_qv[0, 0]), b_qv[0, 1]])
    out_bias = b_out[0]
    up_bias = b_up[0]
    down_bias = b_down[0]

    def alibi_bias(block_index):
        rows = block_index * query_block + jnp.arange(query_block, dtype=jnp.int32)
        columns = jnp.arange((block_index + 1) * query_block, dtype=jnp.int32)
        offset = rows[:, None] - columns[None, :]
        return (offset[None] >= 0, -slopes[:, None, None] * offset.astype(jnp.float32)[None])

    def block_scores(queries, keys, block_index):
        allowed, penalty = alibi_bias(block_index)
        block_queries = queries[block_index * query_block : (block_index + 1) * query_block]
        key_rows = keys[: (block_index + 1) * query_block]
        scores = (
            jnp.einsum("qhe,khe->hqk", block_queries, key_rows, preferred_element_type=jnp.float32)
            * 0.125
            + penalty
        )
        return jnp.where(allowed, scores, -1e30)

    def split_heads(projected):
        return (
            projected[:, 0].reshape(length, local_heads, HEAD),
            projected[:, 1].reshape(length, local_heads, HEAD),
            projected[:, 2].reshape(length, local_heads, HEAD),
        )

    matches = lang_ids[:, None] == jnp.arange(lang_weights.shape[0], dtype=jnp.int32)[None, :]
    row_scale = (
        jnp.sum(jnp.where(matches, lang_weights[None, :], 0), axis=1).astype(jnp.float32) / 64.0
    )
    targets = out_grad.astype(jnp.float32) * row_scale[:, None, None]
    tick_count = micro_count + 1
    received = jnp.zeros((seg_rows, width), jnp.bfloat16)
    sent_list = []
    saved_list = []
    for tick_index in range(tick_count):
        own_rows = inputs[min(tick_index, micro_count - 1)]
        entering = jnp.where(section_index == 0, own_rows, received)
        hidden = entering.astype(jnp.float32)
        normed = layer_norm(hidden, first_gain, first_shift).astype(jnp.bfloat16)
        gathered = lax.all_gather(normed, "tensor", axis=0, tiled=True)
        forward_projected = jnp.einsum(
            "td,dch->tch", gathered, qkv_full, preferred_element_type=jnp.float32
        )
        forward_projected = (forward_projected + bias_rows).astype(jnp.bfloat16)
        forward_queries, forward_keys, forward_values = split_heads(forward_projected)
        saved_probs = []
        saved_totals = []
        context_parts = []
        for forward_block_index in range(block_count):
            forward_scores = block_scores(forward_queries, forward_keys, forward_block_index)
            highest = jnp.max(forward_scores, axis=-1, keepdims=True)
            weights = jnp.exp(forward_scores - highest)
            total = jnp.sum(weights, axis=-1, keepdims=True)
            forward_probs = weights / total
            saved_totals.append(highest + jnp.log(total))
            value_rows = forward_values[: (forward_block_index + 1) * query_block]
            context_parts.append(
                jnp.einsum(
                    "hqk,khe->qhe",
                    forward_probs.astype(jnp.bfloat16),
                    value_rows,
                    preferred_element_type=jnp.float32,
                )
            )
        context = (
            jnp.concatenate(context_parts, 0).reshape(length, local_width).astype(jnp.bfloat16)
        )
        attended = lax.psum_scatter(
            jnp.dot(context, out_full, preferred_element_type=jnp.float32).astype(jnp.bfloat16),
            "tensor",
            scatter_dimension=0,
            tiled=True,
        ).astype(jnp.float32)
        middle = hidden + attended + out_bias
        second = layer_norm(middle, second_gain, second_shift).astype(jnp.bfloat16)
        forward_second_all = lax.all_gather(second, "tensor", axis=0, tiled=True)
        upward = jnp.dot(forward_second_all, up_full, preferred_element_type=jnp.float32) + up_bias
        activated = gelu_tanh(upward).astype(jnp.bfloat16)
        downward = lax.psum_scatter(
            jnp.dot(activated, down_full, preferred_element_type=jnp.float32).astype(jnp.bfloat16),
            "tensor",
            scatter_dimension=0,
            tiled=True,
        ).astype(jnp.float32)
        forward_saved = {
            "hidden": hidden,
            "middle": middle,
            "normed": gathered,
            "projected": forward_projected,
            "probs": saved_probs,
            "totals": saved_totals,
            "context": context,
            "second": forward_second_all,
            "upward": upward,
            "activated": activated,
        }
        leaving = middle + downward + down_bias
        saved = forward_saved
        leaving = leaving.astype(jnp.bfloat16)
        sent_list.append(leaving)
        saved_list.append(saved)
        if tick_index + 1 < tick_count:
            received = passed_along(leaving, "section", 1)
    grad_received = jnp.zeros((seg_rows, width), jnp.bfloat16)
    grads_by_slot = [None] * tick_count
    small_by_slot = [None] * tick_count
    large_by_slot = [None] * tick_count
    for back_index in range(tick_count):
        later = micro_count - 1 - back_index
        own_grad = targets[max(later, 0)]
        valid = jnp.where(section_index == 1, jnp.asarray(later >= 0), jnp.asarray(back_index >= 1))
        incoming = jnp.where(section_index == 1, own_grad, grad_received.astype(jnp.float32))
        incoming = jnp.where(valid, incoming, 0.0)
        slot = micro_count - back_index
        backward_saved = saved_list[slot]
        down_rows = lax.all_gather(incoming.astype(jnp.bfloat16), "tensor", axis=0, tiled=True)
        grad_act = jnp.einsum("td,fd->tf", down_rows, down_full, preferred_element_type=jnp.float32)
        unused_value, gelu_pull = jax.vjp(gelu_tanh, backward_saved["upward"])
        grad_up = gelu_pull(grad_act)[0].astype(jnp.bfloat16)
        grad_second = lax.psum_scatter(
            jnp.einsum("tf,df->td", grad_up, up_full, preferred_element_type=jnp.float32).astype(
                jnp.bfloat16
            ),
            "tensor",
            scatter_dimension=0,
            tiled=True,
        ).astype(jnp.float32)
        unused_norm, second_pull = jax.vjp(
            layer_norm, backward_saved["middle"], second_gain, second_shift
        )
        grad_middle_norm, grad_second_gain, grad_second_shift = second_pull(grad_second)
        grad_middle = incoming + grad_middle_norm
        attn_rows = lax.all_gather(grad_middle.astype(jnp.bfloat16), "tensor", axis=0, tiled=True)
        grad_context = jnp.einsum(
            "td,hd->th", attn_rows, out_full, preferred_element_type=jnp.float32
        ).astype(jnp.bfloat16)
        grad_context = grad_context.reshape(length, local_heads, HEAD)
        backward_queries, backward_keys, values = split_heads(backward_saved["projected"])
        query_parts = []
        grad_keys = jnp.zeros((length, local_heads, HEAD), jnp.float32)
        grad_values = jnp.zeros((length, local_heads, HEAD), jnp.float32)
        for backward_block_index in range(block_count):
            key_count = (backward_block_index + 1) * query_block
            probs = jnp.exp(
                block_scores(backward_queries, backward_keys, backward_block_index)
                - backward_saved["totals"][backward_block_index]
            )
            block_grad = grad_context[backward_block_index * query_block : key_count]
            backward_block_queries = backward_queries[
                backward_block_index * query_block : key_count
            ]
            grad_probs = jnp.einsum(
                "qhe,khe->hqk", block_grad, values[:key_count], preferred_element_type=jnp.float32
            )
            inner = jnp.sum(probs * grad_probs, axis=-1, keepdims=True)
            grad_scores = (probs * (grad_probs - inner)).astype(jnp.bfloat16)
            query_parts.append(
                jnp.einsum(
                    "hqk,khe->qhe",
                    grad_scores,
                    backward_keys[:key_count],
                    preferred_element_type=jnp.float32,
                )
                * 0.125
            )
            tail = ((0, length - key_count), (0, 0), (0, 0))
            grad_keys = grad_keys + jnp.pad(
                jnp.einsum(
                    "hqk,qhe->khe",
                    grad_scores,
                    backward_block_queries,
                    preferred_element_type=jnp.float32,
                )
                * 0.125,
                tail,
            )
            grad_values = grad_values + jnp.pad(
                jnp.einsum(
                    "hqk,qhe->khe",
                    probs.astype(jnp.bfloat16),
                    block_grad,
                    preferred_element_type=jnp.float32,
                ),
                tail,
            )
        grad_queries = jnp.concatenate(query_parts, 0)
        grad_projected = jnp.stack(
            [
                grad_queries.reshape(length, local_width),
                grad_keys.reshape(length, local_width),
                grad_values.reshape(length, local_width),
            ],
            axis=1,
        ).astype(jnp.bfloat16)
        grad_qkv_bias = jnp.sum(grad_projected[:, 0::2].astype(jnp.float32), axis=0)
        grad_normed = lax.psum_scatter(
            jnp.einsum(
                "tch,dch->td", grad_projected, qkv_full, preferred_element_type=jnp.float32
            ).astype(jnp.bfloat16),
            "tensor",
            scatter_dimension=0,
            tiled=True,
        ).astype(jnp.float32)
        unused_first, first_pull = jax.vjp(
            layer_norm, backward_saved["hidden"], first_gain, first_shift
        )
        grad_hidden_norm, grad_first_gain, grad_first_shift = first_pull(grad_normed)
        grad_hidden = grad_middle + grad_hidden_norm
        small = (
            grad_first_gain,
            grad_first_shift,
            jnp.sum(grad_middle, axis=0),
            grad_second_gain,
            grad_second_shift,
            jnp.sum(incoming, axis=0),
        )
        large = (
            grad_projected,
            attn_rows,
            grad_up,
            down_rows,
            grad_qkv_bias,
            jnp.sum(grad_up.astype(jnp.float32), axis=0),
        )
        grad_hidden, small, large = (grad_hidden, small, large)
        grads_by_slot[slot] = grad_hidden
        small_by_slot[slot] = small
        large_by_slot[slot] = large
        if back_index + 1 < tick_count:
            grad_received = passed_along(grad_hidden.astype(jnp.bfloat16), "section", -1)
    first_section = section_index == 0

    def pick(items):
        return jnp.stack(
            [
                jnp.where(first_section, items[micro_index], items[micro_index + 1])
                for micro_index in range(micro_count)
            ]
        )

    acts_out = pick(sent_list)[None]
    grads_out = pick(grads_by_slot)[None]
    small_total = reduce(add_trees, small_by_slot)
    small_shards = lax.psum_scatter(small_total, ("tensor", "dp"), scatter_dimension=0, tiled=True)
    normed_all = pick([saved["normed"] for saved in saved_list])
    context_all = pick([saved["context"] for saved in saved_list])
    second_all = pick([saved["second"] for saved in saved_list])
    activated_all = pick([saved["activated"] for saved in saved_list])
    large_all = tuple((pick([large[member] for large in large_by_slot]) for member in range(6)))
    grad_qkv = jnp.einsum(
        "mtd,mtch->dch", normed_all, large_all[0], preferred_element_type=jnp.float32
    )
    grad_outw = jnp.einsum(
        "mth,mtd->hd", context_all, large_all[1], preferred_element_type=jnp.float32
    )
    grad_upw = jnp.einsum(
        "mtd,mtf->df", second_all, large_all[2], preferred_element_type=jnp.float32
    )
    grad_downw = jnp.einsum(
        "mtf,mtd->fd", activated_all, large_all[3], preferred_element_type=jnp.float32
    )
    bias_qkv = jnp.sum(large_all[4], axis=0)
    bias_up = jnp.sum(large_all[5], axis=0)
    return (
        acts_out,
        grads_out,
        small_shards[0][None],
        small_shards[1][None],
        lax.psum_scatter(
            grad_qkv.astype(jnp.bfloat16), "dp", scatter_dimension=0, tiled=True
        ).astype(jnp.float32)[None],
        lax.psum_scatter(
            bias_qkv.astype(jnp.bfloat16), "dp", scatter_dimension=1, tiled=True
        ).astype(jnp.float32)[None],
        lax.psum_scatter(
            grad_outw.astype(jnp.bfloat16), "dp", scatter_dimension=1, tiled=True
        ).astype(jnp.float32)[None],
        small_shards[2][None],
        small_shards[3][None],
        small_shards[4][None],
        lax.psum_scatter(
            grad_upw.astype(jnp.bfloat16), "dp", scatter_dimension=0, tiled=True
        ).astype(jnp.float32)[None],
        lax.psum_scatter(
            bias_up.astype(jnp.bfloat16), "dp", scatter_dimension=0, tiled=True
        ).astype(jnp.float32)[None],
        lax.psum_scatter(
            grad_downw.astype(jnp.bfloat16), "dp", scatter_dimension=1, tiled=True
        ).astype(jnp.float32)[None],
        small_shards[5][None],
    )


def solution(mesh):
    return jax.shard_map(
        per_device,
        mesh=mesh,
        in_specs=(
            P("dp", "tensor", None),
            P("dp", "tensor", None),
            P("dp"),
            P(),
            P("section", None),
            P("section", None),
            P("section", "dp", None, "tensor"),
            P("section", None, "tensor"),
            P("section", "tensor", "dp"),
            P("section", None),
            P("section", None),
            P("section", None),
            P("section", "dp", "tensor"),
            P("section", "tensor"),
            P("section", "tensor", "dp"),
            P("section", None),
        ),
        out_specs=(
            P("section", "dp", "tensor", None),
            P("section", "dp", "tensor", None),
            P("section", ("tensor", "dp")),
            P("section", ("tensor", "dp")),
            P("section", "dp", None, "tensor"),
            P("section", None, ("tensor", "dp")),
            P("section", "tensor", "dp"),
            P("section", ("tensor", "dp")),
            P("section", ("tensor", "dp")),
            P("section", ("tensor", "dp")),
            P("section", "dp", "tensor"),
            P("section", ("tensor", "dp")),
            P("section", "tensor", "dp"),
            P("section", ("tensor", "dp")),
        ),
        check_vma=False,
    )
```

profile of v0, /device:TPU:0, one launch (start us, length us, event | category | flops | bytes accessed | tf_op | source)
XLA Modules:
  0.0 1378.6 jit_solution(7357244902797506201)
XLA Ops:
  16.4 25.5 %all-gather.1 = bf16[1,256,1024]{2,1,0:T(8,128)(2,1)S(1)} all-gather(bf16[1,256,256]{2,1,0:T(8,128)(2,1)S(1)} %copy-done.107), channel_id=3, replica_groups=mesh['section'=2,'tensor'=4,'dp'=4] {'dp'}, dimensions={2}, use_global_device_ids=true | all-gather | bytes 655360 | tf_op jit(solution)/shard_map/all_gather | solution.py:69
  43.4 14.1 %all-gather.44.cloned.1.call-done = bf16[1,1024,3,256]{1,3,2,0:T(8,128)(2,1)} async-done(((bf16[1,256,3,256]{1,3,2,0:T(8,128)(2,1)}), bf16[1,1024,3,256]{1,3,2,0:T(8,128)(2,1)}) %all-gather.44.cloned.1.call-update) | async-done | bytes 1572880 | tf_op jit(solution)/shard_map/all_gather | solution.py:67
  57.5 24.6 %all-gather.20.cloned.1.call-done = bf16[1024,1024]{1,0:T(8,128)(2,1)} async-done(((bf16[256,1024]{1,0:T(8,128)(2,1)}), bf16[1024,1024]{1,0:T(8,128)(2,1)}) %all-gather.20.cloned.1.call-update) | async-done | bytes 2097168 | tf_op jit(solution)/shard_map/all_gather | solution.py:119
  102.3 30.7 %reduce-scatter.20.cloned.1.call-done = bf16[256,1024]{1,0:T(8,128)(2,1)} async-done(((bf16[1024,1024]{1,0:T(8,128)(2,1)}), bf16[256,1024]{1,0:T(8,128)(2,1)}) %reduce-scatter.20.cloned.1.call-update) | async-done | bytes 524304 | tf_op jit(solution)/shard_map/reduce_scatter | solution.py:147
  138.6 41.8 %all-gather.46.cloned.1.call-done = bf16[1,1024,1024]{2,1,0:T(8,128)(2,1)} async-done(((bf16[1,256,1024]{2,1,0:T(8,128)(2,1)}), bf16[1,1024,1024]{2,1,0:T(8,128)(2,1)}) %all-gather.46.cloned.1.call-update) | async-done | bytes 2097168 | tf_op jit(solution)/shard_map/all_gather | solution.py:68
  180.5 23.4 %all-gather.22.cloned.1.call-done = bf16[1024,1024]{1,0:T(8,128)(2,1)} async-done(((bf16[256,1024]{1,0:T(8,128)(2,1)}), bf16[1024,1024]{1,0:T(8,128)(2,1)}) %all-gather.22.cloned.1.call-update) | async-done | bytes 2097168 | tf_op jit(solution)/shard_map/all_gather | solution.py:155
  203.9 6.5 fusion.118
  210.4 41.2 %all-gather.48.cloned.1.call-done = bf16[1,1024,1024]{2,1,0:T(8,128)(2,1)} async-done(((bf16[1,1024,256]{2,1,0:T(8,128)(2,1)}), bf16[1,1024,1024]{2,1,0:T(8,128)(2,1)}) %all-gather.48.cloned.1.call-update) | async-done | bytes 2097168 | tf_op jit(solution)/shard_map/all_gather | solution.py:70
  251.7 7.0 fusion.139
  258.8 29.7 %reduce-scatter.22.cloned.1.call-done = bf16[256,1024]{1,0:T(8,128)(2,1)} async-done(((bf16[1024,1024]{1,0:T(8,128)(2,1)}), bf16[256,1024]{1,0:T(8,128)(2,1)}) %reduce-scatter.22.cloned.1.call-update) | async-done | bytes 524304 | tf_op jit(solution)/shard_map/reduce_scatter | solution.py:158
  293.3 11.1 collective-permute-done
  306.2 23.7 %all-gather.24.cloned.1.call-done = bf16[1024,1024]{1,0:T(8,128)(2,1)} async-done(((bf16[256,1024]{1,0:T(8,128)(2,1)}), bf16[1024,1024]{1,0:T(8,128)(2,1)}) %all-gather.24.cloned.1.call-update) | async-done | bytes 2097168 | tf_op jit(solution)/shard_map/all_gather | solution.py:119
  351.3 31.6 %reduce-scatter.24.cloned.1.call-done = bf16[256,1024]{1,0:T(8,128)(2,1)} async-done(((bf16[1024,1024]{1,0:T(8,128)(2,1)}), bf16[256,1024]{1,0:T(8,128)(2,1)}) %reduce-scatter.24.cloned.1.call-update) | async-done | bytes 524304 | tf_op jit(solution)/shard_map/reduce_scatter | solution.py:147
  388.2 22.3 %all-gather.26.cloned.1.call-done = bf16[1024,1024]{1,0:T(8,128)(2,1)} async-done(((bf16[256,1024]{1,0:T(8,128)(2,1)}), bf16[1024,1024]{1,0:T(8,128)(2,1)}) %all-gather.26.cloned.1.call-update) | async-done | bytes 2097168 | tf_op jit(solution)/shard_map/all_gather | solution.py:155
  424.3 31.5 %reduce-scatter.26.cloned.1.call-done = bf16[256,1024]{1,0:T(8,128)(2,1)} async-done(((bf16[1024,1024]{1,0:T(8,128)(2,1)}), bf16[256,1024]{1,0:T(8,128)(2,1)}) %reduce-scatter.26.cloned.1.call-update) | async-done | bytes 524304 | tf_op jit(solution)/shard_map/reduce_scatter | solution.py:158
  461.5 11.1 collective-permute-done.1
  474.5 23.5 %all-gather.28.cloned.1.call-done = bf16[1024,1024]{1,0:T(8,128)(2,1)} async-done(((bf16[256,1024]{1,0:T(8,128)(2,1)}), bf16[1024,1024]{1,0:T(8,128)(2,1)}) %all-gather.28.cloned.1.call-update) | async-done | bytes 2097168 | tf_op jit(solution)/shard_map/all_gather | solution.py:119
  519.6 31.6 %reduce-scatter.28.cloned.1.call-done = bf16[256,1024]{1,0:T(8,128)(2,1)} async-done(((bf16[1024,1024]{1,0:T(8,128)(2,1)}), bf16[256,1024]{1,0:T(8,128)(2,1)}) %reduce-scatter.28.cloned.1.call-update) | async-done | bytes 524304 | tf_op jit(solution)/shard_map/reduce_scatter | solution.py:147
  559.2 19.6 %all-gather.30.cloned.1.call-done = bf16[1024,1024]{1,0:T(8,128)(2,1)} async-done(((bf16[256,1024]{1,0:T(8,128)(2,1)}), bf16[1024,1024]{1,0:T(8,128)(2,1)}) %all-gather.30.cloned.1.call-update) | async-done | bytes 2097168 | tf_op jit(solution)/shard_map/all_gather | solution.py:155
  578.8 6.6 fusion.114
  585.4 17.5 %all-gather.32.cloned.1.call-done = bf16[1024,1024]{1,0:T(8,128)(2,1)} async-done(((bf16[256,1024]{1,0:T(8,128)(2,1)}), bf16[1024,1024]{1,0:T(8,128)(2,1)}) %all-gather.32.cloned.1.call-update) | async-done | bytes 2097168 | tf_op jit(solution)/shard_map/all_gather | solution.py:195
  602.9 9.6 convert_reduce_fusion
  617.5 31.5 %reduce-scatter.32.cloned.1.call-done = bf16[256,1024]{1,0:T(8,128)(2,1)} async-done(((bf16[1024,1024]{1,0:T(8,128)(2,1)}), bf16[256,1024]{1,0:T(8,128)(2,1)}) %reduce-scatter.32.cloned.1.call-update) | async-done | bytes 524304 | tf_op jit(solution)/shard_map/reduce_scatter | solution.py:199
  658.5 22.3 %all-gather.34.cloned.1.call-done = bf16[1024,1024]{1,0:T(8,128)(2,1)} async-done(((bf16[256,1024]{1,0:T(8,128)(2,1)}), bf16[1024,1024]{1,0:T(8,128)(2,1)}) %all-gather.34.cloned.1.call-update) | async-done | bytes 2097168 | tf_op jit(solution)/shard_map/all_gather | solution.py:212
  698.3 6.8 multiply_convert_fusion.2
  719.9 31.5 %reduce-scatter.34.cloned.1.call-done = bf16[256,1024]{1,0:T(8,128)(2,1)} async-done(((bf16[1024,1024]{1,0:T(8,128)(2,1)}), bf16[256,1024]{1,0:T(8,128)(2,1)}) %reduce-scatter.34.cloned.1.call-update) | async-done | bytes 524304 | tf_op jit(solution)/shard_map/reduce_scatter | solution.py:275
  759.8 14.3 %collective-permute-done.2 = bf16[256,1024]{1,0:T(8,128)(2,1)S(1)} collective-permute-done((bf16[256,1024]{1,0:T(8,128)(2,1)S(1)}, bf16[256,1024]{1,0:T(8,128)(2,1)S(1)}, u32[]{:S(2)}, u32[]{:S(2)}) %collective-permute-start.2) | collective-permute-done | bytes 524320 | tf_op jit(solution)/shard_map/ppermute | solution.py:19
  775.2 21.6 %all-gather.36.cloned.1.call-done = bf16[1024,1024]{1,0:T(8,128)(2,1)} async-done(((bf16[256,1024]{1,0:T(8,128)(2,1)}), bf16[1024,1024]{1,0:T(8,128)(2,1)}) %all-gather.36.cloned.1.call-update) | async-done | bytes 2097168 | tf_op jit(solution)/shard_map/all_gather | solution.py:195
  796.9 9.6 convert_reduce_fusion.1
  811.6 31.5 %reduce-scatter.36.cloned.1.call-done = bf16[256,1024]{1,0:T(8,128)(2,1)} async-done(((bf16[1024,1024]{1,0:T(8,128)(2,1)}), bf16[256,1024]{1,0:T(8,128)(2,1)}) %reduce-scatter.36.cloned.1.call-update) | async-done | bytes 524304 | tf_op jit(solution)/shard_map/reduce_scatter | solution.py:199
  852.1 22.4 %all-gather.38.cloned.1.call-done = bf16[1024,1024]{1,0:T(8,128)(2,1)} async-done(((bf16[256,1024]{1,0:T(8,128)(2,1)}), bf16[1024,1024]{1,0:T(8,128)(2,1)}) %all-gather.38.cloned.1.call-update) | async-done | bytes 2097168 | tf_op jit(solution)/shard_map/all_gather | solution.py:212
  890.4 6.8 multiply_convert_fusion.1
  910.2 31.5 %reduce-scatter.38.cloned.1.call-done = bf16[256,1024]{1,0:T(8,128)(2,1)} async-done(((bf16[1024,1024]{1,0:T(8,128)(2,1)}), bf16[256,1024]{1,0:T(8,128)(2,1)}) %reduce-scatter.38.cloned.1.call-update) | async-done | bytes 524304 | tf_op jit(solution)/shard_map/reduce_scatter | solution.py:275
  949.0 14.3 %collective-permute-done.3 = bf16[256,1024]{1,0:T(8,128)(2,1)S(1)} collective-permute-done((bf16[256,1024]{1,0:T(8,128)(2,1)S(1)}, bf16[256,1024]{1,0:T(8,128)(2,1)S(1)}, u32[]{:S(2)}, u32[]{:S(2)}) %collective-permute-start.3) | collective-permute-done | bytes 524320 | tf_op jit(solution)/shard_map/ppermute | solution.py:19
  964.7 21.4 %all-gather.40.cloned.1.call-done = bf16[1024,1024]{1,0:T(8,128)(2,1)} async-done(((bf16[256,1024]{1,0:T(8,128)(2,1)}), bf16[1024,1024]{1,0:T(8,128)(2,1)}) %all-gather.40.cloned.1.call-update) | async-done | bytes 2097168 | tf_op jit(solution)/shard_map/all_gather | solution.py:195
  986.1 8.9 convert_reduce_fusion.2
  996.3 5.4 fusion.136
  1001.8 31.5 %reduce-scatter.40.cloned.1.call-done = bf16[256,1024]{1,0:T(8,128)(2,1)} async-done(((bf16[1024,1024]{1,0:T(8,128)(2,1)}), bf16[256,1024]{1,0:T(8,128)(2,1)}) %reduce-scatter.40.cloned.1.call-update) | async-done | bytes 524304 | tf_op jit(solution)/shard_map/reduce_scatter | solution.py:199
  1039.9 7.0 fusion.145
  1052.0 5.8 bitcast_convert_fusion.1
  1083.2 5.7 bitcast_convert_fusion
  1154.3 11.7 all-reduce.11
  1168.9 19.5 %reduce-scatter.50.cloned.1.call-done = bf16[1024,256]{1,0:T(8,128)(2,1)} async-done(((bf16[1024,1024]{1,0:T(8,128)(2,1)}), bf16[1024,256]{1,0:T(8,128)(2,1)}) %reduce-scatter.50.cloned.1.call-update) | async-done | bytes 524304 | tf_op jit(solution)/shard_map/reduce_scatter | solution.py:366
  1190.5 19.2 %reduce-scatter.52.cloned.1.call-done = bf16[64,2]{1,0:T(8,128)(2,1)} async-done(((bf16[256,2]{1,0:T(8,128)(2,1)}), bf16[64,2]{1,0:T(8,128)(2,1)}) %reduce-scatter.52.cloned.1.call-update) | async-done | bytes 272
  1211.0 20.6 %reduce-scatter.46.cloned.1.call-done = bf16[256,256]{1,0:T(8,128)(2,1)} async-done(((bf16[256,1024]{1,0:T(8,128)(2,1)}), bf16[256,256]{1,0:T(8,128)(2,1)}) %reduce-scatter.46.cloned.1.call-update) | async-done | bytes 131088 | tf_op jit(solution)/shard_map/reduce_scatter | solution.py:354
  1233.2 34.2 %reduce-scatter.44.cloned.1.call-done = bf16[256,3,256]{2,0,1:T(8,128)(2,1)} async-done(((bf16[1024,3,256]{2,0,1:T(8,128)(2,1)}), bf16[256,3,256]{2,0,1:T(8,128)(2,1)}) %reduce-scatter.44.cloned.1.call-update) | async-done | bytes 393232 | tf_op jit(solution)/shard_map/reduce_scatter | solution.py:348
  1269.4 31.6 %reduce-scatter.42.cloned.1.call-done = bf16[256,1024]{1,0:T(8,128)(2,1)} async-done(((bf16[1024,1024]{1,0:T(8,128)(2,1)}), bf16[256,1024]{1,0:T(8,128)(2,1)}) %reduce-scatter.42.cloned.1.call-update) | async-done | bytes 524304 | tf_op jit(solution)/shard_map/reduce_scatter | solution.py:275
  1304.1 60.6 %all-reduce.13 = (f32[1024]{0:T(1024)S(1)}, f32[1024]{0:T(1024)S(1)}, f32[1024]{0:T(1024)S(1)}, f32[1024]{0:T(1024)S(1)}, f32[1024]{0:T(1024)S(1)}, /*index=5*/f32[1024]{0:T(1024)S(1)}) all-reduce(f32[1024]{0:T(1024)S(1)} %get-tuple-element.145, ...), channel_id=18, replica_groups=mesh['section'=2,'tensor'=4,'dp'=4] {'tensor','dp'}, use_global_device_ids=true, to_apply=%region_58.59.clone | all-reduce | flops 6144 | bytes 49152
  (631 shorter events, 348.9 us)
Async XLA Ops:
  7.2 50.3 %all-gather.44.cloned.1.call-start = ((), (), s32[]{:S(2)}) async-start(), calls=%async_computation.45 | async-start | bytes 1966080 | tf_op jit(solution)/shard_map/all_gather | solution.py:67
  9.2 72.9 %all-gather.20.cloned.1.call-start = ((), (), s32[]{:S(2)}) async-start(), calls=%async_computation.17 | async-start | bytes 2621440 | tf_op jit(solution)/shard_map/all_gather | solution.py:119
  15.0 118.0 %reduce-scatter.20.cloned.1.call-start = ((), (), s32[]{:S(2)}) async-start(), calls=%async_computation.18 | async-start | bytes 2621440 | tf_op jit(solution)/shard_map/reduce_scatter | solution.py:147
  41.9 475.5 %copy-start.24 = (bf16[1,256,1024]{2,1,0:T(8,128)(2,1)}, bf16[1,256,1024]{2,1,0:T(8,128)(2,1)S(1)}, u32[]{:S(2)}) copy-start(bf16[1,256,1024]{2,1,0:T(8,128)(2,1)S(1)} %all-gather.1) | copy-start | bytes 1572868
  101.4 79.0 %all-gather.46.cloned.1.call-start = ((), (), s32[]{:S(2)}) async-start(), calls=%async_computation.46 | async-start | bytes 2621440 | tf_op jit(solution)/shard_map/all_gather | solution.py:68
  102.0 101.9 %all-gather.22.cloned.1.call-start = ((), (), s32[]{:S(2)}) async-start(), calls=%async_computation.19 | async-start | bytes 2621440 | tf_op jit(solution)/shard_map/all_gather | solution.py:155
  134.3 76.1 %copy-start.116 = (f32[256]{0:T(256)}, f32[256]{0:T(256)S(1)}, u32[]{:S(2)}) copy-start(f32[256]{0:T(256)S(1)} %broadcast_multiply_fusion.4) | copy-start | bytes 3076
  135.8 74.6 %copy-start.149 = (f32[256]{0:T(256)}, f32[256]{0:T(256)S(1)}, u32[]{:S(2)}) copy-start(f32[256]{0:T(256)S(1)} %multiply_reduce_fusion.8) | copy-start | bytes 3076
  135.8 74.6 %copy-start.143 = (f32[256]{0:T(256)}, f32[256]{0:T(256)S(1)}, u32[]{:S(2)}) copy-start(f32[256]{0:T(256)S(1)} %fusion.314) | copy-start | bytes 3076
  138.0 113.6 %all-gather.48.cloned.1.call-start = ((), (), s32[]{:S(2)}) async-start(), calls=%async_computation.47 | async-start | bytes 2621440 | tf_op jit(solution)/shard_map/all_gather | solution.py:70
  138.6 113.1 %copy-start.130 = (f32[1,1024]{1,0:T(1,128)S(1)}, f32[1,1024]{1,0:T(1,128)}, u32[]{:S(2)}) copy-start(f32[1,1024]{1,0:T(1,128)} %param.29) | copy-start | bytes 12292
  138.6 149.9 %reduce-scatter.22.cloned.1.call-start = ((), (), s32[]{:S(2)}) async-start(), calls=%async_computation.20 | async-start | bytes 2621440 | tf_op jit(solution)/shard_map/reduce_scatter | solution.py:158
  258.7 71.1 %all-gather.24.cloned.1.call-start = ((), (), s32[]{:S(2)}) async-start(), calls=%async_computation.21 | async-start | bytes 2621440 | tf_op jit(solution)/shard_map/all_gather | solution.py:119
  289.9 14.5 %collective-permute-start = (bf16[256,1024]{1,0:T(8,128)(2,1)S(1)}, bf16[256,1024]{1,0:T(8,128)(2,1)S(1)}, u32[]{:S(2)}, u32[]{:S(2)}) collective-permute-start(bf16[256,1024]{1,0:T(8,128)(2,1)S(1)} %add_convert_fusion.7), channel_id=1, source_target_pairs={{0,16},{1,17},{2,18},{3,19},{4,20},{5,21},{6,22},{7,23},{8,24},{9,... | collective-permute-start | bytes 1572872 | tf_op jit(solution)/shard_map/ppermute | solution.py:19
  306.1 76.8 %reduce-scatter.24.cloned.1.call-start = ((), (), s32[]{:S(2)}) async-start(), calls=%async_computation.22 | async-start | bytes 2621440 | tf_op jit(solution)/shard_map/reduce_scatter | solution.py:147
  351.3 59.2 %all-gather.26.cloned.1.call-start = ((), (), s32[]{:S(2)}) async-start(), calls=%async_computation.23 | async-start | bytes 2621440 | tf_op jit(solution)/shard_map/all_gather | solution.py:155
  387.8 68.1 %reduce-scatter.26.cloned.1.call-start = ((), (), s32[]{:S(2)}) async-start(), calls=%async_computation.24 | async-start | bytes 2621440 | tf_op jit(solution)/shard_map/reduce_scatter | solution.py:158
  424.3 73.8 %all-gather.28.cloned.1.call-start = ((), (), s32[]{:S(2)}) async-start(), calls=%async_computation.25 | async-start | bytes 2621440 | tf_op jit(solution)/shard_map/all_gather | solution.py:119
  458.3 14.4 %collective-permute-start.1 = (bf16[256,1024]{1,0:T(8,128)(2,1)S(1)}, bf16[256,1024]{1,0:T(8,128)(2,1)S(1)}, u32[]{:S(2)}, u32[]{:S(2)}) collective-permute-start(bf16[256,1024]{1,0:T(8,128)(2,1)S(1)} %get-tuple-element.63), channel_id=1, source_target_pairs={{0,16},{1,17},{2,18},{3,19},{4,20},{5,21},{6,22},{7,23},{8,24},{9,... | collective-permute-start | bytes 1572872 | tf_op jit(solution)/shard_map/ppermute | solution.py:19
  472.9 282.8 %copy-start.3 = (bf16[256,1024]{1,0:T(8,128)(2,1)}, bf16[256,1024]{1,0:T(8,128)(2,1)S(1)}, u32[]{:S(2)}) copy-start(bf16[256,1024]{1,0:T(8,128)(2,1)S(1)} %get-tuple-element.65) | copy-start | bytes 1572868
  474.3 76.8 %reduce-scatter.28.cloned.1.call-start = ((), (), s32[]{:S(2)}) async-start(), calls=%async_computation.26 | async-start | bytes 2621440 | tf_op jit(solution)/shard_map/reduce_scatter | solution.py:147
  519.6 59.2 %all-gather.30.cloned.1.call-start = ((), (), s32[]{:S(2)}) async-start(), calls=%async_computation.27 | async-start | bytes 2621440 | tf_op jit(solution)/shard_map/all_gather | solution.py:155
  556.0 46.9 %all-gather.32.cloned.1.call-start = ((), (), s32[]{:S(2)}) async-start(), calls=%async_computation.29 | async-start | bytes 2621440 | tf_op jit(solution)/shard_map/all_gather | solution.py:195
  557.8 405.4 %copy-start.15 = (f32[2,256,1024]{2,1,0:T(8,128)}, f32[2,256,1024]{2,1,0:T(8,128)S(1)}, u32[]{:S(2)}) copy-start(f32[2,256,1024]{2,1,0:T(8,128)S(1)} %convert_multiply_fusion) | copy-start | bytes 6291460
  558.9 90.2 %reduce-scatter.32.cloned.1.call-start = ((), (), s32[]{:S(2)}) async-start(), calls=%async_computation.30 | async-start | bytes 2621440 | tf_op jit(solution)/shard_map/reduce_scatter | solution.py:199
  617.5 63.3 %all-gather.34.cloned.1.call-start = ((), (), s32[]{:S(2)}) async-start(), calls=%async_computation.31 | async-start | bytes 2621440 | tf_op jit(solution)/shard_map/all_gather | solution.py:212
  658.0 93.4 %reduce-scatter.34.cloned.1.call-start = ((), (), s32[]{:S(2)}) async-start(), calls=%async_computation.32 | async-start | bytes 2621440 | tf_op jit(solution)/shard_map/reduce_scatter | solution.py:275
  719.8 77.0 %all-gather.36.cloned.1.call-start = ((), (), s32[]{:S(2)}) async-start(), calls=%async_computation.33 | async-start | bytes 2621440 | tf_op jit(solution)/shard_map/all_gather | solution.py:195
  758.5 15.6 %collective-permute-start.2 = (bf16[256,1024]{1,0:T(8,128)(2,1)S(1)}, bf16[256,1024]{1,0:T(8,128)(2,1)S(1)}, u32[]{:S(2)}, u32[]{:S(2)}) collective-permute-start(bf16[256,1024]{1,0:T(8,128)(2,1)S(1)} %get-tuple-element.60), channel_id=1, source_target_pairs={{16,0},{17,1},{18,2},{19,3},{20,4},{21,5},{22,6},{23,7},{24,8},{25... | collective-permute-start | bytes 1572872 | tf_op jit(solution)/shard_map/ppermute | solution.py:19
  775.0 68.1 %reduce-scatter.36.cloned.1.call-start = ((), (), s32[]{:S(2)}) async-start(), calls=%async_computation.34 | async-start | bytes 2621440 | tf_op jit(solution)/shard_map/reduce_scatter | solution.py:199
  811.5 63.0 %all-gather.38.cloned.1.call-start = ((), (), s32[]{:S(2)}) async-start(), calls=%async_computation.35 | async-start | bytes 2621440 | tf_op jit(solution)/shard_map/all_gather | solution.py:212
  851.8 90.0 %reduce-scatter.38.cloned.1.call-start = ((), (), s32[]{:S(2)}) async-start(), calls=%async_computation.36 | async-start | bytes 2621440 | tf_op jit(solution)/shard_map/reduce_scatter | solution.py:275
  910.2 75.9 %all-gather.40.cloned.1.call-start = ((), (), s32[]{:S(2)}) async-start(), calls=%async_computation.37 | async-start | bytes 2621440 | tf_op jit(solution)/shard_map/all_gather | solution.py:195
  947.7 15.6 %collective-permute-start.3 = (bf16[256,1024]{1,0:T(8,128)(2,1)S(1)}, bf16[256,1024]{1,0:T(8,128)(2,1)S(1)}, u32[]{:S(2)}, u32[]{:S(2)}) collective-permute-start(bf16[256,1024]{1,0:T(8,128)(2,1)S(1)} %get-tuple-element.58), channel_id=1, source_target_pairs={{16,0},{17,1},{18,2},{19,3},{20,4},{21,5},{22,6},{23,7},{24,8},{25... | collective-permute-start | bytes 1572872 | tf_op jit(solution)/shard_map/ppermute | solution.py:19
  964.2 69.1 %reduce-scatter.40.cloned.1.call-start = ((), (), s32[]{:S(2)}) async-start(), calls=%async_computation.38 | async-start | bytes 2621440 | tf_op jit(solution)/shard_map/reduce_scatter | solution.py:199
  1001.7 87.5 %all-gather.42.cloned.1.call-start = ((), (), s32[]{:S(2)}) async-start(), calls=%async_computation.39 | async-start | bytes 2621440 | tf_op jit(solution)/shard_map/all_gather | solution.py:212
  1039.9 110.6 %reduce-scatter.30.cloned.1.call-start = ((), (), s32[]{:S(2)}) async-start(), calls=%async_computation.28 | async-start | bytes 2621440 | tf_op jit(solution)/shard_map/reduce_scatter | solution.py:158
  1047.0 119.8 %reduce-scatter.48.cloned.1.call-start = ((), (), s32[]{:S(2)}) async-start(), calls=%async_computation.43 | async-start | bytes 2621440 | tf_op jit(solution)/shard_map/reduce_scatter | solution.py:360
  1057.8 130.6 %reduce-scatter.50.cloned.1.call-start = ((), (), s32[]{:S(2)}) async-start(), calls=%async_computation.44 | async-start | bytes 2621440 | tf_op jit(solution)/shard_map/reduce_scatter | solution.py:366
  1088.9 120.7 %reduce-scatter.52.cloned.1.call-start = ((), (), s32[]{:S(2)}) async-start(), calls=%async_computation.48 | async-start | bytes 81920
  1125.4 106.2 %reduce-scatter.46.cloned.1.call-start = ((), (), s32[]{:S(2)}) async-start(), calls=%async_computation.42 | async-start | bytes 655360 | tf_op jit(solution)/shard_map/reduce_scatter | solution.py:354
  1132.7 134.8 %reduce-scatter.44.cloned.1.call-start = ((), (), s32[]{:S(2)}) async-start(), calls=%async_computation.41 | async-start | bytes 1966080 | tf_op jit(solution)/shard_map/reduce_scatter | solution.py:348
  1141.3 159.7 %reduce-scatter.42.cloned.1.call-start = ((), (), s32[]{:S(2)}) async-start(), calls=%async_computation.40 | async-start | bytes 2621440 | tf_op jit(solution)/shard_map/reduce_scatter | solution.py:275
  1150.4 150.5 %copy-start.115 = (f32[256]{0:T(256)S(1)}, f32[256]{0:T(256)}, u32[]{:S(2)}) copy-start(f32[256]{0:T(256)} %copy-done.114) | copy-start | bytes 3076
  1152.1 150.3 %copy-start.146 = (f32[256]{0:T(256)S(1)}, f32[256]{0:T(256)}, u32[]{:S(2)}) copy-start(f32[256]{0:T(256)} %copy-done.145) | copy-start | bytes 3076
  1152.1 150.3 %copy-start.142 = (f32[256]{0:T(256)S(1)}, f32[256]{0:T(256)}, u32[]{:S(2)}) copy-start(f32[256]{0:T(256)} %copy-done.141) | copy-start | bytes 3076
  1152.1 152.0 %copy-start.133 = (f32[1024]{0:T(1024)S(1)}, f32[1024]{0:T(1024)}, u32[]{:S(2)}) copy-start(f32[1024]{0:T(1024)} %get-tuple-element.38) | copy-start | bytes 12292
  1152.2 152.0 %copy-start.134 = (f32[1024]{0:T(1024)S(1)}, f32[1024]{0:T(1024)}, u32[]{:S(2)}) copy-start(f32[1024]{0:T(1024)} %get-tuple-element.26) | copy-start | bytes 12292
  (155 other events, 1770.9 us)
Sparse Core Ops, SparseCore 0:
  10.2 47.2 all-gather.43
  59.6 22.3 all-gather.19
  101.5 31.4 reduce-scatter.19
  134.5 45.9 all-gather.45
  182.5 21.3 all-gather.21
  205.4 46.2 all-gather.47
  258.8 29.6 reduce-scatter.21
  306.2 23.5 all-gather.23
  351.4 31.4 reduce-scatter.23
  387.9 22.5 all-gather.25
  424.4 31.4 reduce-scatter.25
  474.4 23.5 all-gather.27
  519.7 31.4 reduce-scatter.27
  556.1 22.5 all-gather.29
  580.2 22.5 all-gather.31
  617.6 31.4 reduce-scatter.31
  658.2 22.5 all-gather.33
  720.0 31.4 reduce-scatter.33
  775.1 21.6 all-gather.35
  811.7 31.4 reduce-scatter.35
  851.9 22.5 all-gather.37
  910.3 31.4 reduce-scatter.37
  964.3 21.6 all-gather.39
  1001.8 31.4 reduce-scatter.39
  1040.0 22.5 all-gather.41
  1065.0 31.4 reduce-scatter.29
  1098.7 43.8 reduce-scatter.47
  1144.9 43.4 reduce-scatter.49
  1191.3 18.2 reduce-scatter.51
  1211.7 19.8 reduce-scatter.45
  1233.9 33.5 reduce-scatter.43
  1270.6 30.3 reduce-scatter.41
where the time goes:
time: 1390 us; the launch traced here: 1380 us
  waiting for transfers between devices  830 us (60%)
  matrix products  203 us (15%)
  other arithmetic  150 us (11%)
  blocking collectives  97.9 us (7%)
  local copies, waits for them, and re-layouts  66.8 us (5%)
  between operations  18.1 us (1%)
    reduce_scatter x3, waiting for transfers between devices, per_device(): lax.psum_scatter(jnp.einsum('tf,df->td', grad_up, up_full, preferred_elem...  94.6 us
    reduce_scatter x3, waiting for transfers between devices, per_device(): lax.psum_scatter(jnp.einsum('tch,dch->td', grad_projected, qkv_full, pref...  94.6 us
    reduce_scatter x3, waiting for transfers between devices, per_device(): lax.psum_scatter(jnp.dot(context, out_full, preferred_element_type=jnp.fl...  93.8 us
    unnamed x2, blocking collectives  72.4 us
    all_gather x3, waiting for transfers between devices, per_device(): gathered = lax.all_gather(normed, 'tensor', axis=0, tiled=True)  71.8 us
    all_gather x3, waiting for transfers between devices, per_device(): forward_second_all = lax.all_gather(second, 'tensor', axis=0, tiled=True)  65.3 us
    reduce_scatter x3, waiting for transfers between devices, per_device(): lax.psum_scatter(jnp.dot(activated, down_full, preferred_element_type=jnp...  61.3 us
    all_gather x3, waiting for transfers between devices, per_device(): lax.all_gather(incoming.astype(jnp.bfloat16), 'tensor', axis=0, tiled=True)  60.5 us
  transfers between devices with their start and end apart: 36, of which 33 were waited for; matrix products, arithmetic and copies ran while one was open for 10% of the time, Pallas kernels for 0%

commit v1 on v0

v1 whole, which is shorter than its diff:
```python
import jax
import jax.numpy as jnp
from jax import lax
from jax.sharding import PartitionSpec as P

HEADS = 16
HEAD = 64

EPSILON = 1e-05
GELU_SCALE = 0.7978845608028654


def layer_norm(values, gain, shift):
    center = values - jnp.mean(values, axis=-1, keepdims=True)
    spread = jnp.mean(center * center, axis=-1, keepdims=True)
    return center * lax.rsqrt(spread + EPSILON) * gain + shift


def gelu_tanh(values):
    return (
        0.5 * values * (1.0 + jnp.tanh(GELU_SCALE * (values + 0.044715 * values * values * values)))
    )


def swapped(value):
    count = lax.axis_size("section")
    return lax.ppermute(value, "section", [(i, (i + 1) % count) for i in range(count)])


def gather_tokens(value):
    return lax.all_gather(value, "tensor", axis=0, tiled=True)


def scatter_tokens(value):
    return lax.psum_scatter(
        value.astype(jnp.bfloat16), "tensor", scatter_dimension=0, tiled=True
    ).astype(jnp.float32)


def score_bias(slopes, start, rows, columns):
    offset = (start + jnp.arange(rows, dtype=jnp.int32))[:, None] - jnp.arange(
        columns, dtype=jnp.int32
    )[None, :]
    return (offset[None] >= 0, -slopes[:, None, None] * offset.astype(jnp.float32)[None])


def block_scores(queries, keys, slopes, start):
    allowed, penalty = score_bias(slopes, start, queries.shape[0], keys.shape[0])
    scores = (
        jnp.einsum("qhe,khe->hqk", queries, keys, preferred_element_type=jnp.float32) * 0.125
        + penalty
    )
    return jnp.where(allowed, scores, -1e30)


def layer_forward(entering, weights, slopes, query_block):
    hidden = entering.astype(jnp.float32)
    normed = layer_norm(hidden, weights["ln1_gain"], weights["ln1_bias"]).astype(jnp.bfloat16)
    gathered = gather_tokens(normed)
    length = gathered.shape[0]
    local_width = weights["qkv"].shape[2]
    local_heads = local_width // HEAD
    projected = jnp.einsum("td,dch->tch", gathered, weights["qkv"], preferred_element_type=jnp.float32)
    projected = (projected + weights["bias_rows"]).astype(jnp.bfloat16)
    queries, keys, values = [
        projected[:, c].reshape(length, local_heads, HEAD) for c in range(3)
    ]
    totals, parts = [], []
    for start in range(0, length, query_block):
        stop = start + query_block
        scores = block_scores(queries[start:stop], keys[:stop], slopes, start)
        highest = jnp.max(scores, axis=-1, keepdims=True)
        grown = jnp.exp(scores - highest)
        total = jnp.sum(grown, axis=-1, keepdims=True)
        totals.append(highest + jnp.log(total))
        parts.append(
            jnp.einsum(
                "hqk,khe->qhe",
                (grown / total).astype(jnp.bfloat16),
                values[:stop],
                preferred_element_type=jnp.float32,
            )
        )
    context = jnp.concatenate(parts, 0).reshape(length, local_width).astype(jnp.bfloat16)
    attended = scatter_tokens(jnp.dot(context, weights["out"], preferred_element_type=jnp.float32))
    middle = hidden + attended + weights["b_out"]
    second = layer_norm(middle, weights["ln2_gain"], weights["ln2_bias"]).astype(jnp.bfloat16)
    second_all = gather_tokens(second)
    upward = jnp.dot(second_all, weights["up"], preferred_element_type=jnp.float32) + weights["b_up"]
    activated = gelu_tanh(upward).astype(jnp.bfloat16)
    downward = scatter_tokens(
        jnp.dot(activated, weights["down"], preferred_element_type=jnp.float32)
    )
    leaving = (middle + downward + weights["b_down"]).astype(jnp.bfloat16)
    saved = dict(
        hidden=hidden,
        middle=middle,
        normed=gathered,
        projected=projected,
        totals=totals,
        context=context,
        second=second_all,
        upward=upward,
        activated=activated,
    )
    return leaving, saved


def layer_backward(incoming, weights, saved, slopes, query_block):
    down_rows = gather_tokens(incoming.astype(jnp.bfloat16))
    length = down_rows.shape[0]
    grad_act = jnp.einsum("td,fd->tf", down_rows, weights["down"], preferred_element_type=jnp.float32)
    grad_up = jax.vjp(gelu_tanh, saved["upward"])[1](grad_act)[0].astype(jnp.bfloat16)
    grad_second = scatter_tokens(
        jnp.einsum("tf,df->td", grad_up, weights["up"], preferred_element_type=jnp.float32)
    )
    pull = jax.vjp(layer_norm, saved["middle"], weights["ln2_gain"], weights["ln2_bias"])[1]
    grad_norm, grad_gain2, grad_shift2 = pull(grad_second)
    grad_middle = incoming + grad_norm
    attn_rows = gather_tokens(grad_middle.astype(jnp.bfloat16))
    grad_context = jnp.einsum(
        "td,hd->th", attn_rows, weights["out"], preferred_element_type=jnp.float32
    ).astype(jnp.bfloat16)
    local_width = grad_context.shape[1]
    local_heads = local_width // HEAD
    grad_context = grad_context.reshape(length, local_heads, HEAD)
    queries, keys, values = [
        saved["projected"][:, c].reshape(length, local_heads, HEAD) for c in range(3)
    ]
    query_parts = []
    grad_keys = jnp.zeros((length, local_heads, HEAD), jnp.float32)
    grad_values = jnp.zeros((length, local_heads, HEAD), jnp.float32)
    for index, start in enumerate(range(0, length, query_block)):
        stop = start + query_block
        probs = jnp.exp(
            block_scores(queries[start:stop], keys[:stop], slopes, start) - saved["totals"][index]
        )
        block_grad = grad_context[start:stop]
        grad_probs = jnp.einsum(
            "qhe,khe->hqk", block_grad, values[:stop], preferred_element_type=jnp.float32
        )
        inner = jnp.sum(probs * grad_probs, axis=-1, keepdims=True)
        grad_scores = (probs * (grad_probs - inner)).astype(jnp.bfloat16)
        query_parts.append(
            jnp.einsum("hqk,khe->qhe", grad_scores, keys[:stop], preferred_element_type=jnp.float32)
            * 0.125
        )
        tail = ((0, length - stop), (0, 0), (0, 0))
        grad_keys = grad_keys + jnp.pad(
            jnp.einsum(
                "hqk,qhe->khe", grad_scores, queries[start:stop], preferred_element_type=jnp.float32
            )
            * 0.125,
            tail,
        )
        grad_values = grad_values + jnp.pad(
            jnp.einsum(
                "hqk,qhe->khe",
                probs.astype(jnp.bfloat16),
                block_grad,
                preferred_element_type=jnp.float32,
            ),
            tail,
        )
    grad_projected = jnp.stack(
        [
            part.reshape(length, local_width)
            for part in (jnp.concatenate(query_parts, 0), grad_keys, grad_values)
        ],
        axis=1,
    ).astype(jnp.bfloat16)
    grad_normed = scatter_tokens(
        jnp.einsum("tch,dch->td", grad_projected, weights["qkv"], preferred_element_type=jnp.float32)
    )
    pull = jax.vjp(layer_norm, saved["hidden"], weights["ln1_gain"], weights["ln1_bias"])[1]
    grad_norm, grad_gain1, grad_shift1 = pull(grad_normed)
    grad_hidden = grad_middle + grad_norm
    small = jnp.stack(
        [
            grad_gain1,
            grad_shift1,
            jnp.sum(grad_middle, axis=0),
            grad_gain2,
            grad_shift2,
            jnp.sum(incoming, axis=0),
        ]
    )
    large = dict(
        qkv=jnp.einsum("td,tch->dch", saved["normed"], grad_projected, preferred_element_type=jnp.float32),
        out=jnp.einsum("th,td->hd", saved["context"], attn_rows, preferred_element_type=jnp.float32),
        up=jnp.einsum("td,tf->df", saved["second"], grad_up, preferred_element_type=jnp.float32),
        down=jnp.einsum("tf,td->fd", saved["activated"], down_rows, preferred_element_type=jnp.float32),
        b_qv=jnp.sum(grad_projected[:, 0::2].astype(jnp.float32), axis=0),
        b_up=jnp.sum(grad_up.astype(jnp.float32), axis=0),
    )
    return grad_hidden, small, large


def per_device(
    inputs,
    out_grad,
    lang_ids,
    lang_weights,
    ln1_gain,
    ln1_bias,
    w_qkv,
    b_qv,
    w_out,
    b_out,
    ln2_gain,
    ln2_bias,
    w_up,
    b_up,
    w_down,
    b_down,
):
    section = lax.axis_index("section")
    tensor_count = lax.axis_size("tensor")
    layer_count = lax.axis_size("section")
    length = inputs.shape[1] * tensor_count
    query_block = min(512, length // 2)
    local_heads = w_qkv.shape[3] // HEAD
    head_ids = lax.axis_index("tensor") * local_heads + jnp.arange(local_heads, dtype=jnp.int32)
    slopes = jnp.exp2(-8.0 * (head_ids.astype(jnp.float32) + 1.0) / HEADS)

    def both(value):
        other = swapped(value)
        return [jnp.where(section == l, value, other) for l in range(layer_count)]

    def over_dp(value, axis):
        return both(lax.all_gather(value, "dp", axis=axis, tiled=True))

    qkv_all, up_all = over_dp(w_qkv[0], 0), over_dp(w_up[0], 0)
    out_all, down_all = over_dp(w_out[0], 1), over_dp(w_down[0], 1)
    vectors = [
        both(item[0]) for item in (ln1_gain, ln1_bias, b_qv, b_out, ln2_gain, ln2_bias, b_up, b_down)
    ]
    layers = []
    for l in range(layer_count):
        gain1, bias1, qv, bout, gain2, bias2, bup, bdown = [item[l] for item in vectors]
        layers.append(
            dict(
                ln1_gain=gain1,
                ln1_bias=bias1,
                ln2_gain=gain2,
                ln2_bias=bias2,
                qkv=qkv_all[l],
                out=out_all[l],
                up=up_all[l],
                down=down_all[l],
                bias_rows=jnp.stack([qv[0], jnp.zeros_like(qv[0]), qv[1]]),
                b_out=bout,
                b_up=bup,
                b_down=bdown,
            )
        )
    row = lax.dynamic_index_in_dim(inputs, section, 0, keepdims=False)
    target = lax.dynamic_index_in_dim(out_grad, section, 0, keepdims=False)
    lang = lax.dynamic_index_in_dim(lang_ids, section, 0, keepdims=False)
    matches = lang == jnp.arange(lang_weights.shape[0], dtype=jnp.int32)
    scale = jnp.sum(jnp.where(matches, lang_weights, 0)).astype(jnp.float32) / 64.0

    acts, saved = [], []
    for l in range(layer_count):
        row, kept = layer_forward(row, layers[l], slopes, query_block)
        acts.append(row)
        saved.append(kept)
    grads, small, large = [None] * layer_count, [None] * layer_count, [None] * layer_count
    incoming = target.astype(jnp.float32) * scale
    for l in reversed(range(layer_count)):
        grads[l], small[l], large[l] = layer_backward(
            incoming, layers[l], saved[l], slopes, query_block
        )
        incoming = grads[l].astype(jnp.bfloat16).astype(jnp.float32)

    def mine(items):
        return jnp.where(section == 0, items[0], items[1])

    def theirs(items):
        return jnp.where(section == 0, items[1], items[0])

    def rows_of(items):
        own, other = mine(items), swapped(theirs(items))
        return jnp.stack([jnp.where(section == r, own, other) for r in range(layer_count)])[None]

    def reduced(name, axis):
        items = [item[name].astype(jnp.bfloat16) for item in large]
        total = mine(items) + swapped(theirs(items))
        return lax.psum_scatter(total, "dp", scatter_dimension=axis, tiled=True).astype(
            jnp.float32
        )[None]

    small_total = mine(small) + swapped(theirs(small))
    small_shards = lax.psum_scatter(small_total, ("tensor", "dp"), scatter_dimension=1, tiled=True)
    return (
        rows_of(acts),
        rows_of([item.astype(jnp.bfloat16) for item in grads]).astype(jnp.float32),
        small_shards[0][None],
        small_shards[1][None],
        reduced("qkv", 0),
        reduced("b_qv", 1),
        reduced("out", 1),
        small_shards[2][None],
        small_shards[3][None],
        small_shards[4][None],
        reduced("up", 0),
        reduced("b_up", 0),
        reduced("down", 1),
        small_shards[5][None],
    )


def solution(mesh):
    return jax.shard_map(
        per_device,
        mesh=mesh,
        in_specs=(
            P("dp", "tensor", None),
            P("dp", "tensor", None),
            P("dp"),
            P(),
            P("section", None),
            P("section", None),
            P("section", "dp", None, "tensor"),
            P("section", None, "tensor"),
            P("section", "tensor", "dp"),
            P("section", None),
            P("section", None),
            P("section", None),
            P("section", "dp", "tensor"),
            P("section", "tensor"),
            P("section", "tensor", "dp"),
            P("section", None),
        ),
        out_specs=(
            P("section", "dp", "tensor", None),
            P("section", "dp", "tensor", None),
            P("section", ("tensor", "dp")),
            P("section", ("tensor", "dp")),
            P("section", "dp", None, "tensor"),
            P("section", None, ("tensor", "dp")),
            P("section", "tensor", "dp"),
            P("section", ("tensor", "dp")),
            P("section", ("tensor", "dp")),
            P("section", ("tensor", "dp")),
            P("section", "dp", "tensor"),
            P("section", ("tensor", "dp")),
            P("section", "tensor", "dp"),
            P("section", ("tensor", "dp")),
        ),
        check_vma=False,
    )
```

time: 1390 us -> 1060 us (0.76)
  waiting for transfers between devices: 830 us -> 682 us
  blocking collectives: 97.9 us -> 34.8 us
  other arithmetic: 150 us -> 94.3 us
  matrix products: 203 us -> 154 us
  local copies, waits for them, and re-layouts: 66.8 us -> 37 us
  starting transfers between devices: 13.4 us -> 34.4 us
    reduce_scatter x16 -> x12, waiting for transfers between devices: 419 us -> 205 us  [the longest x8 175 us: scatter_tokens(): lax.psum_scatter(value.astype(jnp.bfloat16), 'tensor', scatter_dimension=...]
    ppermute x4 -> x21, waiting for transfers between devices: 50.8 us -> 184 us  [swapped(): lax.ppermute(value, 'section', [(i, (i + 1) % count) for i in range(count)])]
    all_gather x15 -> x11, waiting for transfers between devices: 339 us -> 239 us  [the longest x8 137 us: gather_tokens(): return lax.all_gather(value, 'tensor', axis=0, tiled=True)]
    unnamed x2 -> x1, blocking collectives: 72.4 us -> 11.8 us
    dot_general x64 -> x48, matrix products: 203 us -> 154 us  [the longest x2 17.8 us: layer_backward(): jnp.einsum('td,fd->tf', down_rows, weights['down'], preferred_element_typ...]
    unnamed x33 -> x27, waiting for transfers between devices: 20.7 us -> 53.5 us
    another operation x17 -> x6, other arithmetic: 35.4 us -> 6.82 us  [the longest x3 4.84 us: rows_of(): jnp.stack([jnp.where(section == r, own, other) for r in range(layer_count)])]
    ppermute x4 -> x21, starting transfers between devices: 9.2 us -> 31.3 us  [swapped(): lax.ppermute(value, 'section', [(i, (i + 1) % count) for i in range(count)])]
  transfers between devices with their start and end apart: 36 -> 46, of which waited for: 33 -> 28; matrix products, arithmetic and copies ran while one was open for 10% -> 15% of each run, Pallas kernels for 0% -> 0%
where the time goes in v1:
time: 1060 us; the launch traced here: 1050 us
  waiting for transfers between devices  682 us (64%)
  matrix products  154 us (15%)
  other arithmetic  94.3 us (9%)
  local copies, waits for them, and re-layouts  37 us (3%)
  blocking collectives  34.8 us (3%)
  starting transfers between devices  34.4 us (3%)
  between operations  17.4 us (2%)
    ppermute x21, waiting for transfers between devices, swapped(): lax.ppermute(value, 'section', [(i, (i + 1) % count) for i in range(count)])  184 us
    reduce_scatter x8, waiting for transfers between devices, scatter_tokens(): lax.psum_scatter(value.astype(jnp.bfloat16), 'tensor', scatter_dimension=...  175 us
    all_gather x8, waiting for transfers between devices, gather_tokens(): return lax.all_gather(value, 'tensor', axis=0, tiled=True)  137 us
    all_gather x3, waiting for transfers between devices, over_dp(): return both(lax.all_gather(value, 'dp', axis=axis, tiled=True))  102 us
    unnamed x27, waiting for transfers between devices  53.5 us
    ppermute x21, starting transfers between devices, swapped(): lax.ppermute(value, 'section', [(i, (i + 1) % count) for i in range(count)])  31.3 us
    reduce_scatter x4, waiting for transfers between devices, reduced(): lax.psum_scatter(total, 'dp', scatter_dimension=axis, tiled=True)  29.4 us
    unnamed x204, local copies, waits for them, and re-layouts  26.6 us
  transfers between devices with their start and end apart: 46, of which 28 were waited for; matrix products, arithmetic and copies ran while one was open for 15% of the time, Pallas kernels for 0%

profile of v1, /device:TPU:0, one launch (start us, length us, event | category | flops | bytes accessed | tf_op | source)
XLA Modules:
  0.0 1053.6 jit_solution(4405929299401501654)
XLA Ops:
  19.8 23.1 %all-gather.1 = bf16[1,256,1024]{2,1,0:T(8,128)(2,1)S(1)} all-gather(bf16[1,256,256]{2,1,0:T(8,128)(2,1)} %param.24), channel_id=3, replica_groups=mesh['section'=2,'tensor'=4,'dp'=4] {'dp'}, dimensions={2}, use_global_device_ids=true | all-gather | bytes 655360 | tf_op jit(solution)/shard_map/all_gather | solution.py:231
  43.4 14.6 %all-gather.32.cloned.1.call-done = bf16[1,1024,3,256]{3,1,2,0:T(8,128)(2,1)} async-done(((bf16[1,256,3,256]{3,1,2,0:T(8,128)(2,1)}), bf16[1,1024,3,256]{3,1,2,0:T(8,128)(2,1)}) %all-gather.32.cloned.1.call-update) | async-done | bytes 1572880 | tf_op jit(solution)/shard_map/all_gather | solution.py:231
  61.9 19.5 %all-gather.16.cloned.1.call-done = bf16[1024,1024]{1,0:T(8,128)(2,1)} async-done(((bf16[256,1024]{1,0:T(8,128)(2,1)}), bf16[1024,1024]{1,0:T(8,128)(2,1)}) %all-gather.16.cloned.1.call-update) | async-done | bytes 2097168 | tf_op jit(solution)/shard_map/all_gather | solution.py:31
  81.3 13.1 %collective-permute-done.2 = bf16[1024,3,256]{2,0,1:T(8,128)(2,1)} collective-permute-done((bf16[1024,3,256]{2,0,1:T(8,128)(2,1)}, bf16[1024,3,256]{2,0,1:T(8,128)(2,1)}, u32[]{:S(2)}, u32[]{:S(2)}) %collective-permute-start.2) | collective-permute-done | bytes 1572896 | tf_op jit(solution)/shard_map/ppermute | solution.py:27
  94.4 3.9 add_convert_fusion.1
  121.4 23.8 %reduce-scatter.19.cloned.1.call-done = bf16[256,1024]{1,0:T(8,128)(2,1)} async-done(((bf16[1024,1024]{1,0:T(8,128)(2,1)}), bf16[256,1024]{1,0:T(8,128)(2,1)}) %reduce-scatter.19.cloned.1.call-update) | async-done | bytes 524304 | tf_op jit(solution)/shard_map/reduce_scatter | solution.py:35
  150.1 42.6 %all-gather.34.cloned.1.call-done = bf16[1,1024,1024]{2,1,0:T(8,128)(2,1)} async-done(((bf16[1,256,1024]{2,1,0:T(8,128)(2,1)}), bf16[1,1024,1024]{2,1,0:T(8,128)(2,1)}) %all-gather.34.cloned.1.call-update) | async-done | bytes 2097168 | tf_op jit(solution)/shard_map/all_gather | solution.py:231
  194.1 45.0 %all-gather.36.cloned.1.call-done = bf16[1,1024,1024]{2,1,0:T(8,128)(2,1)} async-done(((bf16[1,1024,256]{2,1,0:T(8,128)(2,1)}), bf16[1,1024,1024]{2,1,0:T(8,128)(2,1)}) %all-gather.36.cloned.1.call-update) | async-done | bytes 2097168 | tf_op jit(solution)/shard_map/all_gather | solution.py:231
  241.2 45.7 %collective-permute-done.9 = f32[1024]{0:T(1024)S(1)} collective-permute-done((f32[1024]{0:T(1024)S(1)}, f32[1024]{0:T(1024)S(1)}, u32[]{:S(2)}, u32[]{:S(2)}) %collective-permute-start.9) | collective-permute-done | bytes 4128 | tf_op jit(solution)/shard_map/ppermute | solution.py:27
  286.9 4.7 fusion.149
  293.7 4.1 convolution_convert_fusion.8
  297.9 4.1 collective-permute-start.11
  304.2 25.9 %reduce-scatter.21.cloned.1.call-done = bf16[256,1024]{1,0:T(8,128)(2,1)} async-done(((bf16[1024,1024]{1,0:T(8,128)(2,1)}), bf16[256,1024]{1,0:T(8,128)(2,1)}) %reduce-scatter.21.cloned.1.call-update) | async-done | bytes 524304 | tf_op jit(solution)/shard_map/reduce_scatter | solution.py:35
  333.4 22.3 %all-gather.20.cloned.1.call-done = bf16[1024,1024]{1,0:T(8,128)(2,1)} async-done(((bf16[256,1024]{1,0:T(8,128)(2,1)}), bf16[1024,1024]{1,0:T(8,128)(2,1)}) %all-gather.20.cloned.1.call-update) | async-done | bytes 2097168 | tf_op jit(solution)/shard_map/all_gather | solution.py:31
  355.7 4.4 add_convert_fusion
  374.6 3.3 convolution_convert_fusion.7
  378.0 30.6 %reduce-scatter.23.cloned.1.call-done = bf16[256,1024]{1,0:T(8,128)(2,1)} async-done(((bf16[1024,1024]{1,0:T(8,128)(2,1)}), bf16[256,1024]{1,0:T(8,128)(2,1)}) %reduce-scatter.23.cloned.1.call-update) | async-done | bytes 524304 | tf_op jit(solution)/shard_map/reduce_scatter | solution.py:35
  418.3 18.0 %all-gather.22.cloned.1.call-done = bf16[1024,1024]{1,0:T(8,128)(2,1)} async-done(((bf16[256,1024]{1,0:T(8,128)(2,1)}), bf16[1024,1024]{1,0:T(8,128)(2,1)}) %all-gather.22.cloned.1.call-update) | async-done | bytes 2097168 | tf_op jit(solution)/shard_map/all_gather | solution.py:31
  436.2 7.1 fusion.151
  443.4 17.7 %all-gather.24.cloned.1.call-done = bf16[1024,1024]{1,0:T(8,128)(2,1)} async-done(((bf16[256,1024]{1,0:T(8,128)(2,1)}), bf16[1024,1024]{1,0:T(8,128)(2,1)}) %all-gather.24.cloned.1.call-update) | async-done | bytes 2097168 | tf_op jit(solution)/shard_map/all_gather | solution.py:31
  461.1 9.3 fusion.194
  471.7 5.3 convolution_convert_fusion.5
  477.2 30.6 %reduce-scatter.27.cloned.1.call-done = bf16[256,1024]{1,0:T(8,128)(2,1)} async-done(((bf16[1024,1024]{1,0:T(8,128)(2,1)}), bf16[256,1024]{1,0:T(8,128)(2,1)}) %reduce-scatter.27.cloned.1.call-update) | async-done | bytes 524304 | tf_op jit(solution)/shard_map/reduce_scatter | solution.py:35
  515.0 22.4 %all-gather.26.cloned.1.call-done = bf16[1024,1024]{1,0:T(8,128)(2,1)} async-done(((bf16[256,1024]{1,0:T(8,128)(2,1)}), bf16[1024,1024]{1,0:T(8,128)(2,1)}) %all-gather.26.cloned.1.call-update) | async-done | bytes 2097168 | tf_op jit(solution)/shard_map/all_gather | solution.py:31
  546.1 4.4 multiply_reduce_fusion.1
  553.2 6.8 multiply_convert_fusion.1
  566.3 5.5 bitcast_convert_fusion.1
  571.9 30.9 %reduce-scatter.29.cloned.1.call-done = bf16[256,1024]{1,0:T(8,128)(2,1)} async-done(((bf16[1024,1024]{1,0:T(8,128)(2,1)}), bf16[256,1024]{1,0:T(8,128)(2,1)}) %reduce-scatter.29.cloned.1.call-update) | async-done | bytes 524304 | tf_op jit(solution)/shard_map/reduce_scatter | solution.py:35
  609.0 22.3 %all-gather.28.cloned.1.call-done = bf16[1024,1024]{1,0:T(8,128)(2,1)} async-done(((bf16[256,1024]{1,0:T(8,128)(2,1)}), bf16[1024,1024]{1,0:T(8,128)(2,1)}) %all-gather.28.cloned.1.call-update) | async-done | bytes 2097168 | tf_op jit(solution)/shard_map/all_gather | solution.py:31
  631.2 8.5 fusion.195
  641.0 3.7 convolution_convert_fusion.4
  644.8 33.4 %reduce-scatter.31.cloned.1.call-done = bf16[256,1024]{1,0:T(8,128)(2,1)} async-done(((bf16[1024,1024]{1,0:T(8,128)(2,1)}), bf16[256,1024]{1,0:T(8,128)(2,1)}) %reduce-scatter.31.cloned.1.call-update) | async-done | bytes 524304 | tf_op jit(solution)/shard_map/reduce_scatter | solution.py:35
  685.0 7.7 convolution_convert_fusion.6
  693.0 14.7 %all-gather.30.cloned.1.call-done = bf16[1024,1024]{1,0:T(8,128)(2,1)} async-done(((bf16[256,1024]{1,0:T(8,128)(2,1)}), bf16[1024,1024]{1,0:T(8,128)(2,1)}) %all-gather.30.cloned.1.call-update) | async-done | bytes 2097168 | tf_op jit(solution)/shard_map/all_gather | solution.py:31
  711.3 5.7 fusion.89
  719.1 3.4 multiply_reduce_fusion.2
  741.5 5.1 bitcast_convert_fusion
  746.8 4.8 convolution_convert_fusion.3
  756.3 46.1 %collective-permute-done.18 = bf16[1024,1024]{1,0:T(8,128)(2,1)S(1)} collective-permute-done((bf16[1024,1024]{1,0:T(8,128)(2,1)S(1)}, bf16[1024,1024]{1,0:T(8,128)(2,1)S(1)}, u32[]{:S(2)}, u32[]{:S(2)}) %collective-permute-start.18) | collective-permute-done | bytes 2097184 | tf_op jit(solution)/shard_map/ppermute | solution.py:27
  804.2 6.0 convolution_convert_fusion.1
  815.2 45.6 %collective-permute-done.20 = bf16[1024,1024]{1,0:T(8,128)(2,1)S(1)} collective-permute-done((bf16[1024,1024]{1,0:T(8,128)(2,1)S(1)}, bf16[1024,1024]{1,0:T(8,128)(2,1)S(1)}, u32[]{:S(2)}, u32[]{:S(2)}) %collective-permute-start.20) | collective-permute-done | bytes 2097184 | tf_op jit(solution)/shard_map/ppermute | solution.py:27
  872.3 3.5 broadcast_select_fusion.26
  880.4 3.6 broadcast_select_fusion.7
  884.6 8.1 collective-permute-done.16
  902.9 22.0 %collective-permute-done.14 = f32[6,1024]{1,0:T(8,128)S(1)} collective-permute-done((f32[6,1024]{1,0:T(8,128)S(1)}, f32[6,1024]{1,0:T(8,128)S(1)}, u32[]{:S(2)}, u32[]{:S(2)}) %collective-permute-start.14) | collective-permute-done | bytes 24608 | tf_op jit(solution)/shard_map/ppermute | solution.py:27
  934.3 11.8 %all-reduce.4 = bf16[1024]{0:T(1024)(128)(2,1)S(1)} all-reduce(bf16[1024]{0:T(1024)(128)(2,1)S(1)} %select_add_fusion.5), channel_id=19, replica_groups=mesh['section'=2,'tensor'=4,'dp'=4] {'dp'}, use_global_device_ids=true, to_apply=%region_58.59.clone | all-reduce | flops 1024 | bytes 4096
  956.7 51.4 %reduce-scatter.43.cloned.1.call-done = f32[64,6]{1,0:T(8,128)} async-done(((f32[1024,6]{1,0:T(8,128)}), f32[64,6]{1,0:T(8,128)}) %reduce-scatter.43.cloned.1.call-update) | async-done | bytes 1552
  1015.4 29.3 %reduce-scatter.35.cloned.1.call-done = bf16[256,3,256]{2,0,1:T(8,128)(2,1)} async-done(((bf16[1024,3,256]{2,0,1:T(8,128)(2,1)}), bf16[256,3,256]{2,0,1:T(8,128)(2,1)}) %reduce-scatter.35.cloned.1.call-update) | async-done | bytes 393232 | tf_op jit(solution)/shard_map/reduce_scatter | solution.py:289
  (444 shorter events, 210.8 us)
Async XLA Ops:
  7.2 50.8 %all-gather.32.cloned.1.call-start = ((), (), s32[]{:S(2)}) async-start(), calls=%async_computation.34 | async-start | bytes 1966080 | tf_op jit(solution)/shard_map/all_gather | solution.py:231
  7.9 73.4 %all-gather.16.cloned.1.call-start = ((), (), s32[]{:S(2)}) async-start(), calls=%async_computation.14 | async-start | bytes 2621440 | tf_op jit(solution)/shard_map/all_gather | solution.py:31
  8.0 6.2 collective-permute-start
  11.0 3.9 collective-permute-start.1
  17.7 127.4 %reduce-scatter.19.cloned.1.call-start = ((), (), s32[]{:S(2)}) async-start(), calls=%async_computation.15 | async-start | bytes 2621440 | tf_op jit(solution)/shard_map/reduce_scatter | solution.py:35
  17.8 44.0 %collective-permute-start.3 = (f32[2,256]{1,0:T(2,128)}, f32[2,256]{1,0:T(2,128)S(1)}, u32[]{:S(2)}, u32[]{:S(2)}) collective-permute-start(f32[2,256]{1,0:T(2,128)} %bitcast.423), channel_id=1, source_target_pairs={{0,16},{16,0},{1,17},{17,1},{2,18},{18,2},{3,19},{19,3},{4,20},{20... | collective-permute-start | bytes 6152 | tf_op jit(solution)/shard_map/ppermute | solution.py:27
  42.9 494.5 %copy-start.18 = (bf16[1,256,1024]{2,1,0:T(8,128)(2,1)}, bf16[1,256,1024]{2,1,0:T(8,128)(2,1)S(1)}, u32[]{:S(2)}) copy-start(bf16[1,256,1024]{2,1,0:T(8,128)(2,1)S(1)} %all-gather.1) | copy-start | bytes 1572868
  42.9 68.1 %collective-permute-start.4 = (bf16[256,1024]{1,0:T(8,128)(2,1)S(1)}, bf16[256,1024]{1,0:T(8,128)(2,1)}, u32[]{:S(2)}, u32[]{:S(2)}) collective-permute-start(bf16[256,1024]{1,0:T(8,128)(2,1)S(1)} %bitcast.352), channel_id=1, source_target_pairs={{0,16},{16,0},{1,17},{17,1},{2,18},{18,2},{3,19},{19,3},{4,20},{20... | collective-permute-start | bytes 1572872 | tf_op jit(solution)/shard_map/ppermute | solution.py:27
  58.0 36.4 %collective-permute-start.2 = (bf16[1024,3,256]{2,0,1:T(8,128)(2,1)}, bf16[1024,3,256]{2,0,1:T(8,128)(2,1)}, u32[]{:S(2)}, u32[]{:S(2)}) collective-permute-start(bf16[1024,3,256]{2,0,1:T(8,128)(2,1)} %bitcast.427), channel_id=1, source_target_pairs={{0,16},{16,0},{1,17},{17,1},{2,18},{18,2},{3,19},{19,3},{4,20},{20... | collective-permute-start | bytes 4718600 | tf_op jit(solution)/shard_map/ppermute | solution.py:27
  113.1 127.6 %copy-start.75 = (f32[1,1024]{1,0:T(1,128)S(1)}, f32[1,1024]{1,0:T(1,128)}, u32[]{:S(2)}) copy-start(f32[1,1024]{1,0:T(1,128)} %param.29) | copy-start | bytes 12292
  113.1 79.6 %all-gather.34.cloned.1.call-start = ((), (), s32[]{:S(2)}) async-start(), calls=%async_computation.35 | async-start | bytes 2621440 | tf_op jit(solution)/shard_map/all_gather | solution.py:231
  113.7 125.5 %all-gather.36.cloned.1.call-start = ((), (), s32[]{:S(2)}) async-start(), calls=%async_computation.36 | async-start | bytes 2621440 | tf_op jit(solution)/shard_map/all_gather | solution.py:231
  114.3 172.6 %all-gather.18.cloned.1.call-start = ((), (), s32[]{:S(2)}) async-start(), calls=%async_computation.16 | async-start | bytes 2621440 | tf_op jit(solution)/shard_map/all_gather | solution.py:31
  114.5 5.2 collective-permute-start.5
  117.7 3.6 collective-permute-start.6
  117.8 3.6 collective-permute-start.7
  150.1 180.1 %reduce-scatter.21.cloned.1.call-start = ((), (), s32[]{:S(2)}) async-start(), calls=%async_computation.17 | async-start | bytes 2621440 | tf_op jit(solution)/shard_map/reduce_scatter | solution.py:35
  192.7 94.2 %collective-permute-start.8 = (bf16[1024,1024]{1,0:T(8,128)(2,1)}, bf16[1024,1024]{1,0:T(8,128)(2,1)}, u32[]{:S(2)}, u32[]{:S(2)}) collective-permute-start(bf16[1024,1024]{1,0:T(8,128)(2,1)} %bitcast.426), channel_id=1, source_target_pairs={{0,16},{16,0},{1,17},{17,1},{2,18},{18,2},{3,19},{19,3},{4,20},{20... | collective-permute-start | bytes 6291464 | tf_op jit(solution)/shard_map/ppermute | solution.py:27
  239.1 52.5 %collective-permute-start.10 = (bf16[1024,1024]{1,0:T(8,128)(2,1)}, bf16[1024,1024]{1,0:T(8,128)(2,1)}, u32[]{:S(2)}, u32[]{:S(2)}) collective-permute-start(bf16[1024,1024]{1,0:T(8,128)(2,1)} %bitcast.425), channel_id=1, source_target_pairs={{0,16},{16,0},{1,17},{17,1},{2,18},{18,2},{3,19},{19,3},{4,20},{20... | collective-permute-start | bytes 6291464 | tf_op jit(solution)/shard_map/ppermute | solution.py:27
  240.7 46.2 %collective-permute-start.9 = (f32[1024]{0:T(1024)S(1)}, f32[1024]{0:T(1024)S(1)}, u32[]{:S(2)}, u32[]{:S(2)}) collective-permute-start(f32[1024]{0:T(1024)S(1)} %bitcast.419), channel_id=1, source_target_pairs={{0,16},{16,0},{1,17},{17,1},{2,18},{18,2},{3,19},{19,3},{4,20},{20... | collective-permute-start | bytes 12296 | tf_op jit(solution)/shard_map/ppermute | solution.py:27
  297.9 57.8 %all-gather.20.cloned.1.call-start = ((), (), s32[]{:S(2)}) async-start(), calls=%async_computation.18 | async-start | bytes 2621440 | tf_op jit(solution)/shard_map/all_gather | solution.py:31
  297.9 5.7 collective-permute-start.11
  332.9 75.7 %reduce-scatter.23.cloned.1.call-start = ((), (), s32[]{:S(2)}) async-start(), calls=%async_computation.19 | async-start | bytes 2621440 | tf_op jit(solution)/shard_map/reduce_scatter | solution.py:35
  377.9 58.3 %all-gather.22.cloned.1.call-start = ((), (), s32[]{:S(2)}) async-start(), calls=%async_computation.20 | async-start | bytes 2621440 | tf_op jit(solution)/shard_map/all_gather | solution.py:31
  413.5 47.6 %all-gather.24.cloned.1.call-start = ((), (), s32[]{:S(2)}) async-start(), calls=%async_computation.22 | async-start | bytes 2621440 | tf_op jit(solution)/shard_map/all_gather | solution.py:31
  418.1 89.7 %reduce-scatter.27.cloned.1.call-start = ((), (), s32[]{:S(2)}) async-start(), calls=%async_computation.23 | async-start | bytes 2621440 | tf_op jit(solution)/shard_map/reduce_scatter | solution.py:35
  477.1 60.3 %all-gather.26.cloned.1.call-start = ((), (), s32[]{:S(2)}) async-start(), calls=%async_computation.24 | async-start | bytes 2621440 | tf_op jit(solution)/shard_map/all_gather | solution.py:31
  514.7 88.1 %reduce-scatter.29.cloned.1.call-start = ((), (), s32[]{:S(2)}) async-start(), calls=%async_computation.25 | async-start | bytes 2621440 | tf_op jit(solution)/shard_map/reduce_scatter | solution.py:35
  571.8 59.4 %all-gather.28.cloned.1.call-start = ((), (), s32[]{:S(2)}) async-start(), calls=%async_computation.26 | async-start | bytes 2621440 | tf_op jit(solution)/shard_map/all_gather | solution.py:31
  608.5 69.7 %reduce-scatter.31.cloned.1.call-start = ((), (), s32[]{:S(2)}) async-start(), calls=%async_computation.27 | async-start | bytes 2621440 | tf_op jit(solution)/shard_map/reduce_scatter | solution.py:35
  644.7 63.0 %all-gather.30.cloned.1.call-start = ((), (), s32[]{:S(2)}) async-start(), calls=%async_computation.28 | async-start | bytes 2621440 | tf_op jit(solution)/shard_map/all_gather | solution.py:31
  685.0 179.1 %reduce-scatter.25.cloned.1.call-start = ((), (), s32[]{:S(2)}) async-start(), calls=%async_computation.21 | async-start | bytes 2621440 | tf_op jit(solution)/shard_map/reduce_scatter | solution.py:35
  692.7 202.8 %reduce-scatter.33.cloned.1.call-start = ((), (), s32[]{:S(2)}) async-start(), calls=%async_computation.29 | async-start | bytes 2621440 | tf_op jit(solution)/shard_map/reduce_scatter | solution.py:35
  746.6 200.1 %reduce-scatter.39.cloned.1.call-start = ((), (), s32[]{:S(2)}) async-start(), calls=%async_computation.32 | async-start | bytes 2621440 | tf_op jit(solution)/shard_map/reduce_scatter | solution.py:289
  754.2 48.3 %collective-permute-start.18 = (bf16[1024,1024]{1,0:T(8,128)(2,1)S(1)}, bf16[1024,1024]{1,0:T(8,128)(2,1)S(1)}, u32[]{:S(2)}, u32[]{:S(2)}) collective-permute-start(bf16[1024,1024]{1,0:T(8,128)(2,1)S(1)} %get-tuple-element.110), channel_id=1, source_target_pairs={{0,16},{16,0},{1,17},{17,1},{2,18},{18,2},{3,19},{19,3},{4,20},{20... | collective-permute-start | bytes 6291464 | tf_op jit(solution)/shard_map/ppermute | solution.py:27
  804.1 144.7 %reduce-scatter.41.cloned.1.call-start = ((), (), s32[]{:S(2)}) async-start(), calls=%async_computation.33 | async-start | bytes 2621440 | tf_op jit(solution)/shard_map/reduce_scatter | solution.py:289
  813.4 47.4 %collective-permute-start.20 = (bf16[1024,1024]{1,0:T(8,128)(2,1)S(1)}, bf16[1024,1024]{1,0:T(8,128)(2,1)S(1)}, u32[]{:S(2)}, u32[]{:S(2)}) collective-permute-start(bf16[1024,1024]{1,0:T(8,128)(2,1)S(1)} %get-tuple-element.116), channel_id=1, source_target_pairs={{0,16},{16,0},{1,17},{17,1},{2,18},{18,2},{3,19},{19,3},{4,20},{20... | collective-permute-start | bytes 6291464 | tf_op jit(solution)/shard_map/ppermute | solution.py:27
  862.5 88.4 %reduce-scatter.45.cloned.1.call-start = ((), (), s32[]{:S(2)}) async-start(), calls=%async_computation.38 | async-start | bytes 81920
  866.3 34.2 %collective-permute-start.12 = (bf16[256,1024]{1,0:T(8,128)(2,1)}, bf16[256,1024]{1,0:T(8,128)(2,1)}, u32[]{:S(2)}, u32[]{:S(2)}) collective-permute-start(bf16[256,1024]{1,0:T(8,128)(2,1)} %broadcast_select_fusion.29), channel_id=1, source_target_pairs={{0,16},{16,0},{1,17},{17,1},{2,18},{18,2},{3,19},{19,3},{4,20},{20... | collective-permute-start | bytes 1572872 | tf_op jit(solution)/shard_map/ppermute | solution.py:27
  875.8 17.7 %collective-permute-start.17 = (bf16[256,1024]{1,0:T(8,128)(2,1)}, bf16[256,1024]{1,0:T(8,128)(2,1)}, u32[]{:S(2)}, u32[]{:S(2)}) collective-permute-start(bf16[256,1024]{1,0:T(8,128)(2,1)} %get-tuple-element.108), channel_id=1, source_target_pairs={{0,16},{16,0},{1,17},{17,1},{2,18},{18,2},{3,19},{19,3},{4,20},{20... | collective-permute-start | bytes 1572872 | tf_op jit(solution)/shard_map/ppermute | solution.py:27
  876.8 15.8 %collective-permute-start.16 = (bf16[2,256]{1,0:T(2,128)(2,1)S(1)}, bf16[2,256]{1,0:T(2,128)(2,1)S(1)}, u32[]{:S(2)}, u32[]{:S(2)}) collective-permute-start(bf16[2,256]{1,0:T(2,128)(2,1)S(1)} %broadcast_select_fusion.45), channel_id=1, source_target_pairs={{0,16},{16,0},{1,17},{17,1},{2,18},{18,2},{3,19},{19,3},{4,20},{20... | collective-permute-start | bytes 3080 | tf_op jit(solution)/shard_map/ppermute | solution.py:27
  884.0 42.1 %collective-permute-start.15 = (bf16[1024,3,256]{2,0,1:T(8,128)(2,1)}, bf16[1024,3,256]{2,0,1:T(8,128)(2,1)}, u32[]{:S(2)}, u32[]{:S(2)}) collective-permute-start(bf16[1024,3,256]{2,0,1:T(8,128)(2,1)} %get-tuple-element.106), channel_id=1, source_target_pairs={{0,16},{16,0},{1,17},{17,1},{2,18},{18,2},{3,19},{19,3},{4,20},{20... | collective-permute-start | bytes 4718600 | tf_op jit(solution)/shard_map/ppermute | solution.py:27
  893.5 61.6 %reduce-scatter.37.cloned.1.call-start = ((), (), s32[]{:S(2)}) async-start(), calls=%async_computation.31 | async-start | bytes 655360 | tf_op jit(solution)/shard_map/reduce_scatter | solution.py:289
  895.5 112.6 %reduce-scatter.43.cloned.1.call-start = ((), (), s32[]{:S(2)}) async-start(), calls=%async_computation.37 | async-start | bytes 557056
  898.8 26.1 %collective-permute-start.14 = (f32[6,1024]{1,0:T(8,128)S(1)}, f32[6,1024]{1,0:T(8,128)S(1)}, u32[]{:S(2)}, u32[]{:S(2)}) collective-permute-start(f32[6,1024]{1,0:T(8,128)S(1)} %broadcast_select_fusion.36), channel_id=1, source_target_pairs={{0,16},{16,0},{1,17},{17,1},{2,18},{18,2},{3,19},{19,3},{4,20},{20... | collective-permute-start | bytes 73736 | tf_op jit(solution)/shard_map/ppermute | solution.py:27
  926.0 118.7 %reduce-scatter.35.cloned.1.call-start = ((), (), s32[]{:S(2)}) async-start(), calls=%async_computation.30 | async-start | bytes 1966080 | tf_op jit(solution)/shard_map/reduce_scatter | solution.py:289
  930.6 3.7 collective-permute-start.19
  953.4 59.4 %collective-permute-start.13 = (bf16[256,1024]{1,0:T(8,128)(2,1)}, bf16[256,1024]{1,0:T(8,128)(2,1)S(1)}, u32[]{:S(2)}, u32[]{:S(2)}) collective-permute-start(bf16[256,1024]{1,0:T(8,128)(2,1)} %get-tuple-element.36), channel_id=1, source_target_pairs={{0,16},{16,0},{1,17},{17,1},{2,18},{18,2},{3,19},{19,3},{4,20},{20... | collective-permute-start | bytes 1572872 | tf_op jit(solution)/shard_map/ppermute | solution.py:27
  (95 other events, 1129.8 us)
Sparse Core Ops, SparseCore 0:
  9.6 48.3 all-gather.31
  60.1 21.1 all-gather.15
  113.2 31.9 reduce-scatter.18
  146.7 45.9 all-gather.33
  194.1 44.9 all-gather.35
  241.2 20.8 all-gather.17
  298.0 32.0 reduce-scatter.20
  333.1 22.5 all-gather.19
  378.1 30.5 reduce-scatter.22
  413.6 22.5 all-gather.21
  438.5 22.5 all-gather.23
  477.2 30.4 reduce-scatter.26
  514.8 22.5 all-gather.25
  571.9 30.7 reduce-scatter.28
  608.6 22.5 all-gather.27
  644.9 33.3 reduce-scatter.30
  685.1 22.5 all-gather.29
  710.6 31.4 reduce-scatter.24
  746.7 32.2 reduce-scatter.32
  804.2 44.3 reduce-scatter.38
  862.6 44.0 reduce-scatter.40
  909.5 18.2 reduce-scatter.44
  930.2 19.7 reduce-scatter.36
  953.8 54.1 reduce-scatter.42
  1010.4 34.2 reduce-scatter.34

commit v2 on v1

v2 whole, which is shorter than its diff:
```python
import functools

import jax
import jax.numpy as jnp
from jax import lax
from jax.experimental import pallas as pl
from jax.experimental.pallas import tpu as pltpu
from jax.sharding import PartitionSpec as P

HEADS = 16
HEAD = 64
PAIR = 2 * HEAD

EPSILON = 1e-05
GELU_SCALE = 0.7978845608028654

MESH = pl.DeviceIdType.MESH
F32 = jnp.float32
BF16 = jnp.bfloat16
CHUNKS = 2
VMEM_LIMIT = 60 * 1024 * 1024


def rows_at(start, size):
    return pl.ds(pl.multiple_of(start, size), size)


def mm(left, right):
    return lax.dot_general(left, right, (((1,), (0,)), ((), ())), preferred_element_type=F32)


def mm_t(left, right):
    return lax.dot_general(left, right, (((1,), (1,)), ((), ())), preferred_element_type=F32)


class Ring:
    def __init__(self, block):
        self.block = block
        self.chunk = block // CHUNKS
        self.me = lax.axis_index("tensor")
        core, chip = lax.rem(self.me, 2), self.me // 2
        self.mate = self.me + 1 - 2 * core
        self.peer = self.me + 2 - 4 * chip
        self.far = self.peer + 1 - 2 * core

    def greet(self):
        barrier = pltpu.get_barrier_semaphore()
        for other in (self.mate, self.peer):
            pl.semaphore_signal(barrier, inc=1, device_id={"tensor": other}, device_id_type=MESH)
        pl.semaphore_wait(barrier, 2)

    def rows(self, owner, c):
        return rows_at(owner * self.block + c * self.chunk, self.chunk)

    def send(self, src, dst, sems, kind, c, other):
        return pltpu.make_async_remote_copy(
            src_ref=src,
            dst_ref=dst,
            send_sem=sems.at[0, kind, c],
            recv_sem=sems.at[1, kind, c],
            device_id={"tensor": other},
            device_id_type=MESH,
        )


class Gather:
    def __init__(self, ring, every, sems):
        self.ring, self.every, self.sems = ring, every, sems

    def copy(self, kind, owner, c):
        ring = self.ring
        at = self.every.at[ring.rows(owner, c)]
        return ring.send(at, at, self.sems, kind, c, ring.peer if kind == 1 else ring.mate)

    def start(self, c):
        self.copy(1, self.ring.me, c).start()
        self.copy(0, self.ring.me, c).start()

    def arrived_mate(self, c):
        self.copy(0, self.ring.mate, c).wait_recv()

    def arrived_peer(self, c):
        self.copy(1, self.ring.peer, c).wait_recv()
        self.copy(2, self.ring.peer, c).start()

    def arrived_far(self, c):
        self.copy(2, self.ring.far, c).wait_recv()

    def finish(self):
        for c in range(CHUNKS):
            for kind, owner in ((0, self.ring.me), (1, self.ring.me), (2, self.ring.peer)):
                self.copy(kind, owner, c).wait_send()


class Scatter:
    def __init__(self, ring, stage, land, sems):
        self.ring, self.stage, self.land, self.sems = ring, stage, land, sems

    def copy(self, kind, c):
        ring = self.ring
        at = pl.ds(c * ring.chunk, ring.chunk)
        return ring.send(
            self.stage.at[kind, at],
            self.land.at[kind, at],
            self.sems,
            kind,
            c,
            ring.peer if kind == 1 else ring.mate,
        )

    def put(self, kind, c, value):
        self.stage[kind, pl.ds(c * self.ring.chunk, self.ring.chunk)] = value.astype(BF16)
        self.copy(kind, c).start()

    def take(self, kind, c):
        self.copy(kind, c).wait_recv()
        return self.land[kind, pl.ds(c * self.ring.chunk, self.ring.chunk)].astype(F32)

    def to_peer(self, c, far_part, peer_part):
        self.put(0, c, far_part)
        self.put(1, c, peer_part + self.take(0, c))

    def finish(self):
        for kind in range(3):
            for c in range(CHUNKS):
                self.copy(kind, c).wait_send()


def normalize(values):
    center = values - jnp.mean(values, axis=-1, keepdims=True)
    scale = lax.rsqrt(jnp.mean(center * center, axis=-1, keepdims=True) + EPSILON)
    return center * scale, scale


def norm_pull(values, gain, grad):
    unit, scale = normalize(values)
    scaled = grad * gain
    pulled = scale * (
        scaled
        - jnp.mean(scaled, axis=-1, keepdims=True)
        - unit * jnp.mean(scaled * unit, axis=-1, keepdims=True)
    )
    return pulled, jnp.sum(grad * unit, axis=0, keepdims=True), jnp.sum(grad, axis=0, keepdims=True)


def scores_of(keys, queries, slope, penalty_ref, start):
    stop, count = keys.shape[0], queries.shape[0]
    scores = mm_t(keys, queries) + slope * penalty_ref[:stop]
    last = scores[start:]
    allowed = lax.broadcasted_iota(jnp.int32, (count, count), 0) <= lax.broadcasted_iota(
        jnp.int32, (count, count), 1
    )
    last = jnp.where(allowed, last, -1e30)
    return last if start == 0 else jnp.concatenate([scores[:start], last], axis=0)


def head_mask(value, which):
    lane = lax.broadcasted_iota(jnp.int32, value.shape, 1)
    inside = lane < HEAD if which == 0 else lane >= HEAD
    return jnp.where(inside, value, jnp.zeros_like(value))


def fill_penalty(penalty_ref):
    penalty_ref[...] = lax.broadcasted_iota(jnp.int32, penalty_ref.shape, 0).astype(F32)


def attend_forward(proj, context, totals, slopes, penalty, block):
    length, width = context.shape

    def pair_step(pair, carry):
        lanes = pl.ds(pl.multiple_of(pair * PAIR, PAIR), PAIR)
        for start in range(0, length, block):
            stop = start + block
            queries = proj[0, start:stop, lanes] * jnp.asarray(0.125, BF16)
            keys = proj[1, :stop, lanes]
            values_t = proj[2, :stop, lanes].T
            outs = []
            for which in range(2):
                head = pair * 2 + which
                slope = slopes[pl.ds(head, 1), :]
                scores = scores_of(keys, head_mask(queries, which), slope, penalty, start)
                highest = jnp.max(scores, axis=0, keepdims=True)
                grown = jnp.exp(scores - highest)
                total = jnp.sum(grown, axis=0, keepdims=True)
                mixed = mm(values_t[which * HEAD : (which + 1) * HEAD], grown.astype(BF16))
                outs.append(mixed / total)
                totals[pl.ds(head, 1), start:stop] = highest + jnp.log(total)
            context[start:stop, lanes] = jnp.concatenate(outs, axis=0).T.astype(BF16)
        return carry

    lax.fori_loop(0, width // PAIR, pair_step, 0)


def attend_backward(proj, grad_context, totals, slopes, penalty, grad_proj, sums, block):
    length, width = grad_context.shape

    def pair_step(pair, carry):
        lanes = pl.ds(pl.multiple_of(pair * PAIR, PAIR), PAIR)
        for start in range(0, length, block):
            stop = start + block
            queries = proj[0, start:stop, lanes] * jnp.asarray(0.125, BF16)
            keys = proj[1, :stop, lanes]
            keys_t = keys.T
            values = proj[2, :stop, lanes]
            grads = grad_context[start:stop, lanes]
            outs = []
            for which in range(2):
                head = pair * 2 + which
                slope = slopes[pl.ds(head, 1), :]
                one_query = head_mask(queries, which)
                one_grad = head_mask(grads, which)
                scores = scores_of(keys, one_query, slope, penalty, start)
                probs = jnp.exp(scores - totals[pl.ds(head, 1), start:stop])
                pulled = probs * mm_t(values, one_grad)
                inner = jnp.sum(pulled, axis=0, keepdims=True)
                grad_scores = (pulled - probs * inner).astype(BF16)
                outs.append(mm(keys_t[which * HEAD : (which + 1) * HEAD], grad_scores) * 0.125)
                grad_keys = mm(grad_scores, one_query)
                grad_values = mm(probs.astype(BF16), one_grad)
                if which == 0:
                    first_keys, first_values = grad_keys, grad_values
                else:
                    grad_keys, grad_values = grad_keys + first_keys, grad_values + first_values
            grad_proj[0, start:stop, lanes] = jnp.concatenate(outs, axis=0).T.astype(BF16)
            if start > 0:
                sums[0, :start] += grad_keys[:start]
                sums[1, :start] += grad_values[:start]
            sums[0, start:stop] = grad_keys[start:]
            sums[1, start:stop] = grad_values[start:]
        grad_proj[1, :, lanes] = sums[0].astype(BF16)
        grad_proj[2, :, lanes] = sums[1].astype(BF16)
        return carry

    lax.fori_loop(0, width // PAIR, pair_step, 0)


def attention_forward_kernel(
    x, gain, shift, w_qkv, b_qkv, w_out, b_out, slopes,
    normed, proj, context, totals, middle,
    penalty, stage, land, gather_sems, scatter_sems,
):
    block = x.shape[0]
    ring = Ring(block)
    ring.greet()
    gather = Gather(ring, normed, gather_sems)
    chunk = ring.chunk
    for c in range(CHUNKS):
        at = pl.ds(c * chunk, chunk)
        unit, _ = normalize(x[at].astype(F32))
        normed[ring.rows(ring.me, c)] = (unit * gain[...] + shift[...]).astype(BF16)
        gather.start(c)
    fill_penalty(penalty)

    def project(owner, c, size):
        at = rows_at(owner * block + c * chunk, size)
        rows = normed[at]
        for part in range(3):
            proj[part, at] = (mm(rows, w_qkv[part]) + b_qkv[part]).astype(BF16)

    project(ring.me, 0, block)
    for c in range(CHUNKS):
        gather.arrived_mate(c)
    project(ring.mate, 0, block)
    for c in range(CHUNKS):
        gather.arrived_peer(c)
        project(ring.peer, c, chunk)
        gather.arrived_far(c)
        project(ring.far, c, chunk)
    attend_forward(proj, context, totals, slopes, penalty, block)
    scatter = Scatter(ring, stage, land, scatter_sems)

    def part_of(owner, c):
        return mm(context[ring.rows(owner, c)], w_out[...])

    for c in range(CHUNKS):
        scatter.put(0, c, part_of(ring.far, c))
        scatter.put(1, c, part_of(ring.peer, c) + scatter.take(0, c))
    for c in range(CHUNKS):
        scatter.put(2, c, part_of(ring.mate, c))
    for c in range(CHUNKS):
        at = pl.ds(c * chunk, chunk)
        total = part_of(ring.me, c) + scatter.take(2, c) + scatter.take(1, c)
        middle[at] = x[at].astype(F32) + total + b_out[...]
    gather.finish()
    scatter.finish()


def mlp_forward_kernel(
    middle, gain, shift, w_up, b_up, w_down, b_down,
    second, activated, slope_of, leaving,
    own, stage, land, gather_sems, scatter_sems,
):
    block = middle.shape[0]
    ring = Ring(block)
    ring.greet()
    gather = Gather(ring, second, gather_sems)
    scatter = Scatter(ring, stage, land, scatter_sems)
    chunk = ring.chunk
    for c in range(CHUNKS):
        at = pl.ds(c * chunk, chunk)
        unit, _ = normalize(middle[at])
        second[ring.rows(ring.me, c)] = (unit * gain[...] + shift[...]).astype(BF16)
        gather.start(c)

    def expand(at):
        upward = mm(second[at], w_up[...]) + b_up[...]
        inner = jnp.tanh(GELU_SCALE * (upward + 0.044715 * upward * upward * upward))
        half = 0.5 * (1.0 + inner)
        value = upward * half
        slope = half + 0.5 * upward * (1.0 - inner * inner) * GELU_SCALE * (
            1.0 + 3 * 0.044715 * upward * upward
        )
        value = value.astype(BF16)
        activated[at] = value
        slope_of[at] = slope.astype(BF16)
        return mm(value, w_down[...])

    own[...] = expand(rows_at(ring.me * block, block))
    for c in range(CHUNKS):
        gather.arrived_mate(c)
    part = expand(rows_at(ring.mate * block, block))
    for c in range(CHUNKS):
        scatter.put(2, c, part[c * chunk : (c + 1) * chunk])
    for c in range(CHUNKS):
        gather.arrived_peer(c)
        peer_part = expand(ring.rows(ring.peer, c))
        gather.arrived_far(c)
        scatter.put(0, c, expand(ring.rows(ring.far, c)))
        scatter.put(1, c, peer_part + scatter.take(0, c))
    for c in range(CHUNKS):
        at = pl.ds(c * chunk, chunk)
        total = own[at] + scatter.take(2, c) + scatter.take(1, c)
        leaving[at] = (middle[at] + total + b_down[...]).astype(BF16)
    gather.finish()
    scatter.finish()


def mlp_backward_kernel(
    incoming, middle, gain, w_up, w_down, slope_of,
    down_rows, grad_up, grad_middle, small, up_sum,
    own, stage, land, gather_sems, scatter_sems,
):
    block = middle.shape[0]
    ring = Ring(block)
    ring.greet()
    gather = Gather(ring, down_rows, gather_sems)
    scatter = Scatter(ring, stage, land, scatter_sems)
    chunk = ring.chunk
    for c in range(CHUNKS):
        down_rows[ring.rows(ring.me, c)] = incoming[pl.ds(c * chunk, chunk)].astype(BF16)
        gather.start(c)
    up_sum[...] = jnp.zeros_like(up_sum)

    def pull(at):
        grad = mm_t(down_rows[at], w_down[...]) * slope_of[at].astype(F32)
        grad = grad.astype(BF16)
        grad_up[at] = grad
        up_sum[...] += jnp.sum(grad.astype(F32), axis=0, keepdims=True)
        return mm_t(grad, w_up[...])

    own[...] = pull(rows_at(ring.me * block, block))
    for c in range(CHUNKS):
        gather.arrived_mate(c)
    part = pull(rows_at(ring.mate * block, block))
    for c in range(CHUNKS):
        scatter.put(2, c, part[c * chunk : (c + 1) * chunk])
    for c in range(CHUNKS):
        gather.arrived_peer(c)
        peer_part = pull(ring.rows(ring.peer, c))
        gather.arrived_far(c)
        scatter.put(0, c, pull(ring.rows(ring.far, c)))
        scatter.put(1, c, peer_part + scatter.take(0, c))
    small[...] = jnp.zeros_like(small)
    for c in range(CHUNKS):
        at = pl.ds(c * chunk, chunk)
        total = own[at] + scatter.take(2, c) + scatter.take(1, c)
        pulled, grad_gain, grad_shift = norm_pull(middle[at], gain[...], total)
        before = incoming[at]
        after = before + pulled
        grad_middle[at] = after
        small[0:1] += jnp.sum(after, axis=0, keepdims=True)
        small[1:2] += grad_gain
        small[2:3] += grad_shift
        small[3:4] += jnp.sum(before, axis=0, keepdims=True)
    gather.finish()
    scatter.finish()


def attention_backward_kernel(
    grad_middle, x, gain, w_qkv, w_out, slopes, proj, totals,
    attn_rows, grad_proj, grad_hidden, small, qv_sum,
    grad_context, sums, penalty, stage, land, gather_sems, scatter_sems,
):
    block = x.shape[0]
    ring = Ring(block)
    ring.greet()
    gather = Gather(ring, attn_rows, gather_sems)
    scatter = Scatter(ring, stage, land, scatter_sems)
    chunk = ring.chunk
    for c in range(CHUNKS):
        attn_rows[ring.rows(ring.me, c)] = grad_middle[pl.ds(c * chunk, chunk)].astype(BF16)
        gather.start(c)
    fill_penalty(penalty)

    def pull(at):
        grad_context[at] = mm_t(attn_rows[at], w_out[...]).astype(BF16)

    pull(rows_at(ring.me * block, block))
    for c in range(CHUNKS):
        gather.arrived_mate(c)
    pull(rows_at(ring.mate * block, block))
    for c in range(CHUNKS):
        gather.arrived_peer(c)
        pull(ring.rows(ring.peer, c))
        gather.arrived_far(c)
        pull(ring.rows(ring.far, c))
    attend_backward(proj, grad_context, totals, slopes, penalty, grad_proj, sums, block)
    qv_sum[...] = jnp.zeros_like(qv_sum)
    qv_sum[0:1] = jnp.sum(grad_proj[0].astype(F32), axis=0, keepdims=True)
    qv_sum[1:2] = jnp.sum(grad_proj[2].astype(F32), axis=0, keepdims=True)

    def part_of(owner, c):
        at = ring.rows(owner, c)
        total = mm_t(grad_proj[0, at], w_qkv[0])
        for part in range(1, 3):
            total += mm_t(grad_proj[part, at], w_qkv[part])
        return total

    for c in range(CHUNKS):
        scatter.put(0, c, part_of(ring.far, c))
        scatter.put(1, c, part_of(ring.peer, c) + scatter.take(0, c))
    for c in range(CHUNKS):
        scatter.put(2, c, part_of(ring.mate, c))
    small[...] = jnp.zeros_like(small)
    for c in range(CHUNKS):
        at = pl.ds(c * chunk, chunk)
        total = part_of(ring.me, c) + scatter.take(2, c) + scatter.take(1, c)
        pulled, grad_gain, grad_shift = norm_pull(x[at].astype(F32), gain[...], total)
        grad_hidden[at] = grad_middle[at] + pulled
        small[0:1] += grad_gain
        small[1:2] += grad_shift
    gather.finish()
    scatter.finish()


def call(kernel, name, number, args, outs, scratch):
    vmem = pl.BlockSpec(memory_space=pltpu.VMEM)
    return pl.pallas_call(
        kernel,
        out_shape=[jax.ShapeDtypeStruct(shape, dtype) for shape, dtype in outs],
        in_specs=[vmem] * len(args),
        out_specs=[vmem] * len(outs),
        scratch_shapes=scratch,
        compiler_params=pltpu.CompilerParams(
            collective_id=number, has_side_effects=True, vmem_limit_bytes=VMEM_LIMIT
        ),
        name=name,
    )(*args)


def link_scratch(block, width):
    return [
        pltpu.VMEM((3, block, width), BF16),
        pltpu.VMEM((3, block, width), BF16),
        pltpu.SemaphoreType.DMA((2, 3, CHUNKS)),
        pltpu.SemaphoreType.DMA((2, 3, CHUNKS)),
    ]


def row_vector(value):
    return value.reshape(1, -1)


def layer_forward(x, w, slopes):
    block, width = x.shape
    length = block * lax.axis_size("tensor")
    local = w["out"].shape[0]
    heads = local // HEAD
    normed, proj, context, totals, middle = call(
        attention_forward_kernel,
        "attention_forward",
        1,
        (x, row_vector(w["ln1_gain"]), row_vector(w["ln1_bias"]), w["qkv"], w["b_qkv"], w["out"], row_vector(w["b_out"]), slopes),
        [((length, width), BF16), ((3, length, local), BF16), ((length, local), BF16), ((heads, length), F32), ((block, width), F32)],
        [pltpu.VMEM((length, block), F32)] + link_scratch(block, width),
    )
    units = w["up"].shape[1]
    second, activated, slope_of, leaving = call(
        mlp_forward_kernel,
        "mlp_forward",
        2,
        (middle, row_vector(w["ln2_gain"]), row_vector(w["ln2_bias"]), w["up"], row_vector(w["b_up"]), w["down"], row_vector(w["b_down"])),
        [((length, width), BF16), ((length, units), BF16), ((length, units), BF16), ((block, width), BF16)],
        [pltpu.VMEM((block, width), F32)] + link_scratch(block, width),
    )
    saved = dict(x=x, normed=normed, proj=proj, context=context, totals=totals, middle=middle, second=second, activated=activated, slope_of=slope_of)
    return leaving, saved


def layer_backward(incoming, w, s, slopes):
    block, width = incoming.shape
    length = block * lax.axis_size("tensor")
    local, units = w["out"].shape[0], w["up"].shape[1]
    down_rows, grad_up, grad_middle, small_a, up_sum = call(
        mlp_backward_kernel,
        "mlp_backward",
        3,
        (incoming, s["middle"], row_vector(w["ln2_gain"]), w["up"], w["down"], s["slope_of"]),
        [((length, width), BF16), ((length, units), BF16), ((block, width), F32), ((8, width), F32), ((1, units), F32)],
        [pltpu.VMEM((block, width), F32)] + link_scratch(block, width),
    )
    attn_rows, grad_proj, grad_hidden, small_b, qv_sum = call(
        attention_backward_kernel,
        "attention_backward",
        4,
        (grad_middle, s["x"], row_vector(w["ln1_gain"]), w["qkv"], w["out"], slopes, s["proj"], s["totals"]),
        [((length, width), BF16), ((3, length, local), BF16), ((block, width), F32), ((8, width), F32), ((8, local), F32)],
        [pltpu.VMEM((length, local), BF16), pltpu.VMEM((2, length, PAIR), F32), pltpu.VMEM((length, block), F32)]
        + link_scratch(block, width),
    )
    small = jnp.stack([small_b[0], small_b[1], small_a[0], small_a[1], small_a[2], small_a[3]])
    large = dict(
        qkv=jnp.einsum("td,cth->cdh", s["normed"], grad_proj, preferred_element_type=F32),
        out=jnp.einsum("th,td->hd", s["context"], attn_rows, preferred_element_type=F32),
        up=jnp.einsum("td,tf->df", s["second"], grad_up, preferred_element_type=F32),
        down=jnp.einsum("tf,td->fd", s["activated"], down_rows, preferred_element_type=F32),
        b_qv=qv_sum[:2],
        b_up=up_sum[0],
    )
    return grad_hidden, small, large


def swapped(value):
    count = lax.axis_size("section")
    return lax.ppermute(value, "section", [(i, (i + 1) % count) for i in range(count)])


def per_device(
    inputs,
    out_grad,
    lang_ids,
    lang_weights,
    ln1_gain,
    ln1_bias,
    w_qkv,
    b_qv,
    w_out,
    b_out,
    ln2_gain,
    ln2_bias,
    w_up,
    b_up,
    w_down,
    b_down,
):
    section = lax.axis_index("section")
    layer_count = lax.axis_size("section")
    local_heads = w_qkv.shape[3] // HEAD
    head_ids = lax.axis_index("tensor") * local_heads + jnp.arange(local_heads, dtype=jnp.int32)
    slopes = jnp.exp2(-8.0 * (head_ids.astype(jnp.float32) + 1.0) / HEADS)
    slopes = jnp.broadcast_to(slopes[:, None], (local_heads, inputs.shape[1]))

    def both(value):
        other = swapped(value)
        return [jnp.where(section == l, value, other) for l in range(layer_count)]

    def over_dp(value, axis):
        return both(lax.all_gather(value, "dp", axis=axis, tiled=True))

    qkv_all, up_all = over_dp(jnp.transpose(w_qkv[0], (1, 0, 2)), 1), over_dp(w_up[0], 0)
    out_all, down_all = over_dp(w_out[0], 1), over_dp(w_down[0], 1)
    vectors = [
        both(item[0]) for item in (ln1_gain, ln1_bias, b_qv, b_out, ln2_gain, ln2_bias, b_up, b_down)
    ]
    layers = []
    for l in range(layer_count):
        gain1, bias1, qv, bout, gain2, bias2, bup, bdown = [item[l] for item in vectors]
        layers.append(
            dict(
                ln1_gain=gain1,
                ln1_bias=bias1,
                ln2_gain=gain2,
                ln2_bias=bias2,
                qkv=qkv_all[l],
                out=out_all[l],
                up=up_all[l],
                down=down_all[l],
                b_qkv=jnp.stack([qv[0], jnp.zeros_like(qv[0]), qv[1]])[:, None, :],
                b_out=bout,
                b_up=bup,
                b_down=bdown,
            )
        )
    row = lax.dynamic_index_in_dim(inputs, section, 0, keepdims=False)
    target = lax.dynamic_index_in_dim(out_grad, section, 0, keepdims=False)
    lang = lax.dynamic_index_in_dim(lang_ids, section, 0, keepdims=False)
    matches = lang == jnp.arange(lang_weights.shape[0], dtype=jnp.int32)
    scale = jnp.sum(jnp.where(matches, lang_weights, 0)).astype(jnp.float32) / 64.0

    acts, saved = [], []
    for l in range(layer_count):
        row, kept = layer_forward(row, layers[l], slopes)
        acts.append(row)
        saved.append(kept)
    grads, small, large = [None] * layer_count, [None] * layer_count, [None] * layer_count
    incoming = target.astype(jnp.float32) * scale
    for l in reversed(range(layer_count)):
        grads[l], small[l], large[l] = layer_backward(
            incoming, layers[l], saved[l], slopes
        )
        incoming = grads[l].astype(jnp.bfloat16).astype(jnp.float32)

    def mine(items):
        return jnp.where(section == 0, items[0], items[1])

    def theirs(items):
        return jnp.where(section == 0, items[1], items[0])

    def rows_of(items):
        own, other = mine(items), swapped(theirs(items))
        return jnp.stack([jnp.where(section == r, own, other) for r in range(layer_count)])[None]

    def reduced(name, axis):
        items = [item[name].astype(jnp.bfloat16) for item in large]
        total = mine(items) + swapped(theirs(items))
        return lax.psum_scatter(total, "dp", scatter_dimension=axis, tiled=True).astype(
            jnp.float32
        )[None]

    small_total = mine(small) + swapped(theirs(small))
    small_shards = lax.psum_scatter(small_total, ("tensor", "dp"), scatter_dimension=1, tiled=True)
    return (
        rows_of(acts),
        rows_of([item.astype(jnp.bfloat16) for item in grads]).astype(jnp.float32),
        small_shards[0][None],
        small_shards[1][None],
        jnp.transpose(reduced("qkv", 1), (0, 2, 1, 3)),
        reduced("b_qv", 1),
        reduced("out", 1),
        small_shards[2][None],
        small_shards[3][None],
        small_shards[4][None],
        reduced("up", 0),
        reduced("b_up", 0),
        reduced("down", 1),
        small_shards[5][None],
    )


def solution(mesh):
    return jax.shard_map(
        per_device,
        mesh=mesh,
        in_specs=(
            P("dp", "tensor", None),
            P("dp", "tensor", None),
            P("dp"),
            P(),
            P("section", None),
            P("section", None),
            P("section", "dp", None, "tensor"),
            P("section", None, "tensor"),
            P("section", "tensor", "dp"),
            P("section", None),
            P("section", None),
            P("section", None),
            P("section", "dp", "tensor"),
            P("section", "tensor"),
            P("section", "tensor", "dp"),
            P("section", None),
        ),
        out_specs=(
            P("section", "dp", "tensor", None),
            P("section", "dp", "tensor", None),
            P("section", ("tensor", "dp")),
            P("section", ("tensor", "dp")),
            P("section", "dp", None, "tensor"),
            P("section", None, ("tensor", "dp")),
            P("section", "tensor", "dp"),
            P("section", ("tensor", "dp")),
            P("section", ("tensor", "dp")),
            P("section", ("tensor", "dp")),
            P("section", "dp", "tensor"),
            P("section", ("tensor", "dp")),
            P("section", "tensor", "dp"),
            P("section", ("tensor", "dp")),
        ),
        check_vma=False,
    )
```

time: 1060 us -> 836 us (0.79)
  waiting for transfers between devices: 682 us -> 351 us
  Pallas kernels: 0 us -> 310 us
  matrix products: 154 us -> 25.2 us
  other arithmetic: 94.3 us -> 46.2 us
  local copies, waits for them, and re-layouts: 37 us -> 16.8 us
    pallas_call x0 -> x8, Pallas kernels: none -> 310 us  [call(): pl.pallas_call(kernel, out_shape=[jax.ShapeDtypeStruct(shape, dtype) for...]
    reduce_scatter x8 -> x0, waiting for transfers between devices: 175 us -> none  [scatter_tokens(): lax.psum_scatter(value.astype(jnp.bfloat16), 'tensor', scatter_dimension=...]
    all_gather x8 -> x0, waiting for transfers between devices: 137 us -> none  [gather_tokens(): return lax.all_gather(value, 'tensor', axis=0, tiled=True)]
    dot_general x48 -> x8, matrix products: 154 us -> 25.2 us  [the longest x2 10.7 us: layer_backward(): jnp.einsum('tf,td->fd', s['activated'], down_rows, preferred_element_type...]
    unnamed x27 -> x11, waiting for transfers between devices: 53.5 us -> 2.08 us
    reduce_scatter x4, waiting for transfers between devices: 29.4 us -> 70.6 us  [reduced(): lax.psum_scatter(total, 'dp', scatter_dimension=axis, tiled=True)]
    reduce_sum x26 -> x0, other arithmetic: 35.3 us -> none  [the longest x8 12.6 us: layer_norm(): return center * lax.rsqrt(spread + EPSILON) * gain + shift]
    convert_element_type x12 -> x1, other arithmetic: 21.5 us -> 2.31 us  [per_device(): incoming = grads[l].astype(jnp.bfloat16).astype(jnp.float32)]
  transfers between devices with their start and end apart: 46 -> 30, of which waited for: 28 -> 12; matrix products, arithmetic and copies ran while one was open for 15% -> 9% of each run, Pallas kernels for 0% -> 5%
where the time goes in v2:
time: 836 us; the launch traced here: 829 us
  waiting for transfers between devices  351 us (42%)
  Pallas kernels  310 us (37%)
  other arithmetic  46.2 us (6%)
  blocking collectives  35.5 us (4%)
  starting transfers between devices  27.9 us (3%)
  matrix products  25.2 us (3%)
  local copies, waits for them, and re-layouts  16.8 us (2%)
  between operations  15.9 us (2%)
    pallas_call x8, Pallas kernels, call(): pl.pallas_call(kernel, out_shape=[jax.ShapeDtypeStruct(shape, dtype) for...  310 us
    ppermute x21, waiting for transfers between devices, swapped(): lax.ppermute(value, 'section', [(i, (i + 1) % count) for i in range(count)])  177 us
    all_gather x3, waiting for transfers between devices, over_dp(): return both(lax.all_gather(value, 'dp', axis=axis, tiled=True))  102 us
    reduce_scatter x4, waiting for transfers between devices, reduced(): lax.psum_scatter(total, 'dp', scatter_dimension=axis, tiled=True)  70.6 us
    ppermute x21, starting transfers between devices, swapped(): lax.ppermute(value, 'section', [(i, (i + 1) % count) for i in range(count)])  27.3 us
    all_gather x1, blocking collectives, over_dp(): return both(lax.all_gather(value, 'dp', axis=axis, tiled=True))  25.1 us
  transfers between devices with their start and end apart: 30, of which 12 were waited for; matrix products, arithmetic and copies ran while one was open for 9% of the time, Pallas kernels for 5%

profile of v2, /device:TPU:0, one launch (start us, length us, event | category | flops | bytes accessed | tf_op | source)
XLA Modules:
  0.0 828.7 jit_solution(6676526650415574186)
XLA Ops:
  9.5 3.0 collective-permute-start.3
  12.6 1.9 collective-permute-start.5
  15.9 1.9 fusion.14
  20.4 25.1 %all-gather = bf16[1,256,1024]{2,1,0:T(8,128)(2,1)S(1)} all-gather(bf16[1,256,256]{2,1,0:T(8,128)(2,1)S(1)} %copy-done.15), channel_id=2, replica_groups=mesh['section'=2,'tensor'=4,'dp'=4] {'dp'}, dimensions={2}, use_global_device_ids=true | all-gather | bytes 655360 | tf_op jit(solution)/shard_map/all_gather | solution.py:568
  45.5 21.4 %all-gather.11.cloned.1.call-done = bf16[1,1024,1024]{2,1,0:T(8,128)(2,1)} async-done(((bf16[1,1024,256]{2,1,0:T(8,128)(2,1)}), bf16[1,1024,1024]{2,1,0:T(8,128)(2,1)}) %all-gather.11.cloned.1.call-update) | async-done | bytes 2097168 | tf_op jit(solution)/shard_map/all_gather | solution.py:568
  68.5 35.4 %all-gather.7.cloned.1.call-done = bf16[3,1024,256]{2,1,0:T(8,128)(2,1)} async-done(((bf16[3,256,256]{2,1,0:T(8,128)(2,1)}), bf16[3,1024,256]{2,1,0:T(8,128)(2,1)}) %all-gather.7.cloned.1.call-update) | async-done | bytes 1572880 | tf_op jit(solution)/shard_map/all_gather | solution.py:568
  105.3 44.9 %all-gather.9.cloned.1.call-done = bf16[1,1024,1024]{2,1,0:T(8,128)(2,1)} async-done(((bf16[1,256,1024]{2,1,0:T(8,128)(2,1)}), bf16[1,1024,1024]{2,1,0:T(8,128)(2,1)}) %all-gather.9.cloned.1.call-update) | async-done | bytes 2097168 | tf_op jit(solution)/shard_map/all_gather | solution.py:568
  155.6 42.4 %collective-permute-done.6 = f32[1024]{0:T(1024)S(1)} collective-permute-done((f32[1024]{0:T(1024)S(1)}, f32[1024]{0:T(1024)S(1)}, u32[]{:S(2)}, u32[]{:S(2)}) %collective-permute-start.6) | collective-permute-done | bytes 4128 | tf_op jit(solution)/shard_map/ppermute | solution.py:535
  200.7 10.2 %collective-permute-done.11 = f32[1024]{0:T(1024)S(1)} collective-permute-done((f32[1024]{0:T(1024)S(1)}, f32[1024]{0:T(1024)S(1)}, u32[]{:S(2)}, u32[]{:S(2)}) %collective-permute-start.11) | collective-permute-done | bytes 4128 | tf_op jit(solution)/shard_map/ppermute | solution.py:535
  213.0 1.5 collective-permute-done.9
  216.2 3.3 broadcast_select_fusion.6
  220.1 42.3 %attention_forward.2 = (bf16[1024,1024]{1,0:T(8,128)(2,1)}, bf16[3,1024,256]{2,1,0:T(8,128)(2,1)}, bf16[1024,256]{1,0:T(8,128)(2,1)}, f32[4,1024]{1,0:T(4,128)}, f32[256,1024]{1,0:T(8,128)}) custom-call(bf16[256,1024]{1,0:T(8,128)(2,1)} %dynamic-slice_bitcast_fusion.x, f32[1,1024]{1,0:T(1,128)} %bitcast.114, f32[1,1024]{1,0:T(1,128)} %bitcast.129, ...), custom_call_target="tpu_custom_call" | custom-call | tf_op jit(solution)/shard_map/attention_forward/pallas_call | solution.py:448
  262.4 4.0 broadcast_select_fusion
  266.4 4.1 broadcast_select_fusion.1
  270.6 32.5 %mlp_forward.2 = (bf16[1024,1024]{1,0:T(8,128)(2,1)}, bf16[1024,1024]{1,0:T(8,128)(2,1)}, bf16[1024,1024]{1,0:T(8,128)(2,1)}, bf16[256,1024]{1,0:T(8,128)(2,1)}) custom-call(f32[256,1024]{1,0:T(8,128)} %get-tuple-element.52.middle, f32[1,1024]{1,0:T(1,128)} %bitcast.116, f32[1,1024]{1,0:T(1,128)} %bitcast.127, bf16[1024,1024]{1,0:T(8,128)(2,1)} %get-tuple-element.125.w_up, ...), custom_call_target="tpu_custom_call" | custom-call | tf_op jit(solution)/shard_map/mlp_forward/pallas_call | solution.py:448
  303.0 42.6 %attention_forward.3 = (bf16[1024,1024]{1,0:T(8,128)(2,1)}, bf16[3,1024,256]{2,1,0:T(8,128)(2,1)}, bf16[1024,256]{1,0:T(8,128)(2,1)}, f32[4,1024]{1,0:T(4,128)}, f32[256,1024]{1,0:T(8,128)}) custom-call(bf16[256,1024]{1,0:T(8,128)(2,1)} %get-tuple-element.53.x, f32[1,1024]{1,0:T(1,128)} %bitcast.120, f32[1,1024]{1,0:T(1,128)} %bitcast.123, ...), custom_call_target="tpu_custom_call" | custom-call | tf_op jit(solution)/shard_map/attention_forward/pallas_call | solution.py:448
  345.7 31.3 %mlp_forward.3 = (bf16[1024,1024]{1,0:T(8,128)(2,1)}, bf16[1024,1024]{1,0:T(8,128)(2,1)}, bf16[1024,1024]{1,0:T(8,128)(2,1)}, bf16[256,1024]{1,0:T(8,128)(2,1)}) custom-call(f32[256,1024]{1,0:T(8,128)} %get-tuple-element.54.middle, f32[1,1024]{1,0:T(1,128)} %bitcast.118, f32[1,1024]{1,0:T(1,128)} %bitcast.124, bf16[1024,1024]{1,0:T(8,128)(2,1)} %get-tuple-element.124.w_up, ...), custom_call_target="tpu_custom_call" | custom-call | tf_op jit(solution)/shard_map/mlp_forward/pallas_call | solution.py:448
  377.0 34.8 %mlp_backward.2 = (bf16[1024,1024]{1,0:T(8,128)(2,1)}, bf16[1024,1024]{1,0:T(8,128)(2,1)}, f32[256,1024]{1,0:T(8,128)}, f32[8,1024]{1,0:T(8,128)}, f32[1,1024]{1,0:T(1,128)}) custom-call(f32[256,1024]{1,0:T(8,128)} %multiply_bitcast_fusion.incoming, f32[256,1024]{1,0:T(8,128)} %get-tuple-element.54.middle, f32[1,1024]{1,0:T(1,128)} %bitcast.119, ...), custom_call_target="tpu_custom_call" | custom-call | tf_op jit(solution)/shard_map/mlp_backward/pallas_call | solution.py:448
  411.8 46.6 %attention_backward.2 = (bf16[1024,1024]{1,0:T(8,128)(2,1)}, bf16[3,1024,256]{2,1,0:T(8,128)(2,1)}, f32[256,1024]{1,0:T(8,128)}, f32[8,1024]{1,0:T(8,128)}, f32[8,256]{1,0:T(8,128)}) custom-call(f32[256,1024]{1,0:T(8,128)} %get-tuple-element.57.grad_middle, bf16[256,1024]{1,0:T(8,128)(2,1)} %get-tuple-element.53.x, f32[1,1024]{1,0:T(1,128)} %bitcast.121, ...), custom_call_target="tpu_custom_call" | custom-call | tf_op jit(solution)/shard_map/attention_backward/pallas_call | solution.py:448
  458.4 2.3 convert_convert_fusion.incoming
  460.7 33.4 %mlp_backward.3 = (bf16[1024,1024]{1,0:T(8,128)(2,1)}, bf16[1024,1024]{1,0:T(8,128)(2,1)}, f32[256,1024]{1,0:T(8,128)}, f32[8,1024]{1,0:T(8,128)}, f32[1,1024]{1,0:T(1,128)}) custom-call(f32[256,1024]{1,0:T(8,128)} %convert_convert_fusion.incoming, f32[256,1024]{1,0:T(8,128)} %get-tuple-element.52.middle, f32[1,1024]{1,0:T(1,128)} %bitcast.117, ...), custom_call_target="tpu_custom_call" | custom-call | tf_op jit(solution)/shard_map/mlp_backward/pallas_call | solution.py:448
  494.1 46.3 %attention_backward.3 = (bf16[1024,1024]{1,0:T(8,128)(2,1)}, bf16[3,1024,256]{2,1,0:T(8,128)(2,1)}, f32[256,1024]{1,0:T(8,128)}, f32[8,1024]{1,0:T(8,128)}, f32[8,256]{1,0:T(8,128)}) custom-call(f32[256,1024]{1,0:T(8,128)} %get-tuple-element.62.grad_middle, bf16[256,1024]{1,0:T(8,128)(2,1)} %dynamic-slice_bitcast_fusion.x, f32[1,1024]{1,0:T(1,128)} %bitcast.115, ...), custom_call_target="tpu_custom_call" | custom-call | tf_op jit(solution)/shard_map/attention_backward/pallas_call | solution.py:448
  540.5 2.5 convolution_convert_fusion.5
  543.0 1.7 broadcast_select_fusion.9
  544.7 1.6 collective-permute-start.17
  546.4 1.8 fusion.4
  548.4 1.8 fusion.7
  556.8 35.1 %collective-permute-done.16 = bf16[2,256]{1,0:T(2,128)(2,1)S(1)} collective-permute-done((bf16[2,256]{1,0:T(2,128)(2,1)S(1)}, bf16[2,256]{1,0:T(2,128)(2,1)S(1)}, u32[]{:S(2)}, u32[]{:S(2)}) %collective-permute-start.16) | collective-permute-done | bytes 1056 | tf_op jit(solution)/shard_map/ppermute | solution.py:535
  594.7 2.1 select_add_fusion.2
  596.8 5.9 convolution_convert_fusion.1
  602.8 2.8 bitcast_add_fusion
  605.9 4.8 broadcast_select_fusion.2
  610.7 2.3 collective-permute-start.20
  613.0 43.5 %collective-permute-done.20 = bf16[1024,1024]{1,0:T(8,128)(2,1)S(1)} collective-permute-done((bf16[1024,1024]{1,0:T(8,128)(2,1)S(1)}, bf16[1024,1024]{1,0:T(8,128)(2,1)S(1)}, u32[]{:S(2)}, u32[]{:S(2)}) %collective-permute-start.20) | collective-permute-done | bytes 2097184 | tf_op jit(solution)/shard_map/ppermute | solution.py:535
  656.5 1.7 select_add_fusion
  658.3 1.5 copy-done.28
  659.8 4.1 convolution_convert_fusion.3
  663.9 2.5 broadcast_select_fusion.3
  666.5 1.8 collective-permute-start.18
  668.3 42.9 %collective-permute-done.18 = bf16[1024,1024]{1,0:T(8,128)(2,1)S(1)} collective-permute-done((bf16[1024,1024]{1,0:T(8,128)(2,1)S(1)}, bf16[1024,1024]{1,0:T(8,128)(2,1)S(1)}, u32[]{:S(2)}, u32[]{:S(2)}) %collective-permute-start.18) | collective-permute-done | bytes 2097184 | tf_op jit(solution)/shard_map/ppermute | solution.py:535
  711.2 1.6 select_add_fusion.1
  714.8 1.5 collective-permute-start.19
  720.1 10.4 %all-reduce = bf16[1024]{0:T(1024)(128)(2,1)S(1)} all-reduce(bf16[1024]{0:T(1024)(128)(2,1)S(1)} %add.68), channel_id=10, replica_groups=mesh['section'=2,'tensor'=4,'dp'=4] {'dp'}, use_global_device_ids=true, to_apply=%region_6.7.clone | all-reduce | flops 1024 | bytes 4096
  743.2 1.6 bitcast_convert_fusion.2
  747.2 27.0 %reduce-scatter.17.cloned.1.call-done = bf16[1024,256]{1,0:T(8,128)(2,1)} async-done(((bf16[1024,1024]{1,0:T(8,128)(2,1)}), bf16[1024,256]{1,0:T(8,128)(2,1)}) %reduce-scatter.17.cloned.1.call-update) | async-done | bytes 524304 | tf_op jit(solution)/shard_map/reduce_scatter | solution.py:626
  774.2 2.1 bitcast_convert_fusion
  776.3 43.6 %reduce-scatter.15.cloned.1.call-done = bf16[256,1024]{1,0:T(8,128)(2,1)} async-done(((bf16[1024,1024]{1,0:T(8,128)(2,1)}), bf16[256,1024]{1,0:T(8,128)(2,1)}) %reduce-scatter.15.cloned.1.call-update) | async-done | bytes 524304 | tf_op jit(solution)/shard_map/reduce_scatter | solution.py:626
  819.8 2.1 bitcast_convert_fusion.1
  (172 shorter events, 50.9 us)
Async XLA Ops:
  7.2 11.3 %copy-start = (bf16[2,256,1024]{2,1,0:T(8,128)(2,1)S(1)}, bf16[2,256,1024]{2,1,0:T(8,128)(2,1)}, u32[]{:S(2)}) copy-start(bf16[2,256,1024]{2,1,0:T(8,128)(2,1)} %param.16) | copy-start | bytes 3145732
  7.2 12.1 %copy-start.14 = (bf16[2,256,1024]{2,1,0:T(8,128)(2,1)S(1)}, bf16[2,256,1024]{2,1,0:T(8,128)(2,1)}, u32[]{:S(2)}) copy-start(bf16[2,256,1024]{2,1,0:T(8,128)(2,1)} %param.17) | copy-start | bytes 3145732
  7.2 13.2 %copy-start.15 = (bf16[1,256,256]{2,1,0:T(8,128)(2,1)S(1)}, bf16[1,256,256]{2,1,0:T(8,128)(2,1)}, u32[]{:S(2)}) copy-start(bf16[1,256,256]{2,1,0:T(8,128)(2,1)} %param.24) | copy-start | bytes 393220
  7.2 59.7 %all-gather.11.cloned.1.call-start = ((), (), s32[]{:S(2)}) async-start(), calls=%async_computation.12 | async-start | bytes 2621440 | tf_op jit(solution)/shard_map/all_gather | solution.py:568
  8.0 95.9 %all-gather.7.cloned.1.call-start = ((), (), s32[]{:S(2)}) async-start(), calls=%async_computation.6 | async-start | bytes 1966080 | tf_op jit(solution)/shard_map/all_gather | solution.py:568
  8.0 60.4 %copy-start.27 = (f32[1,2,256]{2,1,0:T(2,128)S(1)}, f32[1,2,256]{2,1,0:T(2,128)}, u32[]{:S(2)}) copy-start(f32[1,2,256]{2,1,0:T(2,128)} %param.23) | copy-start | bytes 6148
  8.0 145.0 %copy-start.21 = (f32[1,1024]{1,0:T(1,128)S(1)}, f32[1,1024]{1,0:T(1,128)}, u32[]{:S(2)}) copy-start(f32[1,1024]{1,0:T(1,128)} %param.26) | copy-start | bytes 12292
  8.0 145.5 %copy-start.20 = (f32[1,1024]{1,0:T(1,128)S(1)}, f32[1,1024]{1,0:T(1,128)}, u32[]{:S(2)}) copy-start(f32[1,1024]{1,0:T(1,128)} %param.27) | copy-start | bytes 12292
  8.0 147.0 %copy-start.18 = (f32[1,1024]{1,0:T(1,128)S(1)}, f32[1,1024]{1,0:T(1,128)}, u32[]{:S(2)}) copy-start(f32[1,1024]{1,0:T(1,128)} %param.25) | copy-start | bytes 12292
  8.0 147.0 %copy-start.19 = (f32[1,1024]{1,0:T(1,128)S(1)}, f32[1,1024]{1,0:T(1,128)}, u32[]{:S(2)}) copy-start(f32[1,1024]{1,0:T(1,128)} %param.21) | copy-start | bytes 12292
  8.1 191.4 %copy-start.23 = (f32[1,1024]{1,0:T(1,128)S(1)}, f32[1,1024]{1,0:T(1,128)}, u32[]{:S(2)}) copy-start(f32[1,1024]{1,0:T(1,128)} %param.31) | copy-start | bytes 12292
  8.1 202.8 %copy-start.24 = (f32[1,1024]{1,0:T(1,128)S(1)}, f32[1,1024]{1,0:T(1,128)}, u32[]{:S(2)}) copy-start(f32[1,1024]{1,0:T(1,128)} %param.29) | copy-start | bytes 12292
  8.1 204.3 %copy-start.22 = (f32[1,1024]{1,0:T(1,128)S(1)}, f32[1,1024]{1,0:T(1,128)}, u32[]{:S(2)}) copy-start(f32[1,1024]{1,0:T(1,128)} %param.20) | copy-start | bytes 12292
  8.7 141.5 %all-gather.9.cloned.1.call-start = ((), (), s32[]{:S(2)}) async-start(), calls=%async_computation.11 | async-start | bytes 2621440 | tf_op jit(solution)/shard_map/all_gather | solution.py:568
  9.4 721.7 %reduce-scatter.21.cloned.1.call-start = ((), (), s32[]{:S(2)}) async-start(), calls=%async_computation.14 | async-start | bytes 81920
  9.5 59.0 %collective-permute-start.3 = (f32[2,256]{1,0:T(2,128)}, f32[2,256]{1,0:T(2,128)S(1)}, u32[]{:S(2)}, u32[]{:S(2)}) collective-permute-start(f32[2,256]{1,0:T(2,128)} %bitcast.147), channel_id=1, source_target_pairs={{0,16},{16,0},{1,17},{17,1},{2,18},{18,2},{3,19},{19,3},{4,20},{20... | collective-permute-start | bytes 6152 | tf_op jit(solution)/shard_map/ppermute | solution.py:535
  12.5 92.8 %collective-permute-start.1 = (f32[1024]{0:T(1024)}, f32[1024]{0:T(1024)S(1)}, u32[]{:S(2)}, u32[]{:S(2)}) collective-permute-start(f32[1024]{0:T(1024)} %bitcast.135), channel_id=1, source_target_pairs={{0,16},{16,0},{1,17},{17,1},{2,18},{18,2},{3,19},{19,3},{4,20},{20... | collective-permute-start | bytes 12296 | tf_op jit(solution)/shard_map/ppermute | solution.py:535
  12.6 140.4 %collective-permute-start.5 = (f32[1024]{0:T(1024)}, f32[1024]{0:T(1024)S(1)}, u32[]{:S(2)}, u32[]{:S(2)}) collective-permute-start(f32[1024]{0:T(1024)} %bitcast.133), channel_id=1, source_target_pairs={{0,16},{16,0},{1,17},{17,1},{2,18},{18,2},{3,19},{19,3},{4,20},{20... | collective-permute-start | bytes 12296 | tf_op jit(solution)/shard_map/ppermute | solution.py:535
  14.5 139.0 %collective-permute-start = (f32[1024]{0:T(1024)}, f32[1024]{0:T(1024)S(1)}, u32[]{:S(2)}, u32[]{:S(2)}) collective-permute-start(f32[1024]{0:T(1024)} %bitcast.141), channel_id=1, source_target_pairs={{0,16},{16,0},{1,17},{17,1},{2,18},{18,2},{3,19},{19,3},{4,20},{20... | collective-permute-start | bytes 12296 | tf_op jit(solution)/shard_map/ppermute | solution.py:535
  67.0 195.4 %collective-permute-start.10 = (bf16[1024,1024]{1,0:T(8,128)(2,1)}, bf16[1024,1024]{1,0:T(8,128)(2,1)}, u32[]{:S(2)}, u32[]{:S(2)}) collective-permute-start(bf16[1024,1024]{1,0:T(8,128)(2,1)} %bitcast.107), channel_id=1, source_target_pairs={{0,16},{16,0},{1,17},{17,1},{2,18},{18,2},{3,19},{19,3},{4,20},{20... | collective-permute-start | bytes 6291464 | tf_op jit(solution)/shard_map/ppermute | solution.py:535
  103.9 112.3 %copy-start.11 = (bf16[3,1024,256]{2,1,0:T(8,128)(2,1)S(1)}, bf16[3,1024,256]{2,1,0:T(8,128)(2,1)}, u32[]{:S(2)}) copy-start(bf16[3,1024,256]{2,1,0:T(8,128)(2,1)} %all-gather.7.cloned.1.call-done) | copy-start | bytes 4718596
  103.9 112.3 %collective-permute-start.2 = (bf16[3,1024,256]{2,1,0:T(8,128)(2,1)}, bf16[3,1024,256]{2,1,0:T(8,128)(2,1)}, u32[]{:S(2)}, u32[]{:S(2)}) collective-permute-start(bf16[3,1024,256]{2,1,0:T(8,128)(2,1)} %all-gather.7.cloned.1.call-done), channel_id=1, source_target_pairs={{0,16},{16,0},{1,17},{17,1},{2,18},{18,2},{3,19},{19,3},{4,20},{20... | collective-permute-start | bytes 4718600 | tf_op jit(solution)/shard_map/ppermute | solution.py:535
  150.2 116.2 %collective-permute-start.8 = (bf16[1024,1024]{1,0:T(8,128)(2,1)}, bf16[1024,1024]{1,0:T(8,128)(2,1)}, u32[]{:S(2)}, u32[]{:S(2)}) collective-permute-start(bf16[1024,1024]{1,0:T(8,128)(2,1)} %bitcast.108), channel_id=1, source_target_pairs={{0,16},{16,0},{1,17},{17,1},{2,18},{18,2},{3,19},{19,3},{4,20},{20... | collective-permute-start | bytes 6291464 | tf_op jit(solution)/shard_map/ppermute | solution.py:535
  153.0 45.0 %collective-permute-start.6 = (f32[1024]{0:T(1024)S(1)}, f32[1024]{0:T(1024)S(1)}, u32[]{:S(2)}, u32[]{:S(2)}) collective-permute-start(f32[1024]{0:T(1024)S(1)} %bitcast.139), channel_id=1, source_target_pairs={{0,16},{16,0},{1,17},{17,1},{2,18},{18,2},{3,19},{19,3},{4,20},{20... | collective-permute-start | bytes 12296 | tf_op jit(solution)/shard_map/ppermute | solution.py:535
  153.5 46.0 %collective-permute-start.7 = (f32[1024]{0:T(1024)S(1)}, f32[1024]{0:T(1024)S(1)}, u32[]{:S(2)}, u32[]{:S(2)}) collective-permute-start(f32[1024]{0:T(1024)S(1)} %bitcast.137), channel_id=1, source_target_pairs={{0,16},{16,0},{1,17},{17,1},{2,18},{18,2},{3,19},{19,3},{4,20},{20... | collective-permute-start | bytes 12296 | tf_op jit(solution)/shard_map/ppermute | solution.py:535
  198.0 17.1 %collective-permute-start.4 = (bf16[256,1024]{1,0:T(8,128)(2,1)S(1)}, bf16[256,1024]{1,0:T(8,128)(2,1)S(1)}, u32[]{:S(2)}, u32[]{:S(2)}) collective-permute-start(bf16[256,1024]{1,0:T(8,128)(2,1)S(1)} %bitcast.110), channel_id=1, source_target_pairs={{0,16},{16,0},{1,17},{17,1},{2,18},{18,2},{3,19},{19,3},{4,20},{20... | collective-permute-start | bytes 1572872 | tf_op jit(solution)/shard_map/ppermute | solution.py:535
  199.5 11.4 %collective-permute-start.11 = (f32[1024]{0:T(1024)S(1)}, f32[1024]{0:T(1024)S(1)}, u32[]{:S(2)}, u32[]{:S(2)}) collective-permute-start(f32[1024]{0:T(1024)S(1)} %bitcast.143), channel_id=1, source_target_pairs={{0,16},{16,0},{1,17},{17,1},{2,18},{18,2},{3,19},{19,3},{4,20},{20... | collective-permute-start | bytes 12296 | tf_op jit(solution)/shard_map/ppermute | solution.py:535
  210.9 3.6 collective-permute-start.9
  219.5 42.9 %copy-start.6 = (bf16[1,1024,1024]{2,1,0:T(8,128)(2,1)S(1)}, bf16[1,1024,1024]{2,1,0:T(8,128)(2,1)}, u32[]{:S(2)}) copy-start(bf16[1,1024,1024]{2,1,0:T(8,128)(2,1)} %all-gather.11.cloned.1.call-done) | copy-start | bytes 6291460
  494.1 46.4 %copy-start.13 = (bf16[1024,256]{1,0:T(8,128)(2,1)S(1)}, bf16[1024,256]{1,0:T(8,128)(2,1)}, u32[]{:S(2)}) copy-start(bf16[1024,256]{1,0:T(8,128)(2,1)} %get-tuple-element.76) | copy-start | bytes 1572868
  544.7 49.9 %collective-permute-start.17 = (bf16[256,1024]{1,0:T(8,128)(2,1)}, bf16[256,1024]{1,0:T(8,128)(2,1)}, u32[]{:S(2)}, u32[]{:S(2)}) collective-permute-start(bf16[256,1024]{1,0:T(8,128)(2,1)} %get-tuple-element.160), channel_id=1, source_target_pairs={{0,16},{16,0},{1,17},{17,1},{2,18},{18,2},{3,19},{19,3},{4,20},{20... | collective-permute-start | bytes 1572872 | tf_op jit(solution)/shard_map/ppermute | solution.py:535
  550.2 5.6 copy-start.16
  551.6 51.2 %collective-permute-start.15 = (bf16[3,1024,256]{1,2,0:T(8,128)(2,1)}, bf16[3,1024,256]{1,2,0:T(8,128)(2,1)}, u32[]{:S(2)}, u32[]{:S(2)}) collective-permute-start(bf16[3,1024,256]{1,2,0:T(8,128)(2,1)} %select_bitcast_fusion), channel_id=1, source_target_pairs={{0,16},{16,0},{1,17},{17,1},{2,18},{18,2},{3,19},{19,3},{4,20},{20... | collective-permute-start | bytes 4718600 | tf_op jit(solution)/shard_map/ppermute | solution.py:535
  553.2 38.8 %collective-permute-start.16 = (bf16[2,256]{1,0:T(2,128)(2,1)S(1)}, bf16[2,256]{1,0:T(2,128)(2,1)S(1)}, u32[]{:S(2)}, u32[]{:S(2)}) collective-permute-start(bf16[2,256]{1,0:T(2,128)(2,1)S(1)} %broadcast_select_fusion.25), channel_id=1, source_target_pairs={{0,16},{16,0},{1,17},{17,1},{2,18},{18,2},{3,19},{19,3},{4,20},{20... | collective-permute-start | bytes 3080 | tf_op jit(solution)/shard_map/ppermute | solution.py:535
  555.9 37.6 %collective-permute-start.14 = (f32[6,1024]{1,0:T(8,128)S(1)}, f32[6,1024]{1,0:T(8,128)S(1)}, u32[]{:S(2)}, u32[]{:S(2)}) collective-permute-start(f32[6,1024]{1,0:T(8,128)S(1)} %fusion.10), channel_id=1, source_target_pairs={{0,16},{16,0},{1,17},{17,1},{2,18},{18,2},{3,19},{19,3},{4,20},{20... | collective-permute-start | bytes 73736 | tf_op jit(solution)/shard_map/ppermute | solution.py:535
  593.5 139.1 %reduce-scatter.19.cloned.1.call-start = ((), (), s32[]{:S(2)}) async-start(), calls=%async_computation.13 | async-start | bytes 557056
  594.6 148.6 %reduce-scatter.13.cloned.1.call-start = ((), (), s32[]{:S(2)}) async-start(), calls=%async_computation.8 | async-start | bytes 655360 | tf_op jit(solution)/shard_map/reduce_scatter | solution.py:626
  596.8 148.1 %reduce-scatter.11.cloned.1.call-start = ((), (), s32[]{:S(2)}) async-start(), calls=%async_computation.7 | async-start | bytes 1966080 | tf_op jit(solution)/shard_map/reduce_scatter | solution.py:626
  605.6 168.6 %reduce-scatter.17.cloned.1.call-start = ((), (), s32[]{:S(2)}) async-start(), calls=%async_computation.10 | async-start | bytes 2621440 | tf_op jit(solution)/shard_map/reduce_scatter | solution.py:626
  605.9 50.6 %copy-start.10 = (bf16[1024,1024]{1,0:T(8,128)(2,1)S(1)}, bf16[1024,1024]{1,0:T(8,128)(2,1)}, u32[]{:S(2)}) copy-start(bf16[1024,1024]{1,0:T(8,128)(2,1)} %convolution_convert_fusion.1) | copy-start | bytes 6291460
  610.7 45.9 %collective-permute-start.20 = (bf16[1024,1024]{1,0:T(8,128)(2,1)S(1)}, bf16[1024,1024]{1,0:T(8,128)(2,1)S(1)}, u32[]{:S(2)}, u32[]{:S(2)}) collective-permute-start(bf16[1024,1024]{1,0:T(8,128)(2,1)S(1)} %get-tuple-element.164), channel_id=1, source_target_pairs={{0,16},{16,0},{1,17},{17,1},{2,18},{18,2},{3,19},{19,3},{4,20},{20... | collective-permute-start | bytes 6291464 | tf_op jit(solution)/shard_map/ppermute | solution.py:535
  658.2 161.6 %reduce-scatter.15.cloned.1.call-start = ((), (), s32[]{:S(2)}) async-start(), calls=%async_computation.9 | async-start | bytes 2621440 | tf_op jit(solution)/shard_map/reduce_scatter | solution.py:626
  666.5 44.7 %collective-permute-start.18 = (bf16[1024,1024]{1,0:T(8,128)(2,1)S(1)}, bf16[1024,1024]{1,0:T(8,128)(2,1)S(1)}, u32[]{:S(2)}, u32[]{:S(2)}) collective-permute-start(bf16[1024,1024]{1,0:T(8,128)(2,1)S(1)} %get-tuple-element.162), channel_id=1, source_target_pairs={{0,16},{16,0},{1,17},{17,1},{2,18},{18,2},{3,19},{19,3},{4,20},{20... | collective-permute-start | bytes 6291464 | tf_op jit(solution)/shard_map/ppermute | solution.py:535
  712.8 5.0 copy-start.3
  714.8 5.3 collective-permute-start.19
  717.2 23.3 %collective-permute-start.13 = (bf16[256,1024]{1,0:T(8,128)(2,1)}, bf16[256,1024]{1,0:T(8,128)(2,1)}, u32[]{:S(2)}, u32[]{:S(2)}) collective-permute-start(bf16[256,1024]{1,0:T(8,128)(2,1)} %broadcast_select_fusion.10), channel_id=1, source_target_pairs={{0,16},{16,0},{1,17},{17,1},{2,18},{18,2},{3,19},{19,3},{4,20},{20... | collective-permute-start | bytes 1572872 | tf_op jit(solution)/shard_map/ppermute | solution.py:535
  718.6 19.7 %collective-permute-start.12 = (bf16[256,1024]{1,0:T(8,128)(2,1)}, bf16[256,1024]{1,0:T(8,128)(2,1)}, u32[]{:S(2)}, u32[]{:S(2)}) collective-permute-start(bf16[256,1024]{1,0:T(8,128)(2,1)} %broadcast_select_fusion.12), channel_id=1, source_target_pairs={{0,16},{16,0},{1,17},{17,1},{2,18},{18,2},{3,19},{19,3},{4,20},{20... | collective-permute-start | bytes 1572872 | tf_op jit(solution)/shard_map/ppermute | solution.py:535
  744.9 77.1 %copy-start.1 = (bf16[2,256,1024]{2,1,0:T(8,128)(2,1)S(1)}, bf16[2,256,1024]{2,1,0:T(8,128)(2,1)}, u32[]{:S(2)}) copy-start(bf16[2,256,1024]{2,1,0:T(8,128)(2,1)} %param.16) | copy-start | bytes 3145732
  (18 other events, 54.1 us)
Sparse Core Ops, SparseCore 0:
  9.6 57.3 all-gather.10
  68.5 35.2 all-gather.6
  105.4 44.7 all-gather.8
  593.6 18.0 reduce-scatter.20
  616.0 53.9 reduce-scatter.18
  672.2 20.6 reduce-scatter.12
  695.2 33.7 reduce-scatter.10
  731.3 42.8 reduce-scatter.16
  776.6 43.1 reduce-scatter.14

commit v3 on v2

--- a/solution.py
+++ b/solution.py
@@ -164,12 +164,16 @@
     penalty_ref[...] = lax.broadcasted_iota(jnp.int32, penalty_ref.shape, 0).astype(F32)
 
 
-def attend_forward(proj, context, totals, slopes, penalty, block):
+def nothing():
+    pass
+
+
+def attend_forward(proj, context, totals, slopes, penalty, block, tick=nothing):
     length, width = context.shape
-
-    def pair_step(pair, carry):
-        lanes = pl.ds(pl.multiple_of(pair * PAIR, PAIR), PAIR)
+    for pair in range(width // PAIR):
+        lanes = pl.ds(pair * PAIR, PAIR)
         for start in range(0, length, block):
+            tick()
             stop = start + block
             queries = proj[0, start:stop, lanes] * jnp.asarray(0.125, BF16)
             keys = proj[1, :stop, lanes]
@@ -186,9 +190,6 @@
                 outs.append(mixed / total)
                 totals[pl.ds(head, 1), start:stop] = highest + jnp.log(total)
             context[start:stop, lanes] = jnp.concatenate(outs, axis=0).T.astype(BF16)
-        return carry
-
-    lax.fori_loop(0, width // PAIR, pair_step, 0)
 
 
 def attend_backward(proj, grad_context, totals, slopes, penalty, grad_proj, sums, block):
@@ -234,53 +235,114 @@
     lax.fori_loop(0, width // PAIR, pair_step, 0)
 
 
+def attention_forward_body(
+    ring, gather, scatter, x, gain, shift, w_qkv, b_qkv, w_out, b_out, slopes,
+    normed, proj, context, totals, middle, penalty,
+    qkv_ready=nothing, out_ready=nothing, tick=nothing,
+):
+    block, chunk = ring.block, ring.chunk
+    for c in range(CHUNKS):
+        at = pl.ds(c * chunk, chunk)
+        unit, _ = normalize(x[at].astype(F32))
+        normed[ring.rows(ring.me, c)] = (unit * gain() + shift()).astype(BF16)
+        gather.start(c)
+    qkv_ready()
+
+    def project(owner, c, size):
+        at = rows_at(owner * block + c * chunk, size)
+        rows = normed[at]
+        for part in range(3):
+            made = mm(rows, w_qkv[part])
+            proj[part, at] = (made if part == 1 else made + b_qkv(part)).astype(BF16)
+
+    project(ring.me, 0, block)
+    for c in range(CHUNKS):
+        gather.arrived_mate(c)
+    project(ring.mate, 0, block)
+    for c in range(CHUNKS):
+        gather.arrived_peer(c)
+        project(ring.peer, c, chunk)
+        gather.arrived_far(c)
+        project(ring.far, c, chunk)
+    attend_forward(proj, context, totals, slopes, penalty, block, tick)
+    out_ready()
+
+    def part_of(owner, c):
+        return mm(context[ring.rows(owner, c)], w_out[...])
+
+    for c in range(CHUNKS):
+        scatter.put(0, c, part_of(ring.far, c))
+        scatter.put(1, c, part_of(ring.peer, c) + scatter.take(0, c))
+    for c in range(CHUNKS):
+        scatter.put(2, c, part_of(ring.mate, c))
+    for c in range(CHUNKS):
+        at = pl.ds(c * chunk, chunk)
+        total = part_of(ring.me, c) + scatter.take(2, c) + scatter.take(1, c)
+        middle[at] = x[at].astype(F32) + total + b_out()
+
+
+def mlp_forward_body(
+    ring, gather, scatter, middle, gain, shift, w_up, b_up, w_down, b_down,
+    second, activated, slope_of, leaving, own,
+    ready=nothing, tick=nothing,
+):
+    block, chunk = ring.block, ring.chunk
+    for c in range(CHUNKS):
+        at = pl.ds(c * chunk, chunk)
+        unit, _ = normalize(middle[at])
+        second[ring.rows(ring.me, c)] = (unit * gain() + shift()).astype(BF16)
+        gather.start(c)
+
+    def expand(at):
+        upward = mm(second[at], w_up[...]) + b_up()
+        inner = jnp.tanh(GELU_SCALE * (upward + 0.044715 * upward * upward * upward))
+        half = 0.5 * (1.0 + inner)
+        value = upward * half
+        slope = half + 0.5 * upward * (1.0 - inner * inner) * GELU_SCALE * (
+            1.0 + 3 * 0.044715 * upward * upward
+        )
+        value = value.astype(BF16)
+        activated[at] = value
+        slope_of[at] = slope.astype(BF16)
+        return mm(value, w_down[...])
+
+    ready()
+    own[...] = expand(rows_at(ring.me * block, block))
+    tick()
+    for c in range(CHUNKS):
+        gather.arrived_mate(c)
+    part = expand(rows_at(ring.mate * block, block))
+    for c in range(CHUNKS):
+        scatter.put(2, c, part[c * chunk : (c + 1) * chunk])
+    tick()
+    for c in range(CHUNKS):
+        gather.arrived_peer(c)
+        peer_part = expand(ring.rows(ring.peer, c))
+        gather.arrived_far(c)
+        scatter.put(0, c, expand(ring.rows(ring.far, c)))
+        scatter.put(1, c, peer_part + scatter.take(0, c))
+        tick()
+    for c in range(CHUNKS):
+        at = pl.ds(c * chunk, chunk)
+        total = own[at] + scatter.take(2, c) + scatter.take(1, c)
+        leaving[at] = (middle[at] + total + b_down()).astype(BF16)
+
+
 def attention_forward_kernel(
     x, gain, shift, w_qkv, b_qkv, w_out, b_out, slopes,
     normed, proj, context, totals, middle,
     penalty, stage, land, gather_sems, scatter_sems,
 ):
-    block = x.shape[0]
-    ring = Ring(block)
+    ring = Ring(x.shape[0])
     ring.greet()
     gather = Gather(ring, normed, gather_sems)
-    chunk = ring.chunk
-    for c in range(CHUNKS):
-        at = pl.ds(c * chunk, chunk)
-        unit, _ = normalize(x[at].astype(F32))
-        normed[ring.rows(ring.me, c)] = (unit * gain[...] + shift[...]).astype(BF16)
-        gather.start(c)
+    scatter = Scatter(ring, stage, land, scatter_sems)
     fill_penalty(penalty)
-
-    def project(owner, c, size):
-        at = rows_at(owner * block + c * chunk, size)
-        rows = normed[at]
-        for part in range(3):
-            proj[part, at] = (mm(rows, w_qkv[part]) + b_qkv[part]).astype(BF16)
-
-    project(ring.me, 0, block)
-    for c in range(CHUNKS):
-        gather.arrived_mate(c)
-    project(ring.mate, 0, block)
-    for c in range(CHUNKS):
-        gather.arrived_peer(c)
-        project(ring.peer, c, chunk)
-        gather.arrived_far(c)
-        project(ring.far, c, chunk)
-    attend_forward(proj, context, totals, slopes, penalty, block)
-    scatter = Scatter(ring, stage, land, scatter_sems)
-
-    def part_of(owner, c):
-        return mm(context[ring.rows(owner, c)], w_out[...])
-
-    for c in range(CHUNKS):
-        scatter.put(0, c, part_of(ring.far, c))
-        scatter.put(1, c, part_of(ring.peer, c) + scatter.take(0, c))
-    for c in range(CHUNKS):
-        scatter.put(2, c, part_of(ring.mate, c))
-    for c in range(CHUNKS):
-        at = pl.ds(c * chunk, chunk)
-        total = part_of(ring.me, c) + scatter.take(2, c) + scatter.take(1, c)
-        middle[at] = x[at].astype(F32) + total + b_out[...]
+    attention_forward_body(
+        ring, gather, scatter, x, lambda: gain[...], lambda: shift[...], w_qkv,
+        lambda part: b_qkv[part], w_out, lambda: b_out[...], slopes,
+        normed, proj, context, totals, middle, penalty,
+    )
     gather.finish()
     scatter.finish()
 
@@ -290,47 +352,15 @@
     second, activated, slope_of, leaving,
     own, stage, land, gather_sems, scatter_sems,
 ):
-    block = middle.shape[0]
-    ring = Ring(block)
+    ring = Ring(middle.shape[0])
     ring.greet()
     gather = Gather(ring, second, gather_sems)
     scatter = Scatter(ring, stage, land, scatter_sems)
-    chunk = ring.chunk
-    for c in range(CHUNKS):
-        at = pl.ds(c * chunk, chunk)
-        unit, _ = normalize(middle[at])
-        second[ring.rows(ring.me, c)] = (unit * gain[...] + shift[...]).astype(BF16)
-        gather.start(c)
-
-    def expand(at):
-        upward = mm(second[at], w_up[...]) + b_up[...]
-        inner = jnp.tanh(GELU_SCALE * (upward + 0.044715 * upward * upward * upward))
-        half = 0.5 * (1.0 + inner)
-        value = upward * half
-        slope = half + 0.5 * upward * (1.0 - inner * inner) * GELU_SCALE * (
-            1.0 + 3 * 0.044715 * upward * upward
-        )
-        value = value.astype(BF16)
-        activated[at] = value
-        slope_of[at] = slope.astype(BF16)
-        return mm(value, w_down[...])
-
-    own[...] = expand(rows_at(ring.me * block, block))
-    for c in range(CHUNKS):
-        gather.arrived_mate(c)
-    part = expand(rows_at(ring.mate * block, block))
-    for c in range(CHUNKS):
-        scatter.put(2, c, part[c * chunk : (c + 1) * chunk])
-    for c in range(CHUNKS):
-        gather.arrived_peer(c)
-        peer_part = expand(ring.rows(ring.peer, c))
-        gather.arrived_far(c)
-        scatter.put(0, c, expand(ring.rows(ring.far, c)))
-        scatter.put(1, c, peer_part + scatter.take(0, c))
-    for c in range(CHUNKS):
-        at = pl.ds(c * chunk, chunk)
-        total = own[at] + scatter.take(2, c) + scatter.take(1, c)
-        leaving[at] = (middle[at] + total + b_down[...]).astype(BF16)
+    mlp_forward_body(
+        ring, gather, scatter, middle, lambda: gain[...], lambda: shift[...], w_up,
+        lambda: b_up[...], w_down, lambda: b_down[...],
+        second, activated, slope_of, leaving, own,
+    )
     gather.finish()
     scatter.finish()
 
@@ -530,9 +560,404 @@
     return grad_hidden, small, large
 
 
+class Cross:
+    def __init__(self, layer, shards, whole, sems):
+        self.layer, self.shards, self.whole = layer, shards, whole
+        self.first, self.line, self.last, self.local = sems
+        self.section, self.place = lax.axis_index("section"), lax.axis_index("dp")
+        self.count = lax.axis_size("dp")
+        self.other = 1 - self.section
+        self.owner = self.section == layer
+        self.half = jnp.where(self.owner, 0, 1)
+
+    def at(self, i, half, place):
+        ref = self.whole[i]
+        if i == 0:
+            rows = self.shards[i].shape[1] // 2
+            return ref.at[:, rows_at((place * 2 + half) * rows, rows), :]
+        rows = self.shards[i].shape[0] // 2
+        if i == 2:
+            return ref.at[rows_at((place * 2 + half) * rows, rows), :]
+        return ref.at[rows_at(half * rows, rows), rows_at(place * self.shards[i].shape[1], self.shards[i].shape[1])]
+
+    def mine(self, i, half):
+        ref = self.shards[i]
+        rows = ref.shape[1 if i == 0 else 0] // 2
+        return ref.at[:, pl.ds(half * rows, rows), :] if i == 0 else ref.at[pl.ds(half * rows, rows), :]
+
+    def copy(self, src, dst, sems, where, device):
+        return pltpu.make_async_remote_copy(
+            src_ref=src,
+            dst_ref=dst,
+            send_sem=sems.at[(0,) + where],
+            recv_sem=sems.at[(1,) + where],
+            device_id=device,
+            device_id_type=MESH,
+        )
+
+    def over_first(self, i):
+        return self.copy(
+            self.mine(i, 1), self.at(i, 1, self.place), self.first, (i,), {"section": self.other}
+        )
+
+    def over_last(self, i, place, src=None):
+        at = self.at(i, self.half, place)
+        return self.copy(at if src is None else src, at, self.last, (i, place), {"section": self.other})
+
+    def from_last(self, i, place):
+        at = self.at(i, 1 - self.half, place)
+        return self.copy(at, at, self.last, (i, place), {"section": self.other})
+
+    def along(self, i, place, right, src=None):
+        at = self.at(i, self.half, place)
+        return self.copy(
+            at if src is None else src,
+            at,
+            self.line,
+            (i, place, int(right)),
+            {"dp": self.place + (1 if right else -1)},
+        )
+
+    def onward(self, i, place, right, src=None):
+        @pl.when(self.place + 1 < self.count if right else self.place > 0)
+        def _():
+            self.along(i, place, right, src).start()
+
+    def keep(self, i, half):
+        return pltpu.make_async_copy(
+            self.mine(i, half), self.at(i, half, self.place), self.local.at[i, half]
+        )
+
+    def begin(self, i):
+        @pl.when(self.owner)
+        def _():
+            self.over_first(i).start()
+
+    def start(self, i):
+        @pl.when(self.owner)
+        def _():
+            for right in (True, False):
+                self.onward(i, self.place, right, self.mine(i, 0))
+            self.over_last(i, self.place, self.mine(i, 0)).start()
+            for half in range(2):
+                self.keep(i, half).start()
+
+        @pl.when(jnp.logical_not(self.owner))
+        def _():
+            self.over_first(i).wait_recv()
+            for right in (True, False):
+                self.onward(i, self.place, right)
+
+    def step(self, i, hops):
+        for right in (True, False):
+            place = self.place - hops if right else self.place + hops
+
+            @pl.when(place >= 0 if right else place < self.count)
+            def _():
+                self.along(i, place, right).wait_recv()
+                self.over_last(i, place).start()
+                self.onward(i, place, right)
+
+    def finish(self, i):
+        @pl.when(self.owner)
+        def _():
+            for half in range(2):
+                self.keep(i, half).wait()
+
+        for place in range(self.count):
+
+            @pl.when(jnp.logical_or(jnp.logical_not(self.owner), place != self.place))
+            def _():
+                self.from_last(i, place).wait_recv()
+
+    def drain(self, i):
+        @pl.when(self.owner)
+        def _():
+            self.over_first(i).wait_send()
+
+        for place in range(self.count):
+
+            @pl.when(jnp.logical_or(self.owner, place != self.place))
+            def _():
+                self.over_last(i, place).wait_send()
+
+            @pl.when(jnp.logical_and(place <= self.place, self.place + 1 < self.count))
+            def _():
+                self.along(i, place, True).wait_send()
+
+            @pl.when(jnp.logical_and(place >= self.place, self.place > 0))
+            def _():
+                self.along(i, place, False).wait_send()
+
+
+def cross_scratch(layers, count):
+    pieces = 4
+    return [
+        pltpu.SemaphoreType.DMA((layers, 2, pieces)),
+        pltpu.SemaphoreType.DMA((layers, 2, pieces, count, 2)),
+        pltpu.SemaphoreType.DMA((layers, 2, pieces, count)),
+        pltpu.SemaphoreType.DMA((layers, pieces, 2)),
+    ]
+
+
+def greet_all(ring):
+    barrier = pltpu.get_barrier_semaphore()
+    section, place, count = lax.axis_index("section"), lax.axis_index("dp"), lax.axis_size("dp")
+    for device in ({"tensor": ring.mate}, {"tensor": ring.peer}, {"section": 1 - section}):
+        pl.semaphore_signal(barrier, inc=1, device_id=device, device_id_type=MESH)
+
+    @pl.when(place > 0)
+    def _():
+        pl.semaphore_signal(barrier, inc=1, device_id={"dp": place - 1}, device_id_type=MESH)
+
+    @pl.when(place + 1 < count)
+    def _():
+        pl.semaphore_signal(barrier, inc=1, device_id={"dp": place + 1}, device_id_type=MESH)
+
+    pl.semaphore_wait(barrier, 3 + jnp.where(place > 0, 1, 0) + jnp.where(place + 1 < count, 1, 0))
+
+
+class Pump:
+    def __init__(self, crossings):
+        self.pieces = [(crossing, i) for crossing in crossings for i in range(4)]
+        self.hops = crossings[0].count
+        self.done = 0
+        for piece in range(2):
+            self.begin(piece)
+
+    def begin(self, piece):
+        if piece < len(self.pieces):
+            crossing, i = self.pieces[piece]
+            crossing.begin(i)
+
+    def stage(self, number):
+        self.begin(number + 2)
+        for hops in range(self.hops):
+            if 0 <= number - hops < len(self.pieces):
+                crossing, i = self.pieces[number - hops]
+                if hops == 0:
+                    crossing.start(i)
+                else:
+                    crossing.step(i, hops)
+
+    def until(self, number):
+        while self.done <= min(number, len(self.pieces) + self.hops - 2):
+            self.stage(self.done)
+            self.done += 1
+
+    def tick(self):
+        self.until(self.done)
+
+    def have(self, piece):
+        self.until(piece + self.hops - 1)
+        crossing, i = self.pieces[piece]
+        crossing.finish(i)
+
+    def drain(self):
+        for crossing, i in self.pieces:
+            crossing.drain(i)
+
+
+KEPT = 6
+SMALL_ROWS = 8
+
+
+def forward_kernel(layers, *refs):
+    (x, vector, *shards), refs = refs[:6], refs[6:]
+    slopes, refs = refs[0], refs[1:]
+    outs, refs = [refs[j * 13 : (j + 1) * 13] for j in range(layers)], refs[13 * layers :]
+    vectors, refs = refs[0], refs[1:]
+    held, refs = [refs[j * 10 : (j + 1) * 10] for j in range(layers)], refs[10 * layers :]
+    penalty, own, stage, land, gather_sems, scatter_sems, save_sems, vector_sems = refs[:8]
+    cross_sems = refs[8:]
+    ring = Ring(x.shape[0])
+    section = lax.axis_index("section")
+    greet_all(ring)
+    crossings = [
+        Cross(l, shards, held[l][6:10], [sem.at[l] for sem in cross_sems]) for l in range(layers)
+    ]
+    pump = Pump(crossings)
+    vector_out = pltpu.make_async_remote_copy(
+        src_ref=vector,
+        dst_ref=vectors.at[section],
+        send_sem=vector_sems.at[0],
+        recv_sem=vector_sems.at[1],
+        device_id={"section": 1 - section},
+        device_id_type=MESH,
+    )
+    vector_in = pltpu.make_async_remote_copy(
+        src_ref=vector,
+        dst_ref=vectors.at[1 - section],
+        send_sem=vector_sems.at[0],
+        recv_sem=vector_sems.at[1],
+        device_id={"section": 1 - section},
+        device_id_type=MESH,
+    )
+    vector_out.start()
+    vectors[section] = vector[...]
+    fill_penalty(penalty)
+    vector_in.wait_recv()
+    saves = []
+
+    def save(l, i, src):
+        copy = pltpu.make_async_copy(src, outs[l][i], save_sems.at[l, i])
+        copy.start()
+        saves.append(copy)
+
+    links = []
+    entering = x
+    for l in range(layers):
+        normed, proj, context, second, activated, slope_of, wq, wo, wu, wd = held[l]
+        totals, middle, leaving = outs[l][10:13]
+
+        def row(i):
+            return lambda: vectors[l, pl.ds(i, 1), :]
+
+        def qv(part):
+            local = context.shape[1]
+            return vectors[l, pl.ds(7, 1), pl.ds((part // 2) * local, local)]
+
+        def link(every, phase):
+            gather = Gather(ring, every, gather_sems.at[phase])
+            scatter = Scatter(ring, stage.at[phase], land.at[phase], scatter_sems.at[phase])
+            links.append((gather, scatter))
+            return gather, scatter
+
+        def have(i):
+            pump.have(l * 4 + i)
+            save(l, 6 + i, held[l][6 + i])
+
+        gather, scatter = link(normed, 0)
+        attention_forward_body(
+            ring, gather, scatter, entering, row(0), row(1), wq, qv, wo, row(2), slopes,
+            normed, proj, context, totals, middle, penalty,
+            qkv_ready=lambda: have(0), out_ready=lambda: have(1), tick=pump.tick,
+        )
+        save(l, 0, normed)
+        save(l, 1, proj)
+        save(l, 2, context)
+        gather.finish()
+        scatter.finish()
+        gather, scatter = link(second, 1)
+
+        def ready():
+            have(2)
+            have(3)
+
+        mlp_forward_body(
+            ring, gather, scatter, middle, row(3), row(4), wu, row(5), wd, row(6),
+            second, activated, slope_of, leaving, own,
+            ready=ready, tick=pump.tick,
+        )
+        save(l, 3, second)
+        save(l, 4, activated)
+        save(l, 5, slope_of)
+        gather.finish()
+        scatter.finish()
+        entering = leaving
+    vector_out.wait_send()
+    pump.drain()
+    for copy in saves:
+        copy.wait()
+
+
+def forward_call(x, vector, shards, slopes):
+    layers, places = lax.axis_size("section"), lax.axis_size("dp")
+    block, width = x.shape
+    length = block * lax.axis_size("tensor")
+    sq, so, su, sd = shards
+    local, units = so.shape[0], sd.shape[0]
+    heads = local // HEAD
+    kept = [
+        ((length, width), BF16),
+        ((3, length, local), BF16),
+        ((length, local), BF16),
+        ((length, width), BF16),
+        ((length, units), BF16),
+        ((length, units), BF16),
+        ((3, width, local), BF16),
+        ((local, width), BF16),
+        ((width, units), BF16),
+        ((units, width), BF16),
+    ]
+    near = [((heads, length), F32), ((block, width), F32), ((block, width), BF16)]
+    vmem, far = pl.BlockSpec(memory_space=pltpu.VMEM), pl.BlockSpec(memory_space=pl.ANY)
+    made = pl.pallas_call(
+        functools.partial(forward_kernel, layers),
+        out_shape=[jax.ShapeDtypeStruct(shape, dtype) for _ in range(layers) for shape, dtype in kept + near]
+        + [jax.ShapeDtypeStruct((layers,) + vector.shape, F32)],
+        in_specs=[vmem, vmem] + [far] * 4 + [vmem],
+        out_specs=([far] * len(kept) + [vmem] * len(near)) * layers + [vmem],
+        scratch_shapes=[pltpu.VMEM(shape, dtype) for _ in range(layers) for shape, dtype in kept]
+        + [
+            pltpu.VMEM((length, block), F32),
+            pltpu.VMEM((block, width), F32),
+            pltpu.VMEM((2, 3, block, width), BF16),
+            pltpu.VMEM((2, 3, block, width), BF16),
+            pltpu.SemaphoreType.DMA((2, 2, 3, CHUNKS)),
+            pltpu.SemaphoreType.DMA((2, 2, 3, CHUNKS)),
+            pltpu.SemaphoreType.DMA((layers, len(kept))),
+            pltpu.SemaphoreType.DMA((2,)),
+        ]
+        + cross_scratch(layers, places),
+        compiler_params=pltpu.CompilerParams(
+            collective_id=5, has_side_effects=True, vmem_limit_bytes=VMEM_LIMIT
+        ),
+        name="forward",
+    )(x, vector, sq, so, su, sd, slopes)
+    saved, weights = [], []
+    entering = x
+    vectors = made[-1]
+    for l in range(layers):
+        normed, proj, context, second, activated, slope_of, wq, wo, wu, wd, totals, middle, leaving = made[13 * l : 13 * l + 13]
+        saved.append(dict(x=entering, normed=normed, proj=proj, context=context, totals=totals, middle=middle, second=second, activated=activated, slope_of=slope_of))
+        weights.append(dict(qkv=wq, out=wo, up=wu, down=wd, ln1_gain=vectors[l, 0], ln2_gain=vectors[l, 3]))
+        entering = leaving
+    return [made[13 * l + 12] for l in range(layers)], saved, weights
+
+
 def swapped(value):
     count = lax.axis_size("section")
     return lax.ppermute(value, "section", [(i, (i + 1) % count) for i in range(count)])
+
+
+def near_shards(depth, block):
+    return depth % 256 == 0 and block % 256 == 0
+
+
+def gathered_layers(section, layer_count, w_qkv, w_out, w_up, w_down, small_ones):
+    def both(value):
+        other = swapped(value)
+        return [jnp.where(section == l, value, other) for l in range(layer_count)]
+
+    def over_dp(value, axis):
+        return both(lax.all_gather(value, "dp", axis=axis, tiled=True))
+
+    qkv_all, up_all = over_dp(jnp.transpose(w_qkv[0], (1, 0, 2)), 1), over_dp(w_up[0], 0)
+    out_all, down_all = over_dp(w_out[0], 1), over_dp(w_down[0], 1)
+    vectors = [
+        both(item[0]) for item in small_ones
+    ]
+    layers = []
+    for l in range(layer_count):
+        gain1, bias1, qv, bout, gain2, bias2, bup, bdown = [item[l] for item in vectors]
+        layers.append(
+            dict(
+                ln1_gain=gain1,
+                ln1_bias=bias1,
+                ln2_gain=gain2,
+                ln2_bias=bias2,
+                qkv=qkv_all[l],
+                out=out_all[l],
+                up=up_all[l],
+                down=down_all[l],
+                b_qkv=jnp.stack([qv[0], jnp.zeros_like(qv[0]), qv[1]])[:, None, :],
+                b_out=bout,
+                b_up=bup,
+                b_down=bdown,
+            )
+        )
+    return layers
 
 
 def per_device(
@@ -560,48 +985,29 @@
     slopes = jnp.exp2(-8.0 * (head_ids.astype(jnp.float32) + 1.0) / HEADS)
     slopes = jnp.broadcast_to(slopes[:, None], (local_heads, inputs.shape[1]))
 
-    def both(value):
-        other = swapped(value)
-        return [jnp.where(section == l, value, other) for l in range(layer_count)]
-
-    def over_dp(value, axis):
-        return both(lax.all_gather(value, "dp", axis=axis, tiled=True))
-
-    qkv_all, up_all = over_dp(jnp.transpose(w_qkv[0], (1, 0, 2)), 1), over_dp(w_up[0], 0)
-    out_all, down_all = over_dp(w_out[0], 1), over_dp(w_down[0], 1)
-    vectors = [
-        both(item[0]) for item in (ln1_gain, ln1_bias, b_qv, b_out, ln2_gain, ln2_bias, b_up, b_down)
-    ]
-    layers = []
-    for l in range(layer_count):
-        gain1, bias1, qv, bout, gain2, bias2, bup, bdown = [item[l] for item in vectors]
-        layers.append(
-            dict(
-                ln1_gain=gain1,
-                ln1_bias=bias1,
-                ln2_gain=gain2,
-                ln2_bias=bias2,
-                qkv=qkv_all[l],
-                out=out_all[l],
-                up=up_all[l],
-                down=down_all[l],
-                b_qkv=jnp.stack([qv[0], jnp.zeros_like(qv[0]), qv[1]])[:, None, :],
-                b_out=bout,
-                b_up=bup,
-                b_down=bdown,
-            )
-        )
     row = lax.dynamic_index_in_dim(inputs, section, 0, keepdims=False)
     target = lax.dynamic_index_in_dim(out_grad, section, 0, keepdims=False)
     lang = lax.dynamic_index_in_dim(lang_ids, section, 0, keepdims=False)
     matches = lang == jnp.arange(lang_weights.shape[0], dtype=jnp.int32)
     scale = jnp.sum(jnp.where(matches, lang_weights, 0)).astype(jnp.float32) / 64.0
 
-    acts, saved = [], []
-    for l in range(layer_count):
-        row, kept = layer_forward(row, layers[l], slopes)
-        acts.append(row)
-        saved.append(kept)
+    if near_shards(w_qkv[0].shape[0], inputs.shape[1]):
+        vector = jnp.stack(
+            [item[0] for item in (ln1_gain, ln1_bias, b_out, ln2_gain, ln2_bias)]
+            + [b_up[0], b_down[0], jnp.pad(b_qv[0].reshape(-1), (0, b_out.shape[1] - 2 * b_qv.shape[2]))]
+        )
+        shards = (jnp.transpose(w_qkv[0], (1, 0, 2)), w_out[0], w_up[0], w_down[0])
+        acts, saved, layers = forward_call(row, vector, shards, slopes)
+    else:
+        layers = gathered_layers(
+            section, layer_count, w_qkv, w_out, w_up, w_down,
+            (ln1_gain, ln1_bias, b_qv, b_out, ln2_gain, ln2_bias, b_up, b_down),
+        )
+        acts, saved = [], []
+        for l in range(layer_count):
+            row, kept = layer_forward(row, layers[l], slopes)
+            acts.append(row)
+            saved.append(kept)
     grads, small, large = [None] * layer_count, [None] * layer_count, [None] * layer_count
     incoming = target.astype(jnp.float32) * scale
     for l in reversed(range(layer_count)):

time: 836 us -> 713 us (0.85)
  waiting for transfers between devices: 351 us -> 193 us
  Pallas kernels: 310 us -> 393 us
  blocking collectives: 35.5 us -> 11.3 us
  other arithmetic: 46.2 us -> 30.6 us
  starting transfers between devices: 27.9 us -> 16.3 us
    pallas_call x0 -> x1, Pallas kernels: none -> 233 us  [forward_call(): pl.pallas_call(functools.partial(forward_kernel, layers), out_shape=[jax....]
    pallas_call x8 -> x4, Pallas kernels: 310 us -> 160 us  [call(): pl.pallas_call(kernel, out_shape=[jax.ShapeDtypeStruct(shape, dtype) for...]
    all_gather x3 -> x0, waiting for transfers between devices: 102 us -> none  [over_dp(): return both(lax.all_gather(value, 'dp', axis=axis, tiled=True))]
    ppermute x21 -> x9, waiting for transfers between devices: 177 us -> 122 us  [swapped(): lax.ppermute(value, 'section', [(i, (i + 1) % count) for i in range(count)])]
    all_gather x1 -> x0, blocking collectives: 25.1 us -> none  [over_dp(): return both(lax.all_gather(value, 'dp', axis=axis, tiled=True))]
    select_n x9 -> x0, other arithmetic: 14.9 us -> none  [both(): return [jnp.where(section == l, value, other) for l in range(layer_count)]]
    ppermute x21 -> x9, starting transfers between devices: 27.3 us -> 15.9 us  [swapped(): lax.ppermute(value, 'section', [(i, (i + 1) % count) for i in range(count)])]
  transfers between devices with their start and end apart: 30 -> 15, of which waited for: 12 -> 5; matrix products, arithmetic and copies ran while one was open for 9% -> 8% of each run, Pallas kernels for 5% -> 0%
where the time goes in v3:
time: 713 us; the launch traced here: 705 us
  Pallas kernels  393 us (55%)
  waiting for transfers between devices  193 us (27%)
  other arithmetic  30.6 us (4%)
  matrix products  25.2 us (4%)
  local copies, waits for them, and re-layouts  19.1 us (3%)
  starting transfers between devices  16.3 us (2%)
  between operations  16 us (2%)
  blocking collectives  11.3 us (2%)
    pallas_call x1, Pallas kernels, forward_call(): pl.pallas_call(functools.partial(forward_kernel, layers), out_shape=[jax....  233 us
    pallas_call x4, Pallas kernels, call(): pl.pallas_call(kernel, out_shape=[jax.ShapeDtypeStruct(shape, dtype) for...  160 us
    ppermute x9, waiting for transfers between devices, swapped(): lax.ppermute(value, 'section', [(i, (i + 1) % count) for i in range(count)])  122 us
    reduce_scatter x4, waiting for transfers between devices, reduced(): lax.psum_scatter(total, 'dp', scatter_dimension=axis, tiled=True)  71.2 us
    ppermute x9, starting transfers between devices, swapped(): lax.ppermute(value, 'section', [(i, (i + 1) % count) for i in range(count)])  15.9 us
  transfers between devices with their start and end apart: 15, of which 5 were waited for; matrix products, arithmetic and copies ran while one was open for 8% of the time, Pallas kernels for 0%

profile of v3, /device:TPU:0, one launch (start us, length us, event | category | flops | bytes accessed | tf_op | source)
XLA Modules:
  0.0 705.3 jit_solution(4903099850388634788)
XLA Ops:
  9.3 1.4 stack.33.refs_1_
  11.4 233.4 %forward.1 = (bf16[1024,1024]{1,0:T(8,128)(2,1)}, bf16[3,1024,256]{2,1,0:T(8,128)(2,1)}, bf16[1024,256]{1,0:T(8,128)(2,1)}, bf16[1024,1024]{1,0:T(8,128)(2,1)}, ...) custom-call(bf16[256,1024]{1,0:T(8,128)(2,1)} %dynamic-slice_bitcast, ...), custom_call_target="tpu_custom_call" | custom-call | tf_op jit(solution)/shard_map/forward/pallas_call | solution.py:885
  244.8 1.5 slice_bitcast_fusion
  246.9 1.3 fusion.14
  248.8 1.1 multiply_bitcast_fusion.incoming
  249.9 33.2 %mlp_backward.2 = (bf16[1024,1024]{1,0:T(8,128)(2,1)}, bf16[1024,1024]{1,0:T(8,128)(2,1)}, f32[256,1024]{1,0:T(8,128)}, f32[8,1024]{1,0:T(8,128)}, f32[1,1024]{1,0:T(1,128)}) custom-call(f32[256,1024]{1,0:T(8,128)} %multiply_bitcast_fusion.incoming, f32[256,1024]{1,0:T(8,128)} %get-tuple-element.63.middle, f32[1,1024]{1,0:T(1,128)} %get-tuple-element.145.gain, ...), custom_call_target="tpu_custom_call" | custom-call | tf_op jit(solution)/shard_map/mlp_backward/pallas_call | solution.py:478
  283.1 46.4 %attention_backward.2 = (bf16[1024,1024]{1,0:T(8,128)(2,1)}, bf16[3,1024,256]{2,1,0:T(8,128)(2,1)}, f32[256,1024]{1,0:T(8,128)}, f32[8,1024]{1,0:T(8,128)}, f32[8,256]{1,0:T(8,128)}) custom-call(f32[256,1024]{1,0:T(8,128)} %get-tuple-element.68.grad_middle, bf16[256,1024]{1,0:T(8,128)(2,1)} %get-tuple-element.61.x, f32[1,1024]{1,0:T(1,128)} %get-tuple-element.144.gain, ...), custom_call_target="tpu_custom_call" | custom-call | tf_op jit(solution)/shard_map/attention_backward/pallas_call | solution.py:478
  329.5 2.3 convert_convert_fusion.incoming
  331.8 34.0 %mlp_backward.3 = (bf16[1024,1024]{1,0:T(8,128)(2,1)}, bf16[1024,1024]{1,0:T(8,128)(2,1)}, f32[256,1024]{1,0:T(8,128)}, f32[8,1024]{1,0:T(8,128)}, f32[1,1024]{1,0:T(1,128)}) custom-call(f32[256,1024]{1,0:T(8,128)} %convert_convert_fusion.incoming, f32[256,1024]{1,0:T(8,128)} %get-tuple-element.74.middle, f32[1,1024]{1,0:T(1,128)} %get-tuple-element.143.gain, ...), custom_call_target="tpu_custom_call" | custom-call | tf_op jit(solution)/shard_map/mlp_backward/pallas_call | solution.py:478
  365.9 46.3 %attention_backward.3 = (bf16[1024,1024]{1,0:T(8,128)(2,1)}, bf16[3,1024,256]{2,1,0:T(8,128)(2,1)}, f32[256,1024]{1,0:T(8,128)}, f32[8,1024]{1,0:T(8,128)}, f32[8,256]{1,0:T(8,128)}) custom-call(f32[256,1024]{1,0:T(8,128)} %get-tuple-element.78.grad_middle, bf16[256,1024]{1,0:T(8,128)(2,1)} %dynamic-slice_bitcast_fusion.refs_0_.x, ...), custom_call_target="tpu_custom_call" | custom-call | tf_op jit(solution)/shard_map/attention_backward/pallas_call | solution.py:478
  412.2 2.5 convolution_convert_fusion.5
  414.7 1.7 broadcast_select_fusion.2
  416.4 5.1 collective-permute-start.5
  421.6 1.8 fusion.4
  423.6 1.8 fusion.7
  425.5 1.3 select_bitcast_fusion
  428.4 1.2 collective-permute-start.4
  432.0 35.2 %collective-permute-done.4 = bf16[2,256]{1,0:T(2,128)(2,1)S(1)} collective-permute-done((bf16[2,256]{1,0:T(2,128)(2,1)S(1)}, bf16[2,256]{1,0:T(2,128)(2,1)S(1)}, u32[]{:S(2)}, u32[]{:S(2)}) %collective-permute-start.4) | collective-permute-done | bytes 1056 | tf_op jit(solution)/shard_map/ppermute | solution.py:921
  468.9 1.0 copy.38
  470.0 2.1 select_add_fusion.2
  472.1 5.9 convolution_convert_fusion.1
  478.0 2.8 bitcast_add_fusion
  481.1 4.8 broadcast_select_fusion
  485.9 2.4 collective-permute-start.8
  488.3 43.8 %collective-permute-done.8 = bf16[1024,1024]{1,0:T(8,128)(2,1)S(1)} collective-permute-done((bf16[1024,1024]{1,0:T(8,128)(2,1)S(1)}, bf16[1024,1024]{1,0:T(8,128)(2,1)S(1)}, u32[]{:S(2)}, u32[]{:S(2)}) %collective-permute-start.8) | collective-permute-done | bytes 2097184 | tf_op jit(solution)/shard_map/ppermute | solution.py:921
  532.1 1.6 select_add_fusion
  533.8 1.5 copy-done.17
  535.3 4.1 convolution_convert_fusion.3
  539.5 2.5 broadcast_select_fusion.1
  542.0 1.8 collective-permute-start.6
  543.8 43.2 %collective-permute-done.6 = bf16[1024,1024]{1,0:T(8,128)(2,1)S(1)} collective-permute-done((bf16[1024,1024]{1,0:T(8,128)(2,1)S(1)}, bf16[1024,1024]{1,0:T(8,128)(2,1)S(1)}, u32[]{:S(2)}, u32[]{:S(2)}) %collective-permute-start.6) | collective-permute-done | bytes 2097184 | tf_op jit(solution)/shard_map/ppermute | solution.py:921
  587.0 1.7 select_add_fusion.1
  589.4 1.5 collective-permute-start.7
  590.9 0.9 broadcast_select_fusion.3
  593.5 1.3 collective-permute-start
  596.0 11.3 %all-reduce.1 = bf16[1024]{0:T(1024)(128)(2,1)S(1)} all-reduce(bf16[1024]{0:T(1024)(128)(2,1)S(1)} %add.70), channel_id=7, replica_groups=mesh['section'=2,'tensor'=4,'dp'=4] {'dp'}, use_global_device_ids=true, to_apply=%region_6.7.clone | all-reduce | flops 1024 | bytes 4096
  609.3 1.2 fusion.15
  614.0 1.1 select_bitcast_fusion.4
  615.2 1.1 maximum_bitcast_fusion
  616.4 1.1 select_bitcast_fusion.1
  617.5 1.5 maximum_convert_fusion
  618.9 1.6 bitcast_convert_fusion.2
  620.6 1.1 convert_bitcast_fusion
  621.7 1.1 copy.35
  622.9 27.8 %reduce-scatter.17.cloned.1.call-done = bf16[1024,256]{1,0:T(8,128)(2,1)} async-done(((bf16[1024,1024]{1,0:T(8,128)(2,1)}), bf16[1024,256]{1,0:T(8,128)(2,1)}) %reduce-scatter.17.cloned.1.call-update) | async-done | bytes 524304 | tf_op jit(solution)/shard_map/reduce_scatter | solution.py:1032
  650.6 2.1 bitcast_convert_fusion
  652.7 43.4 %reduce-scatter.15.cloned.1.call-done = bf16[256,1024]{1,0:T(8,128)(2,1)} async-done(((bf16[1024,1024]{1,0:T(8,128)(2,1)}), bf16[256,1024]{1,0:T(8,128)(2,1)}) %reduce-scatter.15.cloned.1.call-update) | async-done | bytes 524304 | tf_op jit(solution)/shard_map/reduce_scatter | solution.py:1032
  696.1 2.1 bitcast_convert_fusion.1
  (105 shorter events, 18.1 us)
Async XLA Ops:
  7.2 1.2 copy-start
  7.2 239.1 %copy-start.23 = (s32[2]{0:T(128)S(1)}, s32[2]{0:T(128)}, u32[]{:S(2)}) copy-start(s32[2]{0:T(128)} %param.18) | copy-start | bytes 28
  7.2 239.7 %copy-start.24 = (s32[46]{0:T(128)S(1)}, s32[46]{0:T(128)}, u32[]{:S(2)}) copy-start(s32[46]{0:T(128)} %param.19) | copy-start | bytes 556
  7.2 241.6 %copy-start.11 = (bf16[2,256,1024]{2,1,0:T(8,128)(2,1)S(1)}, bf16[2,256,1024]{2,1,0:T(8,128)(2,1)}, u32[]{:S(2)}) copy-start(bf16[2,256,1024]{2,1,0:T(8,128)(2,1)} %param.17) | copy-start | bytes 3145732
  7.2 600.7 %reduce-scatter.21.cloned.1.call-start = ((), (), s32[]{:S(2)}) async-start(), calls=%async_computation.11 | async-start | bytes 81920
  365.9 46.3 %copy-start.10 = (bf16[1024,256]{1,0:T(8,128)(2,1)S(1)}, bf16[1024,256]{1,0:T(8,128)(2,1)}, u32[]{:S(2)}) copy-start(bf16[1024,256]{1,0:T(8,128)(2,1)} %get-tuple-element.94) | copy-start | bytes 1572868
  412.2 2.5 copy-start.7
  412.2 2.5 copy-start.9
  414.7 6.9 copy-start.4
  414.7 6.9 copy-start.20
  414.7 6.8 copy-start.22
  416.4 53.5 %collective-permute-start.5 = (bf16[256,1024]{1,0:T(8,128)(2,1)}, bf16[256,1024]{1,0:T(8,128)(2,1)}, u32[]{:S(2)}, u32[]{:S(2)}) collective-permute-start(bf16[256,1024]{1,0:T(8,128)(2,1)} %get-tuple-element.152), channel_id=1, source_target_pairs={{0,16},{16,0},{1,17},{17,1},{2,18},{18,2},{3,19},{19,3},{4,20},{20... | collective-permute-start | bytes 1572872 | tf_op jit(solution)/shard_map/ppermute | solution.py:921
  421.6 1.9 copy-start.19
  421.6 2.0 copy-start.21
  425.4 4.9 copy-start.13
  425.5 5.6 copy-start.12
  426.8 51.2 %collective-permute-start.3 = (bf16[3,1024,256]{1,2,0:T(8,128)(2,1)}, bf16[3,1024,256]{1,2,0:T(8,128)(2,1)}, u32[]{:S(2)}, u32[]{:S(2)}) collective-permute-start(bf16[3,1024,256]{1,2,0:T(8,128)(2,1)} %select_bitcast_fusion), channel_id=1, source_target_pairs={{0,16},{16,0},{1,17},{17,1},{2,18},{18,2},{3,19},{19,3},{4,20},{20... | collective-permute-start | bytes 4718600 | tf_op jit(solution)/shard_map/ppermute | solution.py:921
  428.4 38.9 %collective-permute-start.4 = (bf16[2,256]{1,0:T(2,128)(2,1)S(1)}, bf16[2,256]{1,0:T(2,128)(2,1)S(1)}, u32[]{:S(2)}, u32[]{:S(2)}) collective-permute-start(bf16[2,256]{1,0:T(2,128)(2,1)S(1)} %broadcast_select_fusion.9), channel_id=1, source_target_pairs={{0,16},{16,0},{1,17},{17,1},{2,18},{18,2},{3,19},{19,3},{4,20},{20... | collective-permute-start | bytes 3080 | tf_op jit(solution)/shard_map/ppermute | solution.py:921
  431.1 37.7 %collective-permute-start.2 = (f32[6,1024]{1,0:T(8,128)S(1)}, f32[6,1024]{1,0:T(8,128)S(1)}, u32[]{:S(2)}, u32[]{:S(2)}) collective-permute-start(f32[6,1024]{1,0:T(8,128)S(1)} %fusion.10), channel_id=1, source_target_pairs={{0,16},{16,0},{1,17},{17,1},{2,18},{18,2},{3,19},{19,3},{4,20},{20... | collective-permute-start | bytes 73736 | tf_op jit(solution)/shard_map/ppermute | solution.py:921
  468.8 140.6 %reduce-scatter.19.cloned.1.call-start = ((), (), s32[]{:S(2)}) async-start(), calls=%async_computation.10 | async-start | bytes 557056
  469.9 149.0 %reduce-scatter.13.cloned.1.call-start = ((), (), s32[]{:S(2)}) async-start(), calls=%async_computation.7 | async-start | bytes 655360 | tf_op jit(solution)/shard_map/reduce_scatter | solution.py:1032
  472.1 148.5 %reduce-scatter.11.cloned.1.call-start = ((), (), s32[]{:S(2)}) async-start(), calls=%async_computation.6 | async-start | bytes 1966080 | tf_op jit(solution)/shard_map/reduce_scatter | solution.py:1032
  480.8 169.8 %reduce-scatter.17.cloned.1.call-start = ((), (), s32[]{:S(2)}) async-start(), calls=%async_computation.9 | async-start | bytes 2621440 | tf_op jit(solution)/shard_map/reduce_scatter | solution.py:1032
  481.1 51.0 %copy-start.8 = (bf16[1024,1024]{1,0:T(8,128)(2,1)S(1)}, bf16[1024,1024]{1,0:T(8,128)(2,1)}, u32[]{:S(2)}) copy-start(bf16[1024,1024]{1,0:T(8,128)(2,1)} %convolution_convert_fusion.1) | copy-start | bytes 6291460
  485.9 46.2 %collective-permute-start.8 = (bf16[1024,1024]{1,0:T(8,128)(2,1)S(1)}, bf16[1024,1024]{1,0:T(8,128)(2,1)S(1)}, u32[]{:S(2)}, u32[]{:S(2)}) collective-permute-start(bf16[1024,1024]{1,0:T(8,128)(2,1)S(1)} %get-tuple-element.156), channel_id=1, source_target_pairs={{0,16},{16,0},{1,17},{17,1},{2,18},{18,2},{3,19},{19,3},{4,20},{20... | collective-permute-start | bytes 6291464 | tf_op jit(solution)/shard_map/ppermute | solution.py:921
  533.7 1.6 copy-start.17
  533.7 162.4 %reduce-scatter.15.cloned.1.call-start = ((), (), s32[]{:S(2)}) async-start(), calls=%async_computation.8 | async-start | bytes 2621440 | tf_op jit(solution)/shard_map/reduce_scatter | solution.py:1032
  535.3 4.1 copy-start.16
  535.3 4.1 copy-start.18
  542.0 45.0 %collective-permute-start.6 = (bf16[1024,1024]{1,0:T(8,128)(2,1)S(1)}, bf16[1024,1024]{1,0:T(8,128)(2,1)S(1)}, u32[]{:S(2)}, u32[]{:S(2)}) collective-permute-start(bf16[1024,1024]{1,0:T(8,128)(2,1)S(1)} %get-tuple-element.154), channel_id=1, source_target_pairs={{0,16},{16,0},{1,17},{17,1},{2,18},{18,2},{3,19},{19,3},{4,20},{20... | collective-permute-start | bytes 6291464 | tf_op jit(solution)/shard_map/ppermute | solution.py:921
  587.0 1.8 copy-start.15
  588.7 0.7 copy-start.14
  588.7 2.2 copy-start.2
  588.7 2.2 copy-start.5
  588.7 3.9 copy-start.3
  588.7 3.9 copy-start.6
  589.4 6.6 collective-permute-start.7
  590.9 3.8 copy-start.25
  591.9 24.4 %collective-permute-start.1 = (bf16[256,1024]{1,0:T(8,128)(2,1)}, bf16[256,1024]{1,0:T(8,128)(2,1)}, u32[]{:S(2)}, u32[]{:S(2)}) collective-permute-start(bf16[256,1024]{1,0:T(8,128)(2,1)} %broadcast_select_fusion.3), channel_id=1, source_target_pairs={{0,16},{16,0},{1,17},{17,1},{2,18},{18,2},{3,19},{19,3},{4,20},{20... | collective-permute-start | bytes 1572872 | tf_op jit(solution)/shard_map/ppermute | solution.py:921
  593.5 20.5 %collective-permute-start = (bf16[256,1024]{1,0:T(8,128)(2,1)}, bf16[256,1024]{1,0:T(8,128)(2,1)}, u32[]{:S(2)}, u32[]{:S(2)}) collective-permute-start(bf16[256,1024]{1,0:T(8,128)(2,1)} %broadcast_select_fusion.5), channel_id=1, source_target_pairs={{0,16},{16,0},{1,17},{17,1},{2,18},{18,2},{3,19},{19,3},{4,20},{20... | collective-permute-start | bytes 1572872 | tf_op jit(solution)/shard_map/ppermute | solution.py:921
  620.6 77.7 %copy-start.1 = (bf16[2,256,1024]{2,1,0:T(8,128)(2,1)S(1)}, bf16[2,256,1024]{2,1,0:T(8,128)(2,1)}, u32[]{:S(2)}) copy-start(bf16[2,256,1024]{2,1,0:T(8,128)(2,1)} %param.16) | copy-start | bytes 3145732
Sparse Core Ops, SparseCore 0:
  468.9 19.2 reduce-scatter.20
  492.7 53.8 reduce-scatter.18
  548.9 20.6 reduce-scatter.12
  571.8 33.8 reduce-scatter.10
  607.8 42.8 reduce-scatter.16
  652.9 43.1 reduce-scatter.14

commit v4 on v3

--- a/solution.py
+++ b/solution.py
@@ -14,11 +14,13 @@
 EPSILON = 1e-05
 GELU_SCALE = 0.7978845608028654
 
+SECTION, TENSOR, DP = "section", "tensor", "dp"
 MESH = pl.DeviceIdType.MESH
 F32 = jnp.float32
 BF16 = jnp.bfloat16
 CHUNKS = 2
-VMEM_LIMIT = 60 * 1024 * 1024
+LANES = 128
+VMEM_LIMIT = 61 * 1024 * 1024
 
 
 def rows_at(start, size):
@@ -37,7 +39,7 @@
     def __init__(self, block):
         self.block = block
         self.chunk = block // CHUNKS
-        self.me = lax.axis_index("tensor")
+        self.me = lax.axis_index(TENSOR)
         core, chip = lax.rem(self.me, 2), self.me // 2
         self.mate = self.me + 1 - 2 * core
         self.peer = self.me + 2 - 4 * chip
@@ -46,7 +48,7 @@
     def greet(self):
         barrier = pltpu.get_barrier_semaphore()
         for other in (self.mate, self.peer):
-            pl.semaphore_signal(barrier, inc=1, device_id={"tensor": other}, device_id_type=MESH)
+            pl.semaphore_signal(barrier, inc=1, device_id={TENSOR: other}, device_id_type=MESH)
         pl.semaphore_wait(barrier, 2)
 
     def rows(self, owner, c):
@@ -58,7 +60,7 @@
             dst_ref=dst,
             send_sem=sems.at[0, kind, c],
             recv_sem=sems.at[1, kind, c],
-            device_id={"tensor": other},
+            device_id={TENSOR: other},
             device_id_type=MESH,
         )
 
@@ -145,7 +147,7 @@
 
 def scores_of(keys, queries, slope, penalty_ref, start):
     stop, count = keys.shape[0], queries.shape[0]
-    scores = mm_t(keys, queries) + slope * penalty_ref[:stop]
+    scores = mm_t(keys, queries) + slope * jnp.concatenate([penalty_ref[:stop]] * (count // LANES), axis=1)
     last = scores[start:]
     allowed = lax.broadcasted_iota(jnp.int32, (count, count), 0) <= lax.broadcasted_iota(
         jnp.int32, (count, count), 1
@@ -164,7 +166,7 @@
     penalty_ref[...] = lax.broadcasted_iota(jnp.int32, penalty_ref.shape, 0).astype(F32)
 
 
-def nothing():
+def nothing(point=0):
     pass
 
 
@@ -173,7 +175,7 @@
     for pair in range(width // PAIR):
         lanes = pl.ds(pair * PAIR, PAIR)
         for start in range(0, length, block):
-            tick()
+            tick(pair * 4 + start // block)
             stop = start + block
             queries = proj[0, start:stop, lanes] * jnp.asarray(0.125, BF16)
             keys = proj[1, :stop, lanes]
@@ -192,12 +194,12 @@
             context[start:stop, lanes] = jnp.concatenate(outs, axis=0).T.astype(BF16)
 
 
-def attend_backward(proj, grad_context, totals, slopes, penalty, grad_proj, sums, block):
+def attend_backward(proj, grad_context, totals, slopes, penalty, grad_proj, sums, block, tick=nothing):
     length, width = grad_context.shape
-
-    def pair_step(pair, carry):
-        lanes = pl.ds(pl.multiple_of(pair * PAIR, PAIR), PAIR)
+    for pair in range(width // PAIR):
+        lanes = pl.ds(pair * PAIR, PAIR)
         for start in range(0, length, block):
+            tick()
             stop = start + block
             queries = proj[0, start:stop, lanes] * jnp.asarray(0.125, BF16)
             keys = proj[1, :stop, lanes]
@@ -230,9 +232,6 @@
             sums[1, start:stop] = grad_values[start:]
         grad_proj[1, :, lanes] = sums[0].astype(BF16)
         grad_proj[2, :, lanes] = sums[1].astype(BF16)
-        return carry
-
-    lax.fori_loop(0, width // PAIR, pair_step, 0)
 
 
 def attention_forward_body(
@@ -273,8 +272,10 @@
     for c in range(CHUNKS):
         scatter.put(0, c, part_of(ring.far, c))
         scatter.put(1, c, part_of(ring.peer, c) + scatter.take(0, c))
+        tick(8 + c)
     for c in range(CHUNKS):
         scatter.put(2, c, part_of(ring.mate, c))
+    tick(10)
     for c in range(CHUNKS):
         at = pl.ds(c * chunk, chunk)
         total = part_of(ring.me, c) + scatter.take(2, c) + scatter.take(1, c)
@@ -306,22 +307,23 @@
         slope_of[at] = slope.astype(BF16)
         return mm(value, w_down[...])
 
+    tick(11)
     ready()
     own[...] = expand(rows_at(ring.me * block, block))
-    tick()
+    tick(12)
     for c in range(CHUNKS):
         gather.arrived_mate(c)
     part = expand(rows_at(ring.mate * block, block))
     for c in range(CHUNKS):
         scatter.put(2, c, part[c * chunk : (c + 1) * chunk])
-    tick()
+    tick(13)
     for c in range(CHUNKS):
         gather.arrived_peer(c)
         peer_part = expand(ring.rows(ring.peer, c))
         gather.arrived_far(c)
         scatter.put(0, c, expand(ring.rows(ring.far, c)))
         scatter.put(1, c, peer_part + scatter.take(0, c))
-        tick()
+        tick(14 + c)
     for c in range(CHUNKS):
         at = pl.ds(c * chunk, chunk)
         total = own[at] + scatter.take(2, c) + scatter.take(1, c)
@@ -365,72 +367,62 @@
     scatter.finish()
 
 
-def mlp_backward_kernel(
-    incoming, middle, gain, w_up, w_down, slope_of,
-    down_rows, grad_up, grad_middle, small, up_sum,
-    own, stage, land, gather_sems, scatter_sems,
+def mlp_backward_body(
+    ring, gather, scatter, incoming, middle, gain, w_up, w_down, slope_of,
+    down_rows, grad_up, grad_middle, small, up_sum, own,
+    ready=nothing, made=nothing, tick=nothing,
 ):
-    block = middle.shape[0]
-    ring = Ring(block)
-    ring.greet()
-    gather = Gather(ring, down_rows, gather_sems)
-    scatter = Scatter(ring, stage, land, scatter_sems)
-    chunk = ring.chunk
+    block, chunk = ring.block, ring.chunk
     for c in range(CHUNKS):
         down_rows[ring.rows(ring.me, c)] = incoming[pl.ds(c * chunk, chunk)].astype(BF16)
         gather.start(c)
-    up_sum[...] = jnp.zeros_like(up_sum)
+    ready()
 
     def pull(at):
         grad = mm_t(down_rows[at], w_down[...]) * slope_of[at].astype(F32)
         grad = grad.astype(BF16)
         grad_up[at] = grad
-        up_sum[...] += jnp.sum(grad.astype(F32), axis=0, keepdims=True)
+        up_sum(jnp.sum(grad.astype(F32), axis=0, keepdims=True))
         return mm_t(grad, w_up[...])
 
     own[...] = pull(rows_at(ring.me * block, block))
+    tick()
     for c in range(CHUNKS):
         gather.arrived_mate(c)
     part = pull(rows_at(ring.mate * block, block))
     for c in range(CHUNKS):
         scatter.put(2, c, part[c * chunk : (c + 1) * chunk])
+    tick()
     for c in range(CHUNKS):
         gather.arrived_peer(c)
         peer_part = pull(ring.rows(ring.peer, c))
         gather.arrived_far(c)
         scatter.put(0, c, pull(ring.rows(ring.far, c)))
         scatter.put(1, c, peer_part + scatter.take(0, c))
-    small[...] = jnp.zeros_like(small)
+    made()
     for c in range(CHUNKS):
         at = pl.ds(c * chunk, chunk)
         total = own[at] + scatter.take(2, c) + scatter.take(1, c)
-        pulled, grad_gain, grad_shift = norm_pull(middle[at], gain[...], total)
-        before = incoming[at]
+        pulled, grad_gain, grad_shift = norm_pull(middle[at], gain(), total)
+        before = incoming[at].astype(F32)
         after = before + pulled
         grad_middle[at] = after
-        small[0:1] += jnp.sum(after, axis=0, keepdims=True)
-        small[1:2] += grad_gain
-        small[2:3] += grad_shift
-        small[3:4] += jnp.sum(before, axis=0, keepdims=True)
-    gather.finish()
-    scatter.finish()
-
-
-def attention_backward_kernel(
-    grad_middle, x, gain, w_qkv, w_out, slopes, proj, totals,
-    attn_rows, grad_proj, grad_hidden, small, qv_sum,
-    grad_context, sums, penalty, stage, land, gather_sems, scatter_sems,
+        small(2, jnp.sum(after, axis=0, keepdims=True))
+        small(3, grad_gain)
+        small(4, grad_shift)
+        small(5, jnp.sum(before, axis=0, keepdims=True))
+
+
+def attention_backward_body(
+    ring, gather, scatter, grad_middle, x, gain, w_qkv, w_out, slopes, proj, totals,
+    attn_rows, grad_proj, grad_hidden, small, grad_context, sums, penalty,
+    out_ready=nothing, ready=nothing, gathered=nothing, made=nothing, tick=nothing,
 ):
-    block = x.shape[0]
-    ring = Ring(block)
-    ring.greet()
-    gather = Gather(ring, attn_rows, gather_sems)
-    scatter = Scatter(ring, stage, land, scatter_sems)
-    chunk = ring.chunk
+    block, chunk = ring.block, ring.chunk
     for c in range(CHUNKS):
         attn_rows[ring.rows(ring.me, c)] = grad_middle[pl.ds(c * chunk, chunk)].astype(BF16)
         gather.start(c)
-    fill_penalty(penalty)
+    out_ready()
 
     def pull(at):
         grad_context[at] = mm_t(attn_rows[at], w_out[...]).astype(BF16)
@@ -439,15 +431,16 @@
     for c in range(CHUNKS):
         gather.arrived_mate(c)
     pull(rows_at(ring.mate * block, block))
+    tick()
     for c in range(CHUNKS):
         gather.arrived_peer(c)
         pull(ring.rows(ring.peer, c))
         gather.arrived_far(c)
         pull(ring.rows(ring.far, c))
-    attend_backward(proj, grad_context, totals, slopes, penalty, grad_proj, sums, block)
-    qv_sum[...] = jnp.zeros_like(qv_sum)
-    qv_sum[0:1] = jnp.sum(grad_proj[0].astype(F32), axis=0, keepdims=True)
-    qv_sum[1:2] = jnp.sum(grad_proj[2].astype(F32), axis=0, keepdims=True)
+        tick()
+    gathered()
+    ready()
+    attend_backward(proj, grad_context, totals, slopes, penalty, grad_proj, sums, block, tick)
 
     def part_of(owner, c):
         at = ring.rows(owner, c)
@@ -461,14 +454,64 @@
         scatter.put(1, c, part_of(ring.peer, c) + scatter.take(0, c))
     for c in range(CHUNKS):
         scatter.put(2, c, part_of(ring.mate, c))
-    small[...] = jnp.zeros_like(small)
+    made()
     for c in range(CHUNKS):
         at = pl.ds(c * chunk, chunk)
         total = part_of(ring.me, c) + scatter.take(2, c) + scatter.take(1, c)
-        pulled, grad_gain, grad_shift = norm_pull(x[at].astype(F32), gain[...], total)
+        pulled, grad_gain, grad_shift = norm_pull(x[at].astype(F32), gain(), total)
         grad_hidden[at] = grad_middle[at] + pulled
-        small[0:1] += grad_gain
-        small[1:2] += grad_shift
+        small(0, grad_gain)
+        small(1, grad_shift)
+
+
+def mlp_backward_kernel(
+    incoming, middle, gain, w_up, w_down, slope_of,
+    down_rows, grad_up, grad_middle, small, up_sum,
+    own, stage, land, gather_sems, scatter_sems,
+):
+    ring = Ring(middle.shape[0])
+    ring.greet()
+    gather = Gather(ring, down_rows, gather_sems)
+    scatter = Scatter(ring, stage, land, scatter_sems)
+    small[...] = jnp.zeros_like(small)
+    up_sum[...] = jnp.zeros_like(up_sum)
+
+    def add_small(i, value):
+        small[pl.ds(i, 1)] += value
+
+    def add_up(value):
+        up_sum[...] += value
+
+    mlp_backward_body(
+        ring, gather, scatter, incoming, middle, lambda: gain[...], w_up, w_down, slope_of,
+        down_rows, grad_up, grad_middle, add_small, add_up, own,
+    )
+    gather.finish()
+    scatter.finish()
+
+
+def attention_backward_kernel(
+    grad_middle, x, gain, w_qkv, w_out, slopes, proj, totals,
+    attn_rows, grad_proj, grad_hidden, small, qv_sum,
+    grad_context, sums, penalty, stage, land, gather_sems, scatter_sems,
+):
+    ring = Ring(x.shape[0])
+    ring.greet()
+    gather = Gather(ring, attn_rows, gather_sems)
+    scatter = Scatter(ring, stage, land, scatter_sems)
+    fill_penalty(penalty)
+    small[...] = jnp.zeros_like(small)
+
+    def add_small(i, value):
+        small[pl.ds(i, 1)] += value
+
+    attention_backward_body(
+        ring, gather, scatter, grad_middle, x, lambda: gain[...], w_qkv, w_out, slopes, proj,
+        totals, attn_rows, grad_proj, grad_hidden, add_small, grad_context, sums, penalty,
+    )
+    qv_sum[...] = jnp.zeros_like(qv_sum)
+    qv_sum[0:1] = jnp.sum(grad_proj[0].astype(F32), axis=0, keepdims=True)
+    qv_sum[1:2] = jnp.sum(grad_proj[2].astype(F32), axis=0, keepdims=True)
     gather.finish()
     scatter.finish()
 
@@ -503,7 +546,7 @@
 
 def layer_forward(x, w, slopes):
     block, width = x.shape
-    length = block * lax.axis_size("tensor")
+    length = block * lax.axis_size(TENSOR)
     local = w["out"].shape[0]
     heads = local // HEAD
     normed, proj, context, totals, middle = call(
@@ -512,7 +555,7 @@
         1,
         (x, row_vector(w["ln1_gain"]), row_vector(w["ln1_bias"]), w["qkv"], w["b_qkv"], w["out"], row_vector(w["b_out"]), slopes),
         [((length, width), BF16), ((3, length, local), BF16), ((length, local), BF16), ((heads, length), F32), ((block, width), F32)],
-        [pltpu.VMEM((length, block), F32)] + link_scratch(block, width),
+        [pltpu.VMEM((length, LANES), F32)] + link_scratch(block, width),
     )
     units = w["up"].shape[1]
     second, activated, slope_of, leaving = call(
@@ -529,7 +572,7 @@
 
 def layer_backward(incoming, w, s, slopes):
     block, width = incoming.shape
-    length = block * lax.axis_size("tensor")
+    length = block * lax.axis_size(TENSOR)
     local, units = w["out"].shape[0], w["up"].shape[1]
     down_rows, grad_up, grad_middle, small_a, up_sum = call(
         mlp_backward_kernel,
@@ -545,10 +588,10 @@
         4,
         (grad_middle, s["x"], row_vector(w["ln1_gain"]), w["qkv"], w["out"], slopes, s["proj"], s["totals"]),
         [((length, width), BF16), ((3, length, local), BF16), ((block, width), F32), ((8, width), F32), ((8, local), F32)],
-        [pltpu.VMEM((length, local), BF16), pltpu.VMEM((2, length, PAIR), F32), pltpu.VMEM((length, block), F32)]
+        [pltpu.VMEM((length, local), BF16), pltpu.VMEM((2, length, PAIR), F32), pltpu.VMEM((length, LANES), F32)]
         + link_scratch(block, width),
     )
-    small = jnp.stack([small_b[0], small_b[1], small_a[0], small_a[1], small_a[2], small_a[3]])
+    small = jnp.concatenate([small_b[:2], small_a[2:6]])
     large = dict(
         qkv=jnp.einsum("td,cth->cdh", s["normed"], grad_proj, preferred_element_type=F32),
         out=jnp.einsum("th,td->hd", s["context"], attn_rows, preferred_element_type=F32),
@@ -564,8 +607,8 @@
     def __init__(self, layer, shards, whole, sems):
         self.layer, self.shards, self.whole = layer, shards, whole
         self.first, self.line, self.last, self.local = sems
-        self.section, self.place = lax.axis_index("section"), lax.axis_index("dp")
-        self.count = lax.axis_size("dp")
+        self.section, self.place = lax.axis_index(SECTION), lax.axis_index(DP)
+        self.count = lax.axis_size(DP)
         self.other = 1 - self.section
         self.owner = self.section == layer
         self.half = jnp.where(self.owner, 0, 1)
@@ -597,16 +640,16 @@
 
     def over_first(self, i):
         return self.copy(
-            self.mine(i, 1), self.at(i, 1, self.place), self.first, (i,), {"section": self.other}
+            self.mine(i, 1), self.at(i, 1, self.place), self.first, (i,), {SECTION: self.other}
         )
 
     def over_last(self, i, place, src=None):
         at = self.at(i, self.half, place)
-        return self.copy(at if src is None else src, at, self.last, (i, place), {"section": self.other})
+        return self.copy(at if src is None else src, at, self.last, (i, place), {SECTION: self.other})
 
     def from_last(self, i, place):
         at = self.at(i, 1 - self.half, place)
-        return self.copy(at, at, self.last, (i, place), {"section": self.other})
+        return self.copy(at, at, self.last, (i, place), {SECTION: self.other})
 
     def along(self, i, place, right, src=None):
         at = self.at(i, self.half, place)
@@ -615,7 +658,7 @@
             at,
             self.line,
             (i, place, int(right)),
-            {"dp": self.place + (1 if right else -1)},
+            {DP: self.place + (1 if right else -1)},
         )
 
     def onward(self, i, place, right, src=None):
@@ -632,16 +675,13 @@
         @pl.when(self.owner)
         def _():
             self.over_first(i).start()
-
-    def start(self, i):
-        @pl.when(self.owner)
-        def _():
             for right in (True, False):
                 self.onward(i, self.place, right, self.mine(i, 0))
             self.over_last(i, self.place, self.mine(i, 0)).start()
             for half in range(2):
                 self.keep(i, half).start()
 
+    def start(self, i):
         @pl.when(jnp.logical_not(self.owner))
         def _():
             self.over_first(i).wait_recv()
@@ -700,21 +740,33 @@
     ]
 
 
-def greet_all(ring):
+def greet_all(ring, whole_line=False):
     barrier = pltpu.get_barrier_semaphore()
-    section, place, count = lax.axis_index("section"), lax.axis_index("dp"), lax.axis_size("dp")
-    for device in ({"tensor": ring.mate}, {"tensor": ring.peer}, {"section": 1 - section}):
+    section, place, count = lax.axis_index(SECTION), lax.axis_index(DP), lax.axis_size(DP)
+    for device in ({TENSOR: ring.mate}, {TENSOR: ring.peer}, {SECTION: 1 - section}):
         pl.semaphore_signal(barrier, inc=1, device_id=device, device_id_type=MESH)
+    if whole_line:
+        for there in range(count):
+
+            @pl.when(there != place)
+            def _():
+                pl.semaphore_signal(barrier, inc=1, device_id={DP: there}, device_id_type=MESH)
+
+        pl.semaphore_wait(barrier, 2 + count)
+        return
 
     @pl.when(place > 0)
     def _():
-        pl.semaphore_signal(barrier, inc=1, device_id={"dp": place - 1}, device_id_type=MESH)
+        pl.semaphore_signal(barrier, inc=1, device_id={DP: place - 1}, device_id_type=MESH)
 
     @pl.when(place + 1 < count)
     def _():
-        pl.semaphore_signal(barrier, inc=1, device_id={"dp": place + 1}, device_id_type=MESH)
+        pl.semaphore_signal(barrier, inc=1, device_id={DP: place + 1}, device_id_type=MESH)
 
     pl.semaphore_wait(barrier, 3 + jnp.where(place > 0, 1, 0) + jnp.where(place + 1 < count, 1, 0))
+
+
+PUMP_POINTS = ({3: 4, 6: 5, 9: 6, 11: 7, 12: 8, 13: 9, 14: 10}, {})
 
 
 class Pump:
@@ -722,16 +774,10 @@
         self.pieces = [(crossing, i) for crossing in crossings for i in range(4)]
         self.hops = crossings[0].count
         self.done = 0
-        for piece in range(2):
-            self.begin(piece)
-
-    def begin(self, piece):
-        if piece < len(self.pieces):
-            crossing, i = self.pieces[piece]
+        for crossing, i in self.pieces:
             crossing.begin(i)
 
     def stage(self, number):
-        self.begin(number + 2)
         for hops in range(self.hops):
             if 0 <= number - hops < len(self.pieces):
                 crossing, i = self.pieces[number - hops]
@@ -745,8 +791,8 @@
             self.stage(self.done)
             self.done += 1
 
-    def tick(self):
-        self.until(self.done)
+    def tick(self, layer, point):
+        self.until(PUMP_POINTS[layer].get(point, -1))
 
     def have(self, piece):
         self.until(piece + self.hops - 1)
@@ -771,7 +817,7 @@
     penalty, own, stage, land, gather_sems, scatter_sems, save_sems, vector_sems = refs[:8]
     cross_sems = refs[8:]
     ring = Ring(x.shape[0])
-    section = lax.axis_index("section")
+    section = lax.axis_index(SECTION)
     greet_all(ring)
     crossings = [
         Cross(l, shards, held[l][6:10], [sem.at[l] for sem in cross_sems]) for l in range(layers)
@@ -782,7 +828,7 @@
         dst_ref=vectors.at[section],
         send_sem=vector_sems.at[0],
         recv_sem=vector_sems.at[1],
-        device_id={"section": 1 - section},
+        device_id={SECTION: 1 - section},
         device_id_type=MESH,
     )
     vector_in = pltpu.make_async_remote_copy(
@@ -790,7 +836,7 @@
         dst_ref=vectors.at[1 - section],
         send_sem=vector_sems.at[0],
         recv_sem=vector_sems.at[1],
-        device_id={"section": 1 - section},
+        device_id={SECTION: 1 - section},
         device_id_type=MESH,
     )
     vector_out.start()
@@ -819,7 +865,7 @@
 
         def link(every, phase):
             gather = Gather(ring, every, gather_sems.at[phase])
-            scatter = Scatter(ring, stage.at[phase], land.at[phase], scatter_sems.at[phase])
+            scatter = Scatter(ring, stage, land.at[phase], scatter_sems.at[phase])
             links.append((gather, scatter))
             return gather, scatter
 
@@ -831,7 +877,7 @@
         attention_forward_body(
             ring, gather, scatter, entering, row(0), row(1), wq, qv, wo, row(2), slopes,
             normed, proj, context, totals, middle, penalty,
-            qkv_ready=lambda: have(0), out_ready=lambda: have(1), tick=pump.tick,
+            qkv_ready=lambda: have(0), out_ready=lambda: have(1), tick=lambda point, l=l: pump.tick(l, point),
         )
         save(l, 0, normed)
         save(l, 1, proj)
@@ -847,7 +893,7 @@
         mlp_forward_body(
             ring, gather, scatter, middle, row(3), row(4), wu, row(5), wd, row(6),
             second, activated, slope_of, leaving, own,
-            ready=ready, tick=pump.tick,
+            ready=ready, tick=lambda point, l=l: pump.tick(l, point),
         )
         save(l, 3, second)
         save(l, 4, activated)
@@ -862,9 +908,9 @@
 
 
 def forward_call(x, vector, shards, slopes):
-    layers, places = lax.axis_size("section"), lax.axis_size("dp")
+    layers, places = lax.axis_size(SECTION), lax.axis_size(DP)
     block, width = x.shape
-    length = block * lax.axis_size("tensor")
+    length = block * lax.axis_size(TENSOR)
     sq, so, su, sd = shards
     local, units = so.shape[0], sd.shape[0]
     heads = local // HEAD
@@ -890,9 +936,9 @@
         out_specs=([far] * len(kept) + [vmem] * len(near)) * layers + [vmem],
         scratch_shapes=[pltpu.VMEM(shape, dtype) for _ in range(layers) for shape, dtype in kept]
         + [
-            pltpu.VMEM((length, block), F32),
+            pltpu.VMEM((length, LANES), F32),
             pltpu.VMEM((block, width), F32),
-            pltpu.VMEM((2, 3, block, width), BF16),
+            pltpu.VMEM((3, block, width), BF16),
             pltpu.VMEM((2, 3, block, width), BF16),
             pltpu.SemaphoreType.DMA((2, 2, 3, CHUNKS)),
             pltpu.SemaphoreType.DMA((2, 2, 3, CHUNKS)),
@@ -913,12 +959,575 @@
         saved.append(dict(x=entering, normed=normed, proj=proj, context=context, totals=totals, middle=middle, second=second, activated=activated, slope_of=slope_of))
         weights.append(dict(qkv=wq, out=wo, up=wu, down=wd, ln1_gain=vectors[l, 0], ln2_gain=vectors[l, 3]))
         entering = leaving
-    return [made[13 * l + 12] for l in range(layers)], saved, weights
+    return [made[13 * l + 12] for l in range(layers)], saved, weights, vectors
+
+
+class Fold:
+    def __init__(self, layer, kind, parts, first_land, line_land, last_land, out, sems, number):
+        self.kind, self.parts, self.out = kind, parts, out
+        self.first_land, self.line_land, self.last_land = first_land, line_land, last_land
+        self.first, self.line, self.last = sems
+        self.number = number
+        self.section, self.place = lax.axis_index(SECTION), lax.axis_index(DP)
+        self.count = lax.axis_size(DP)
+        self.owner = self.section == layer
+        self.half = jnp.where(self.owner, 0, 1)
+        self.events = self.count + 2
+        self.ran = 0
+
+    def at(self, half, place):
+        ref = self.parts
+        if self.kind == 0:
+            rows = ref.shape[1] // (2 * self.count)
+            return ref.at[:, rows_at((place * 2 + half) * rows, rows), :]
+        if self.kind == 2:
+            rows = ref.shape[0] // (2 * self.count)
+            return ref.at[rows_at((place * 2 + half) * rows, rows), :]
+        rows, columns = ref.shape[0] // 2, ref.shape[1] // self.count
+        return ref.at[rows_at(half * rows, rows), rows_at(place * columns, columns)]
+
+    def out_at(self, half):
+        ref = self.out
+        rows = ref.shape[1 if self.kind == 0 else 0] // 2
+        return ref.at[:, pl.ds(half * rows, rows), :] if self.kind == 0 else ref.at[pl.ds(half * rows, rows), :]
+
+    def copy(self, src, dst, sems, where, device):
+        return pltpu.make_async_remote_copy(
+            src_ref=src,
+            dst_ref=dst,
+            send_sem=sems.at[(0, self.number) + where],
+            recv_sem=sems.at[(1, self.number) + where],
+            device_id=device,
+            device_id_type=MESH,
+        )
+
+    def over_first(self, place):
+        return self.copy(
+            self.at(1 - self.half, place),
+            self.first_land.at[place],
+            self.first,
+            (place,),
+            {SECTION: 1 - self.section},
+        )
+
+    def along(self, place, right, to):
+        slot = place if right else jnp.where(place == to, self.count, place)
+        return self.copy(
+            self.at(self.half, place),
+            self.line_land.at[slot],
+            self.line,
+            (place, int(right)),
+            {DP: self.place + (1 if right else -1)},
+        )
+
+    def over_last(self):
+        return self.copy(
+            self.at(self.half, self.place),
+            self.last_land,
+            self.last,
+            (),
+            {SECTION: 1 - self.section},
+        )
+
+    def begin(self):
+        for hops in range(self.count - 1, -1, -1):
+            for right in (True, False) if hops else (True,):
+                place = self.place + hops if right else self.place - hops
+
+                @pl.when(place < self.count if right else place >= 0)
+                def _():
+                    self.over_first(place).start()
+
+    def met(self, place):
+        self.over_first(place).wait_recv()
+        at = self.at(self.half, place)
+        at[...] = (at[...].astype(F32) + self.first_land[place].astype(F32)).astype(BF16)
+
+    def took(self, place, right):
+        at = self.at(self.half, place)
+        self.along(place, right, self.place).wait_recv()
+        slot = place if right else jnp.where(place == self.place, self.count, place)
+        at[...] = (at[...].astype(F32) + self.line_land[slot].astype(F32)).astype(BF16)
+
+    def event(self):
+        hops = self.count - 1 - self.ran
+        self.ran += 1
+        if hops > 0:
+            for right in (True, False):
+                place = self.place + hops if right else self.place - hops
+
+                @pl.when(place < self.count if right else place >= 0)
+                def _():
+                    self.met(place)
+
+                    @pl.when(self.place > 0 if right else self.place + 1 < self.count)
+                    def _():
+                        self.took(place, right)
+
+                    self.along(place, right, self.place + (1 if right else -1)).start()
+
+        elif hops == 0:
+            self.met(self.place)
+
+            @pl.when(self.place > 0)
+            def _():
+                self.took(self.place, True)
+
+            @pl.when(self.place + 1 < self.count)
+            def _():
+                self.took(self.place, False)
+
+            @pl.when(self.owner)
+            def _():
+                self.out_at(0)[...] = self.at(0, self.place)[...].astype(F32)
+
+            @pl.when(jnp.logical_not(self.owner))
+            def _():
+                self.over_last().start()
+
+        elif hops == -1:
+
+            @pl.when(self.owner)
+            def _():
+                self.over_last().wait_recv()
+                self.out_at(1)[...] = self.last_land[...].astype(F32)
+
+    def drain(self):
+        for place in range(self.count):
+            self.over_first(place).wait_send()
+
+            @pl.when(jnp.logical_and(place > self.place, self.place + 1 < self.count))
+            def _():
+                self.along(place, True, self.place + 1).wait_send()
+
+            @pl.when(jnp.logical_and(place < self.place, self.place > 0))
+            def _():
+                self.along(place, False, self.place - 1).wait_send()
+
+        @pl.when(jnp.logical_not(self.owner))
+        def _():
+            self.over_last().wait_send()
+
+
+class Folds:
+    def __init__(self):
+        self.folds = []
+
+    def begin(self, fold):
+        fold.begin()
+        self.folds.append(fold)
+
+    def tick(self):
+        before = None
+        for fold in list(self.folds):
+            limit = fold.events - 1 if before is None else before - 1
+            if fold.ran < fold.events - 1 and (fold.ran < limit or before is None):
+                fold.event()
+            before = fold.ran if fold.ran < fold.events - 1 else fold.events
+
+    def finish(self):
+        while any(fold.ran < fold.events - 1 for fold in self.folds):
+            self.tick()
+        for fold in self.folds:
+            fold.drain()
+
+
+def fold_shapes(kind, count, width, local, units):
+    if kind == 0:
+        return (3, width, local), (3, width // count // 2, local), (3, width // count, local)
+    if kind == 1:
+        return (local, width), (local // 2, width // count), (local, width // count)
+    if kind == 2:
+        return (width, units), (width // count // 2, units), (width // count, units)
+    return (units, width), (units // 2, width // count), (units, width // count)
+
+
+QKV, OUT, UP, DOWN = 0, 1, 2, 3
+
+
+class Names:
+    pass
+
+
+def take_refs(names, refs):
+    bag = Names()
+    for name, ref in zip(names, refs, strict=True):
+        setattr(bag, name, ref)
+    return bag
+
+
+def backward_kernel(layer, top, names, kinds, *refs):
+    r = take_refs(names, refs)
+    block, width = r.x.shape
+    local, units = r.wo.shape[0], r.wd.shape[0]
+    count = lax.axis_size(DP)
+    section, place = lax.axis_index(SECTION), lax.axis_index(DP)
+    other = 1 - section
+    ring = Ring(block)
+    greet_all(ring, not top)
+    loads = {}
+    for number, name in enumerate(("wd", "slope", "wu", "activated", "second", "wo", "proj", "wq", "context")):
+        loads[name] = pltpu.make_async_copy(
+            getattr(r, name), getattr(r, name + "_here"), r.load_sems.at[number]
+        )
+        loads[name].start()
+    normed_load = pltpu.make_async_copy(r.normed, r.activated_here, r.load_sems.at[9])
+    folds = Folds()
+    made_folds = {}
+
+    def make_fold(key, of_layer, kind, parts, out, number):
+        made_folds[key] = Fold(
+            of_layer, kind, parts, getattr(r, "first_" + key), getattr(r, "line_" + key),
+            getattr(r, "last_" + key), out, (r.first_sems, r.line_sems, r.end_sems), number,
+        )
+
+    def passing(src, dst, sem):
+        return pltpu.make_async_remote_copy(
+            src_ref=src, dst_ref=dst, send_sem=r.pass_sems.at[0, sem], recv_sem=r.pass_sems.at[1, sem],
+            device_id={SECTION: other}, device_id_type=MESH,
+        )
+
+    r.small[...] = jnp.zeros_like(r.small)
+
+    def add_small(i, value):
+        r.small[pl.ds(i, 1)] += value
+
+    def add_up(value):
+        r.small[6:7] += value
+
+    kept = []
+    if top:
+        for s in range(2):
+
+            @pl.when(section == s)
+            def _():
+                r.acts_out[s] = (r.act0 if s == 0 else r.act1)[...]
+                passing(r.act1 if s == 0 else r.act0, r.acts_out.at[s], 0).start()
+
+        incoming = r.incoming
+    else:
+        incoming_load = pltpu.make_async_copy(r.incoming, r.grads_out.at[1], r.load_sems.at[11])
+        incoming_load.start()
+        incoming_load.wait()
+        r.rounded[...] = r.grads_out[1].astype(BF16)
+        incoming = r.rounded
+
+        @pl.when(section == 0)
+        def _():
+            passing(r.rounded, r.grads_land, 0).start()
+
+        for number, (src, dst) in enumerate(((r.gu_in, r.gu), (r.gd_in, r.gd), (r.go_in, r.go))):
+            copy = pltpu.make_async_copy(src, dst, r.keep_sems.at[number])
+            kept.append(copy)
+
+            @pl.when(section == 1)
+            def _():
+                copy.start()
+
+        make_fold("q1", 1, QKV, r.q1_here, r.gq, 4)
+        q1_load = pltpu.make_async_copy(r.q1, r.q1_here, r.load_sems.at[10])
+        q1_load.start()
+        q1_load.wait()
+        folds.begin(made_folds["q1"])
+    fill_penalty(r.penalty)
+
+    phase = 0
+    gather = Gather(ring, r.down_rows, r.gather_sems.at[0])
+    scatter = Scatter(ring, r.stage, r.land.at[0], r.scatter_sems.at[0])
+
+    def ready_mlp():
+        for name in ("wd", "slope", "wu"):
+            loads[name].wait()
+
+    def mlp_made():
+        loads["activated"].wait()
+        for start in range(0, units, block):
+            at = pl.ds(start, block)
+            r.part_d[at] = mm_a(r.activated_here[:, at], r.down_rows[...]).astype(BF16)
+        make_fold("d", layer, DOWN, r.part_d, r.gd, 0)
+        folds.begin(made_folds["d"])
+        normed_load.start()
+        loads["second"].wait()
+        for start in range(0, width, block):
+            at = pl.ds(start, block)
+            r.part_u[at] = mm_a(r.second_here[:, at], r.slope_here[...]).astype(BF16)
+        make_fold("u", layer, UP, r.part_u, r.gu, 1)
+        folds.begin(made_folds["u"])
+
+    mlp_backward_body(
+        ring, gather, scatter, incoming, r.middle, lambda: r.vectors[layer, 3:4, :],
+        r.wu_here, r.wd_here, r.slope_here, r.down_rows, r.slope_here, r.grad_hidden,
+        add_small, add_up, r.own,
+        ready=ready_mlp, made=mlp_made, tick=folds.tick,
+    )
+    gather.finish()
+    scatter.finish()
+    gather = Gather(ring, r.attn_rows, r.gather_sems.at[1])
+    scatter = Scatter(ring, r.stage, r.land.at[1], r.scatter_sems.at[1])
+
+    def out_ready():
+        loads["wo"].wait()
+
+    def gathered():
+        loads["context"].wait()
+        r.part_o[...] = mm_a(r.context_here[...], r.attn_rows[...]).astype(BF16)
+        make_fold("o", layer, OUT, r.part_o, r.go, 2)
+        folds.begin(made_folds["o"])
+
+    def attn_ready():
+        loads["proj"].wait()
+        loads["wq"].wait()
+
+    def attn_made():
+        normed_load.wait()
+        for part in range(3):
+            for start in range(0, width, block):
+                at = pl.ds(start, block)
+                made = mm_a(r.activated_here[:, at], r.grad_proj[part]).astype(BF16)
+                r.part_q[part, at] = made
+        r.small[7:8, 0:local] = jnp.sum(r.grad_proj[0].astype(F32), axis=0, keepdims=True)
+        r.small[7:8, local : 2 * local] = jnp.sum(r.grad_proj[2].astype(F32), axis=0, keepdims=True)
+        if not top:
+            make_fold("q", layer, QKV, r.part_q, r.gq, 3)
+            folds.begin(made_folds["q"])
+
+    attention_backward_body(
+        ring, gather, scatter, r.grad_hidden, r.x, lambda: r.vectors[layer, 0:1, :],
+        r.wq_here, r.wo_here, r.slopes, r.proj_here, r.totals, r.attn_rows, r.grad_proj,
+        r.grad_hidden, add_small, r.grad_context, r.sums, r.penalty,
+        out_ready=out_ready, ready=attn_ready, gathered=gathered, made=attn_made, tick=folds.tick,
+    )
+    gather.finish()
+    scatter.finish()
+    if top:
+        folds.finish()
+        for s in range(2):
+
+            @pl.when(section == s)
+            def _():
+                passing(r.act1 if s == 0 else r.act0, r.acts_out.at[s], 0).wait_send()
+                passing(r.act0, r.acts_out.at[1 - s], 0).wait_recv()
+
+        return
+
+    @pl.when(section == 0)
+    def _():
+        r.small_go[0] = r.small_in[...]
+        r.small_keep[...] = r.small[...]
+
+    @pl.when(section == 1)
+    def _():
+        r.small_go[0] = r.small[...]
+        r.small_keep[...] = r.small_in[...]
+        r.rounded[...] = r.grad_hidden[...].astype(BF16)
+        passing(r.rounded, r.grads_land, 0).start()
+
+    small_pass = passing(r.small_go.at[0], r.small_land.at[0], 1)
+    small_pass.start()
+    small_pass.wait()
+    r.small_go[1] = r.small_keep[...] + r.small_land[0]
+
+    def to_place(there, slot, sem):
+        return pltpu.make_async_remote_copy(
+            src_ref=r.small_go.at[1], dst_ref=r.small_land.at[slot], send_sem=r.small_sems.at[0, sem],
+            recv_sem=r.small_sems.at[1, slot], device_id={DP: there}, device_id_type=MESH,
+        )
+
+    for there in range(count):
+
+        @pl.when(there != place)
+        def _():
+            to_place(there, 1 + place, 1 + there).start()
+
+    r.small_land[1 + place] = r.small_go[1]
+    for there in range(count):
+
+        @pl.when(there != place)
+        def _():
+            to_place(there, 1 + there, 1 + there).wait_recv()
+            to_place(there, 1 + place, 1 + there).wait_send()
+
+    total = r.small_land[1]
+    for there in range(1, count):
+        total += r.small_land[1 + there]
+    r.small_go[2] = total
+    for step, device in enumerate((ring.mate, ring.peer)):
+        hop = pltpu.make_async_remote_copy(
+            src_ref=r.small_go.at[2 + step], dst_ref=r.small_land.at[1 + count + step],
+            send_sem=r.small_sems.at[0, 1 + count + step], recv_sem=r.small_sems.at[1, 1 + count + step],
+            device_id={TENSOR: device}, device_id_type=MESH,
+        )
+        hop.start()
+        hop.wait()
+        r.small_go[3 + step] = r.small_go[2 + step] + r.small_land[1 + count + step]
+    r.small_out[0:6] = r.small_go[4, 0:6]
+    r.small_out[6:8] = total[6:8]
+
+    q1_parts = folds.finish()
+    for copy in kept:
+
+        @pl.when(section == 1)
+        def _():
+            copy.wait()
+
+    grads_pass = passing(r.rounded, r.grads_land, 0)
+    grads_pass.wait()
+    for s in range(2):
+
+        @pl.when(section == s)
+        def _():
+            if s == 0:
+                r.grads_out[0] = r.grad_hidden[...]
+            r.grads_out[1 - s] = r.grads_land[...].astype(F32)
+
+
+def mm_a(left, right):
+    return lax.dot_general(left, right, (((0,), (0,)), ((), ())), preferred_element_type=F32)
+
+
+def backward_call(layer, top, values, slopes):
+    count = lax.axis_size(DP)
+    block, width = values["x"].shape
+    length = block * lax.axis_size(TENSOR)
+    local, units = values["wo"].shape[0], values["wd"].shape[0]
+    vmem, far = pl.BlockSpec(memory_space=pltpu.VMEM), pl.BlockSpec(memory_space=pl.ANY)
+    ins = ["middle", "x", "totals", "vectors", "slopes"]
+    ins_far = ["wd", "wu", "wo", "wq", "slope", "activated", "second", "normed", "proj", "context"]
+    outs = [("grad_hidden", (block, width), F32), ("small", (8, width), F32)]
+    shards = [
+        ("gu", fold_shapes(UP, count, width, local, units)[2], F32),
+        ("gd", fold_shapes(DOWN, count, width, local, units)[2], F32),
+        ("go", fold_shapes(OUT, count, width, local, units)[2], F32),
+    ]
+    whole = {kind: fold_shapes(kind, count, width, local, units)[0] for kind in range(4)}
+    if top:
+        ins += ["incoming", "act0", "act1"]
+        outs += shards + [("part_q", whole[QKV], BF16), ("acts_out", (2, block, width), BF16)]
+    else:
+        ins += ["small_in"]
+        ins_far += ["incoming", "gu_in", "gd_in", "go_in", "q1"]
+        outs += shards + [
+            ("gq", fold_shapes(QKV, count, width, local, units)[2], F32),
+            ("small_out", (8, width), F32),
+            ("grads_out", (2, block, width), F32),
+        ]
+    dma = pltpu.SemaphoreType.DMA
+    scratch = dict(
+        wd_here=pltpu.VMEM((units, width), BF16),
+        wu_here=pltpu.VMEM((width, units), BF16),
+        wo_here=pltpu.VMEM((local, width), BF16),
+        wq_here=pltpu.VMEM((3, width, local), BF16),
+        slope_here=pltpu.VMEM((length, units), BF16),
+        activated_here=pltpu.VMEM((length, units), BF16),
+        second_here=pltpu.VMEM((length, width), BF16),
+        proj_here=pltpu.VMEM((3, length, local), BF16),
+        context_here=pltpu.VMEM((length, local), BF16),
+        down_rows=pltpu.VMEM((length, width), BF16),
+        attn_rows=pltpu.VMEM((length, width), BF16),
+        grad_proj=pltpu.VMEM((3, length, local), BF16),
+        grad_context=pltpu.VMEM((length, local), BF16),
+        sums=pltpu.VMEM((2, length, PAIR), F32),
+        penalty=pltpu.VMEM((length, LANES), F32),
+        own=pltpu.VMEM((block, width), F32),
+        stage=pltpu.VMEM((3, block, width), BF16),
+        land=pltpu.VMEM((2, 3, block, width), BF16),
+        gather_sems=dma((2, 2, 3, CHUNKS)),
+        scatter_sems=dma((2, 2, 3, CHUNKS)),
+        load_sems=dma((12,)),
+        pass_sems=dma((2, 2)),
+        first_sems=dma((2, 5, count)),
+        line_sems=dma((2, 5, count, 2)),
+        end_sems=dma((2, 5)),
+        part_d=pltpu.VMEM(whole[DOWN], BF16),
+        part_u=pltpu.VMEM(whole[UP], BF16),
+        part_o=pltpu.VMEM(whole[OUT], BF16),
+    )
+    keys = {"d": DOWN, "u": UP, "o": OUT}
+    if not top:
+        keys.update({"q": QKV, "q1": QKV})
+        scratch.update(
+            part_q=pltpu.VMEM(whole[QKV], BF16),
+            q1_here=pltpu.VMEM(whole[QKV], BF16),
+            rounded=pltpu.VMEM((block, width), BF16),
+            grads_land=pltpu.VMEM((block, width), BF16),
+            small_go=pltpu.VMEM((5, 8, width), F32),
+            small_keep=pltpu.VMEM((8, width), F32),
+            small_land=pltpu.VMEM((3 + count, 8, width), F32),
+            small_sems=dma((2, 3 + count)),
+            keep_sems=dma((3,)),
+        )
+    for key, kind in keys.items():
+        half = fold_shapes(kind, count, width, local, units)[1]
+        scratch["first_" + key] = pltpu.VMEM((count,) + half, BF16)
+        scratch["line_" + key] = pltpu.VMEM((count + 1,) + half, BF16)
+        scratch["last_" + key] = pltpu.VMEM(half, BF16)
+    values = dict(values, slopes=slopes)
+    names = ins + ins_far + [item[0] for item in outs] + list(scratch)
+    made = pl.pallas_call(
+        functools.partial(backward_kernel, layer, top, names, None),
+        out_shape=[jax.ShapeDtypeStruct(shape, dtype) for _, shape, dtype in outs],
+        in_specs=[vmem] * len(ins) + [far] * len(ins_far),
+        out_specs=[vmem] * len(outs),
+        scratch_shapes=list(scratch.values()),
+        compiler_params=pltpu.CompilerParams(
+            collective_id=6 + layer, has_side_effects=True, vmem_limit_bytes=VMEM_LIMIT
+        ),
+        name="backward_%d" % layer,
+    )(*[values[name] for name in ins + ins_far])
+    return {item[0]: value for item, value in zip(outs, made)}
 
 
 def swapped(value):
-    count = lax.axis_size("section")
-    return lax.ppermute(value, "section", [(i, (i + 1) % count) for i in range(count)])
+    count = lax.axis_size(SECTION)
+    return lax.ppermute(value, SECTION, [(i, (i + 1) % count) for i in range(count)])
+
+
+def backward_near(incoming, acts, saved, layers, vectors, slopes, local):
+    def values(l, **more):
+        w, s = layers[l], saved[l]
+        return dict(
+            middle=s["middle"], x=s["x"], totals=s["totals"], vectors=vectors, slope=s["slope_of"],
+            activated=s["activated"], second=s["second"], normed=s["normed"], proj=s["proj"],
+            context=s["context"], wd=w["down"], wu=w["up"], wo=w["out"], wq=w["qkv"], **more,
+        )
+
+    high = backward_call(1, True, values(1, incoming=incoming, act0=acts[0], act1=acts[1]), slopes)
+    low = backward_call(
+        0,
+        False,
+        values(
+            0, incoming=high["grad_hidden"], small_in=high["small"], gu_in=high["gu"],
+            gd_in=high["gd"], go_in=high["go"], q1=high["part_q"],
+        ),
+        slopes,
+    )
+    places = lax.axis_size(DP)
+    tensor, place = lax.axis_index(TENSOR), lax.axis_index(DP)
+    small = low["small_out"]
+    width = small.shape[1]
+    share = width // (lax.axis_size(TENSOR) * places)
+    vector = lax.dynamic_slice_in_dim(small[:6], (tensor * places + place) * share, share, axis=1)
+    up_share, qv_share = width // places, local // places
+    up = lax.dynamic_slice_in_dim(small[6], place * up_share, up_share)
+    qv = lax.dynamic_slice_in_dim(
+        small[7, : 2 * local].reshape(2, local), place * qv_share, qv_share, axis=1
+    )
+    return (
+        high["acts_out"][None],
+        low["grads_out"][None],
+        vector[0][None],
+        vector[1][None],
+        jnp.transpose(low["gq"], (1, 0, 2))[None],
+        qv[None],
+        low["go"][None],
+        vector[2][None],
+        vector[3][None],
+        vector[4][None],
+        low["gu"][None],
+        up[None],
+        low["gd"][None],
+        vector[5][None],
+    )
 
 
 def near_shards(depth, block):
@@ -931,7 +1540,7 @@
         return [jnp.where(section == l, value, other) for l in range(layer_count)]
 
     def over_dp(value, axis):
-        return both(lax.all_gather(value, "dp", axis=axis, tiled=True))
+        return both(lax.all_gather(value, DP, axis=axis, tiled=True))
 
     qkv_all, up_all = over_dp(jnp.transpose(w_qkv[0], (1, 0, 2)), 1), over_dp(w_up[0], 0)
     out_all, down_all = over_dp(w_out[0], 1), over_dp(w_down[0], 1)
@@ -978,10 +1587,10 @@
     w_down,
     b_down,
 ):
-    section = lax.axis_index("section")
-    layer_count = lax.axis_size("section")
+    section = lax.axis_index(SECTION)
+    layer_count = lax.axis_size(SECTION)
     local_heads = w_qkv.shape[3] // HEAD
-    head_ids = lax.axis_index("tensor") * local_heads + jnp.arange(local_heads, dtype=jnp.int32)
+    head_ids = lax.axis_index(TENSOR) * local_heads + jnp.arange(local_heads, dtype=jnp.int32)
     slopes = jnp.exp2(-8.0 * (head_ids.astype(jnp.float32) + 1.0) / HEADS)
     slopes = jnp.broadcast_to(slopes[:, None], (local_heads, inputs.shape[1]))
 
@@ -997,7 +1606,10 @@
             + [b_up[0], b_down[0], jnp.pad(b_qv[0].reshape(-1), (0, b_out.shape[1] - 2 * b_qv.shape[2]))]
         )
         shards = (jnp.transpose(w_qkv[0], (1, 0, 2)), w_out[0], w_up[0], w_down[0])
-        acts, saved, layers = forward_call(row, vector, shards, slopes)
+        acts, saved, layers, vectors = forward_call(row, vector, shards, slopes)
+        return backward_near(
+            target.astype(F32) * scale, acts, saved, layers, vectors, slopes, b_qv.shape[2]
+        )
     else:
         layers = gathered_layers(
             section, layer_count, w_qkv, w_out, w_up, w_down,
@@ -1029,12 +1641,12 @@
     def reduced(name, axis):
         items = [item[name].astype(jnp.bfloat16) for item in large]
         total = mine(items) + swapped(theirs(items))
-        return lax.psum_scatter(total, "dp", scatter_dimension=axis, tiled=True).astype(
+        return lax.psum_scatter(total, DP, scatter_dimension=axis, tiled=True).astype(
             jnp.float32
         )[None]
 
     small_total = mine(small) + swapped(theirs(small))
-    small_shards = lax.psum_scatter(small_total, ("tensor", "dp"), scatter_dimension=1, tiled=True)
+    small_shards = lax.psum_scatter(small_total, (TENSOR, DP), scatter_dimension=1, tiled=True)
     return (
         rows_of(acts),
         rows_of([item.astype(jnp.bfloat16) for item in grads]).astype(jnp.float32),
@@ -1058,38 +1670,38 @@
         per_device,
         mesh=mesh,
         in_specs=(
-            P("dp", "tensor", None),
-            P("dp", "tensor", None),
-            P("dp"),
+            P(DP, TENSOR, None),
+            P(DP, TENSOR, None),
+            P(DP),
             P(),
-            P("section", None),
-            P("section", None),
-            P("section", "dp", None, "tensor"),
-            P("section", None, "tensor"),
-            P("section", "tensor", "dp"),
-            P("section", None),
-            P("section", None),
-            P("section", None),
-            P("section", "dp", "tensor"),
-            P("section", "tensor"),
-            P("section", "tensor", "dp"),
-            P("section", None),
+            P(SECTION, None),
+            P(SECTION, None),
+            P(SECTION, DP, None, TENSOR),
+            P(SECTION, None, TENSOR),
+            P(SECTION, TENSOR, DP),
+            P(SECTION, None),
+            P(SECTION, None),
+            P(SECTION, None),
+            P(SECTION, DP, TENSOR),
+            P(SECTION, TENSOR),
+            P(SECTION, TENSOR, DP),
+            P(SECTION, None),
         ),
         out_specs=(
-            P("section", "dp", "tensor", None),
-            P("section", "dp", "tensor", None),
-            P("section", ("tensor", "dp")),
-            P("section", ("tensor", "dp")),
-            P("section", "dp", None, "tensor"),
-            P("section", None, ("tensor", "dp")),
-            P("section", "tensor", "dp"),
-            P("section", ("tensor", "dp")),
-            P("section", ("tensor", "dp")),
-            P("section", ("tensor", "dp")),
-            P("section", "dp", "tensor"),
-            P("section", ("tensor", "dp")),
-            P("section", "tensor", "dp"),
-            P("section", ("tensor", "dp")),
+            P(SECTION, DP, TENSOR, None),
+            P(SECTION, DP, TENSOR, None),
+            P(SECTION, (TENSOR, DP)),
+            P(SECTION, (TENSOR, DP)),
+            P(SECTION, DP, None, TENSOR),
+            P(SECTION, None, (TENSOR, DP)),
+            P(SECTION, TENSOR, DP),
+            P(SECTION, (TENSOR, DP)),
+            P(SECTION, (TENSOR, DP)),
+            P(SECTION, (TENSOR, DP)),
+            P(SECTION, DP, TENSOR),
+            P(SECTION, (TENSOR, DP)),
+            P(SECTION, TENSOR, DP),
+            P(SECTION, (TENSOR, DP)),
         ),
         check_vma=False,
     )

time: 713 us -> 563 us (0.79)
  waiting for transfers between devices: 193 us -> 0 us
  Pallas kernels: 393 us -> 535 us
  other arithmetic: 30.6 us -> 2.38 us
  matrix products: 25.2 us -> 0 us
  starting transfers between devices: 16.3 us -> 0 us
  between operations: 16 us -> 1.6 us
  blocking collectives: 11.3 us -> 0 us
    pallas_call x4 -> x2, Pallas kernels: 160 us -> 312 us  [backward_call(): pl.pallas_call(functools.partial(backward_kernel, layer, top, names, None...]
    ppermute x9 -> x0, waiting for transfers between devices: 122 us -> none  [swapped(): lax.ppermute(value, 'section', [(i, (i + 1) % count) for i in range(count)])]
    reduce_scatter x4 -> x0, waiting for transfers between devices: 71.2 us -> none  [reduced(): lax.psum_scatter(total, 'dp', scatter_dimension=axis, tiled=True)]
    dot_general x8 -> x0, matrix products: 25.2 us -> none  [the longest x2 10.7 us: layer_backward(): jnp.einsum('tf,td->fd', s['activated'], down_rows, preferred_element_type...]
    ppermute x9 -> x0, starting transfers between devices: 15.9 us -> none  [swapped(): lax.ppermute(value, 'section', [(i, (i + 1) % count) for i in range(count)])]
    unnamed x1 -> x0, blocking collectives: 11.3 us -> none
    pallas_call x1, Pallas kernels: 233 us -> 223 us  [forward_call(): pl.pallas_call(functools.partial(forward_kernel, layers), out_shape=[jax....]
    add x7 -> x0, other arithmetic: 8.92 us -> none  [the longest x6 8.9 us: reduced(): total = mine(items) + swapped(theirs(items))]
  transfers between devices with their start and end apart: 15 -> 0, of which waited for: 5 -> 0; matrix products, arithmetic and copies ran while one was open for 8% -> 0% of each run, Pallas kernels for 0% -> 0%
where the time goes in v4:
time: 563 us; the launch traced here: 554 us
  Pallas kernels  535 us (95%)
  local copies, waits for them, and re-layouts  15.6 us (3%)
    pallas_call x2, Pallas kernels, backward_call(): pl.pallas_call(functools.partial(backward_kernel, layer, top, names, None...  312 us
    pallas_call x1, Pallas kernels, forward_call(): pl.pallas_call(functools.partial(forward_kernel, layers), out_shape=[jax....  223 us

profile of v4, /device:TPU:0, one launch (start us, length us, event | category | flops | bytes accessed | tf_op | source)
XLA Modules:
  0.0 554.2 jit_solution(16173573255589462699)
XLA Ops:
  0.6 0.0 copy-start
  0.7 0.0 copy-start.8
  0.7 0.0 copy-start.9
  0.7 0.0 copy-start.7
  0.7 1.2 copy-done
  1.9 0.8 dynamic-slice_bitcast_fusion.refs_0_.refs_1_
  2.7 0.7 broadcast_in_dim.32.refs_6_.refs_4_
  3.4 0.7 copy.30
  4.1 1.4 stack.7.refs_1_
  5.5 222.6 %forward.1 = (bf16[1024,1024]{1,0:T(8,128)(2,1)}, bf16[3,1024,256]{2,1,0:T(8,128)(2,1)}, bf16[1024,256]{1,0:T(8,128)(2,1)}, bf16[1024,1024]{1,0:T(8,128)(2,1)}, ...) custom-call(bf16[256,1024]{1,0:T(8,128)(2,1)} %dynamic-slice_bitcast, ...), custom_call_target="tpu_custom_call" | custom-call | tf_op jit(solution)/shard_map/forward/pallas_call | solution.py:931
  228.1 0.0 copy-done.8
  228.1 0.6 dynamic_slice.22
  228.7 0.0 copy-done.9
  228.7 1.3 fusion.1
  230.6 0.0 copy-done.7
  230.6 1.1 multiply_bitcast_fusion.refs_5_
  231.7 115.7 %backward_1.1 = (f32[256,1024]{1,0:T(8,128)}, f32[8,1024]{1,0:T(8,128)}, f32[256,1024]{1,0:T(8,128)}, f32[1024,256]{1,0:T(8,128)}, f32[256,256]{1,0:T(8,128)}, /...) custom-call(f32[256,1024]{1,0:T(8,128)} %get-tuple-element.54.refs_0_, ...), custom_call_target="tpu_custom_call" | custom-call | tf_op jit(solution)/shard_map/backward_1/pallas_call | solution.py:1466
  347.4 0.0 copy-start.2
  347.4 196.4 %backward_0.1 = (f32[256,1024]{1,0:T(8,128)}, f32[8,1024]{1,0:T(8,128)}, f32[256,1024]{1,0:T(8,128)}, f32[1024,256]{1,0:T(8,128)}, f32[256,256]{1,0:T(8,128)}, /...) custom-call(f32[256,1024]{1,0:T(8,128)} %get-tuple-element.70.refs_0_, ...), custom_call_target="tpu_custom_call" | custom-call | tf_op jit(solution)/shard_map/backward_0/pallas_call | solution.py:1466
  543.8 0.8 constant_dynamic-slice_fusion.2
  544.6 0.5 fusion.2
  545.1 0.8 slice.34
  545.9 0.6 constant_dynamic-slice_fusion
  546.5 0.7 slice_reduce_fusion
  547.2 0.0 copy-start.1
  547.2 0.6 fusion
  547.8 0.0 copy-done.2
  547.9 1.0 copy.37
  548.8 0.0 copy-done.1
  548.8 0.0 copy-start.5
  548.8 0.0 copy-start.6
  548.8 1.3 copy.38
  550.1 0.4 copy-done.5
  550.5 0.0 copy-start.4
  550.5 0.0 copy-start.3
  550.5 0.9 copy.39
  551.4 0.0 copy-done.6
  551.4 0.7 copy.40
  552.1 0.0 copy-done.4
  552.1 1.0 copy.41
  553.1 0.0 copy-done.3
  553.1 1.0 copy.42
  (3 shorter events, 0.0 us)
Async XLA Ops:
  0.6 1.2 copy-start
  0.7 227.4 %copy-start.8 = (s32[2]{0:T(128)S(1)}, s32[2]{0:T(128)}, u32[]{:S(2)}) copy-start(s32[2]{0:T(128)} %param.18) | copy-start | bytes 28
  0.7 228.0 %copy-start.9 = (s32[46]{0:T(128)S(1)}, s32[46]{0:T(128)}, u32[]{:S(2)}) copy-start(s32[46]{0:T(128)} %param.19) | copy-start | bytes 556
  0.7 230.0 %copy-start.7 = (bf16[2,256,1024]{2,1,0:T(8,128)(2,1)S(1)}, bf16[2,256,1024]{2,1,0:T(8,128)(2,1)}, u32[]{:S(2)}) copy-start(bf16[2,256,1024]{2,1,0:T(8,128)(2,1)} %param.17) | copy-start | bytes 3145732
  347.4 200.4 %copy-start.2 = (bf16[2,256,1024]{2,1,0:T(8,128)(2,1)S(1)}, bf16[2,256,1024]{2,1,0:T(8,128)(2,1)}, u32[]{:S(2)}) copy-start(bf16[2,256,1024]{2,1,0:T(8,128)(2,1)} %get-tuple-element.69) | copy-start | bytes 3145732
  547.2 1.6 copy-start.1
  548.8 1.7 copy-start.5
  548.8 2.6 copy-start.6
  550.5 1.6 copy-start.4
  550.5 2.6 copy-start.3

commit v5 on v4

--- a/solution.py
+++ b/solution.py
@@ -199,7 +199,7 @@
     for pair in range(width // PAIR):
         lanes = pl.ds(pair * PAIR, PAIR)
         for start in range(0, length, block):
-            tick()
+            tick(pair * 4 + start // block)
             stop = start + block
             queries = proj[0, start:stop, lanes] * jnp.asarray(0.125, BF16)
             keys = proj[1, :stop, lanes]
@@ -386,20 +386,22 @@
         return mm_t(grad, w_up[...])
 
     own[...] = pull(rows_at(ring.me * block, block))
-    tick()
+    tick(0)
     for c in range(CHUNKS):
         gather.arrived_mate(c)
     part = pull(rows_at(ring.mate * block, block))
     for c in range(CHUNKS):
         scatter.put(2, c, part[c * chunk : (c + 1) * chunk])
-    tick()
+    tick(1)
     for c in range(CHUNKS):
         gather.arrived_peer(c)
         peer_part = pull(ring.rows(ring.peer, c))
         gather.arrived_far(c)
         scatter.put(0, c, pull(ring.rows(ring.far, c)))
         scatter.put(1, c, peer_part + scatter.take(0, c))
+        tick(2 + c)
     made()
+    tick(4)
     for c in range(CHUNKS):
         at = pl.ds(c * chunk, chunk)
         total = own[at] + scatter.take(2, c) + scatter.take(1, c)
@@ -411,6 +413,7 @@
         small(3, grad_gain)
         small(4, grad_shift)
         small(5, jnp.sum(before, axis=0, keepdims=True))
+        tick(5 + c)
 
 
 def attention_backward_body(
@@ -431,16 +434,16 @@
     for c in range(CHUNKS):
         gather.arrived_mate(c)
     pull(rows_at(ring.mate * block, block))
-    tick()
+    tick(7)
     for c in range(CHUNKS):
         gather.arrived_peer(c)
         pull(ring.rows(ring.peer, c))
         gather.arrived_far(c)
         pull(ring.rows(ring.far, c))
-        tick()
+        tick(8 + c)
     gathered()
     ready()
-    attend_backward(proj, grad_context, totals, slopes, penalty, grad_proj, sums, block, tick)
+    attend_backward(proj, grad_context, totals, slopes, penalty, grad_proj, sums, block, lambda at: tick(10 + at))
 
     def part_of(owner, c):
         at = ring.rows(owner, c)
@@ -455,6 +458,7 @@
     for c in range(CHUNKS):
         scatter.put(2, c, part_of(ring.mate, c))
     made()
+    tick(18)
     for c in range(CHUNKS):
         at = pl.ds(c * chunk, chunk)
         total = part_of(ring.me, c) + scatter.take(2, c) + scatter.take(1, c)
@@ -462,6 +466,7 @@
         grad_hidden[at] = grad_middle[at] + pulled
         small(0, grad_gain)
         small(1, grad_shift)
+        tick(19 + c)
 
 
 def mlp_backward_kernel(
@@ -1110,26 +1115,41 @@
 
 
 class Folds:
-    def __init__(self):
-        self.folds = []
-
-    def begin(self, fold):
-        fold.begin()
-        self.folds.append(fold)
-
-    def tick(self):
+    def __init__(self, plan):
+        self.plan, self.folds, self.begun = plan, {}, []
+
+    def add(self, name, fold):
+        self.folds[name] = fold
+
+    def reach(self, name, target):
+        fold = self.folds[name]
+        if fold not in self.begun:
+            fold.begin()
+            self.begun.append(fold)
+        while fold.ran < min(target, fold.events - 1):
+            fold.event()
+
+    def tick(self, point):
+        for name, target in self.plan.get(point, ()):
+            self.reach(name, target)
+
+    def round(self):
         before = None
-        for fold in list(self.folds):
-            limit = fold.events - 1 if before is None else before - 1
-            if fold.ran < fold.events - 1 and (fold.ran < limit or before is None):
+        for fold in self.begun:
+            if fold.ran < fold.events - 1 and (before is None or fold.ran < before):
                 fold.event()
-            before = fold.ran if fold.ran < fold.events - 1 else fold.events
+            before = fold.ran if fold.ran < fold.events - 1 else None
 
     def finish(self):
-        while any(fold.ran < fold.events - 1 for fold in self.folds):
-            self.tick()
-        for fold in self.folds:
+        while any(fold.ran < fold.events - 1 for fold in self.begun):
+            self.round()
+        for fold in self.begun:
             fold.drain()
+
+
+D_, U_, O_, Q_, R_ = range(5)
+HIGH_PLAN = {4: ((D_, 0),), 7: ((U_, 0),), 8: ((D_, 1),), 9: ((D_, 2),), 10: ((O_, 0),), 12: ((D_, 3),), 14: ((U_, 1),), 15: ((D_, 4),), 17: ((U_, 2),), 18: ((U_, 3), (O_, 1)), 19: ((D_, 5), (U_, 4), (O_, 2)), 20: ((U_, 5), (O_, 3))}
+LOW_PLAN = {4: ((R_, 1), (D_, 0)), 5: ((R_, 2),), 6: ((R_, 3),), 7: ((R_, 4), (U_, 0)), 8: ((D_, 1),), 9: ((R_, 5), (D_, 2)), 10: ((O_, 0),), 12: ((D_, 3),), 14: ((U_, 1),), 15: ((D_, 4),), 17: ((U_, 2),), 18: ((U_, 3), (O_, 1), (Q_, 0)), 19: ((D_, 5), (U_, 4), (O_, 2)), 20: ((U_, 5), (O_, 3), (Q_, 1))}
 
 
 def fold_shapes(kind, count, width, local, units):
@@ -1172,13 +1192,15 @@
         )
         loads[name].start()
     normed_load = pltpu.make_async_copy(r.normed, r.activated_here, r.load_sems.at[9])
-    folds = Folds()
-    made_folds = {}
+    folds = Folds(HIGH_PLAN if top else LOW_PLAN)
 
     def make_fold(key, of_layer, kind, parts, out, number):
-        made_folds[key] = Fold(
-            of_layer, kind, parts, getattr(r, "first_" + key), getattr(r, "line_" + key),
-            getattr(r, "last_" + key), out, (r.first_sems, r.line_sems, r.end_sems), number,
+        folds.add(
+            number,
+            Fold(
+                of_layer, kind, parts, getattr(r, "first_" + key), getattr(r, "line_" + key),
+                getattr(r, "last_" + key), out, (r.first_sems, r.line_sems, r.end_sems), number,
+            ),
         )
 
     def passing(src, dst, sem):
@@ -1224,11 +1246,11 @@
             def _():
                 copy.start()
 
-        make_fold("q1", 1, QKV, r.q1_here, r.gq, 4)
+        make_fold("q1", 1, QKV, r.q1_here, r.gq, R_)
         q1_load = pltpu.make_async_copy(r.q1, r.q1_here, r.load_sems.at[10])
         q1_load.start()
         q1_load.wait()
-        folds.begin(made_folds["q1"])
+        folds.reach(R_, 0)
     fill_penalty(r.penalty)
 
     phase = 0
@@ -1244,15 +1266,14 @@
         for start in range(0, units, block):
             at = pl.ds(start, block)
             r.part_d[at] = mm_a(r.activated_here[:, at], r.down_rows[...]).astype(BF16)
-        make_fold("d", layer, DOWN, r.part_d, r.gd, 0)
-        folds.begin(made_folds["d"])
+        make_fold("d", layer, DOWN, r.part_d, r.gd, D_)
+        folds.reach(D_, 0)
         normed_load.start()
         loads["second"].wait()
         for start in range(0, width, block):
             at = pl.ds(start, block)
             r.part_u[at] = mm_a(r.second_here[:, at], r.slope_here[...]).astype(BF16)
-        make_fold("u", layer, UP, r.part_u, r.gu, 1)
-        folds.begin(made_folds["u"])
+        make_fold("u", layer, UP, r.part_u, r.gu, U_)
 
     mlp_backward_body(
         ring, gather, scatter, incoming, r.middle, lambda: r.vectors[layer, 3:4, :],
@@ -1271,8 +1292,7 @@
     def gathered():
         loads["context"].wait()
         r.part_o[...] = mm_a(r.context_here[...], r.attn_rows[...]).astype(BF16)
-        make_fold("o", layer, OUT, r.part_o, r.go, 2)
-        folds.begin(made_folds["o"])
+        make_fold("o", layer, OUT, r.part_o, r.go, O_)
 
     def attn_ready():
         loads["proj"].wait()
@@ -1288,8 +1308,7 @@
         r.small[7:8, 0:local] = jnp.sum(r.grad_proj[0].astype(F32), axis=0, keepdims=True)
         r.small[7:8, local : 2 * local] = jnp.sum(r.grad_proj[2].astype(F32), axis=0, keepdims=True)
         if not top:
-            make_fold("q", layer, QKV, r.part_q, r.gq, 3)
-            folds.begin(made_folds["q"])
+            make_fold("q", layer, QKV, r.part_q, r.gq, Q_)
 
     attention_backward_body(
         ring, gather, scatter, r.grad_hidden, r.x, lambda: r.vectors[layer, 0:1, :],
@@ -1324,6 +1343,7 @@
 
     small_pass = passing(r.small_go.at[0], r.small_land.at[0], 1)
     small_pass.start()
+    folds.round()
     small_pass.wait()
     r.small_go[1] = r.small_keep[...] + r.small_land[0]
 
@@ -1340,6 +1360,7 @@
             to_place(there, 1 + place, 1 + there).start()
 
     r.small_land[1 + place] = r.small_go[1]
+    folds.round()
     for there in range(count):
 
         @pl.when(there != place)
@@ -1358,12 +1379,13 @@
             device_id={TENSOR: device}, device_id_type=MESH,
         )
         hop.start()
+        folds.round()
         hop.wait()
         r.small_go[3 + step] = r.small_go[2 + step] + r.small_land[1 + count + step]
     r.small_out[0:6] = r.small_go[4, 0:6]
     r.small_out[6:8] = total[6:8]
 
-    q1_parts = folds.finish()
+    folds.finish()
     for copy in kept:
 
         @pl.when(section == 1)

time: 563 us -> 496 us (0.88)
  Pallas kernels: 535 us -> 468 us
    pallas_call x2, Pallas kernels: 312 us -> 245 us  [backward_call(): pl.pallas_call(functools.partial(backward_kernel, layer, top, names, None...]
where the time goes in v5:
time: 496 us; the launch traced here: 487 us
  Pallas kernels  468 us (94%)
  local copies, waits for them, and re-layouts  15.6 us (3%)
    pallas_call x2, Pallas kernels, backward_call(): pl.pallas_call(functools.partial(backward_kernel, layer, top, names, None...  245 us
    pallas_call x1, Pallas kernels, forward_call(): pl.pallas_call(functools.partial(forward_kernel, layers), out_shape=[jax....  223 us

profile of v5, /device:TPU:0, one launch (start us, length us, event | category | flops | bytes accessed | tf_op | source)
XLA Modules:
  0.0 487.3 jit_solution(13980641545604492200)
XLA Ops:
  0.6 0.0 copy-start
  0.7 0.0 copy-start.8
  0.7 0.0 copy-start.9
  0.7 0.0 copy-start.7
  0.7 1.2 copy-done
  1.9 0.8 dynamic-slice_bitcast_fusion.refs_0_.refs_1_
  2.7 0.7 broadcast_in_dim.32.refs_6_.refs_4_
  3.4 0.7 copy.30
  4.1 1.4 stack.7.refs_1_
  5.5 222.6 %forward.1 = (bf16[1024,1024]{1,0:T(8,128)(2,1)}, bf16[3,1024,256]{2,1,0:T(8,128)(2,1)}, bf16[1024,256]{1,0:T(8,128)(2,1)}, bf16[1024,1024]{1,0:T(8,128)(2,1)}, ...) custom-call(bf16[256,1024]{1,0:T(8,128)(2,1)} %dynamic-slice_bitcast, ...), custom_call_target="tpu_custom_call" | custom-call | tf_op jit(solution)/shard_map/forward/pallas_call | solution.py:936
  228.1 0.0 copy-done.8
  228.1 0.6 dynamic_slice.22
  228.7 0.0 copy-done.9
  228.7 1.3 fusion.1
  230.6 0.0 copy-done.7
  230.6 1.1 multiply_bitcast_fusion.refs_5_
  231.7 97.2 %backward_1.1 = (f32[256,1024]{1,0:T(8,128)}, f32[8,1024]{1,0:T(8,128)}, f32[256,1024]{1,0:T(8,128)}, f32[1024,256]{1,0:T(8,128)}, f32[256,256]{1,0:T(8,128)}, /...) custom-call(f32[256,1024]{1,0:T(8,128)} %get-tuple-element.54.refs_0_, ...), custom_call_target="tpu_custom_call" | custom-call | tf_op jit(solution)/shard_map/backward_1/pallas_call | solution.py:1488
  328.9 0.0 copy-start.2
  328.9 148.0 %backward_0.1 = (f32[256,1024]{1,0:T(8,128)}, f32[8,1024]{1,0:T(8,128)}, f32[256,1024]{1,0:T(8,128)}, f32[1024,256]{1,0:T(8,128)}, f32[256,256]{1,0:T(8,128)}, /...) custom-call(f32[256,1024]{1,0:T(8,128)} %get-tuple-element.70.refs_0_, ...), custom_call_target="tpu_custom_call" | custom-call | tf_op jit(solution)/shard_map/backward_0/pallas_call | solution.py:1488
  476.9 0.8 constant_dynamic-slice_fusion.2
  477.6 0.5 fusion.2
  478.2 0.8 slice.34
  478.9 0.6 constant_dynamic-slice_fusion
  479.5 0.7 slice_reduce_fusion
  480.3 0.0 copy-start.1
  480.3 0.6 fusion
  480.9 0.0 copy-done.2
  480.9 1.0 copy.37
  481.9 0.0 copy-done.1
  481.9 0.0 copy-start.5
  481.9 0.0 copy-start.6
  481.9 1.3 copy.38
  483.2 0.4 copy-done.5
  483.6 0.0 copy-start.4
  483.6 0.0 copy-start.3
  483.6 0.9 copy.39
  484.4 0.0 copy-done.6
  484.4 0.7 copy.40
  485.1 0.0 copy-done.4
  485.2 1.0 copy.41
  486.1 0.0 copy-done.3
  486.1 1.0 copy.42
  (3 shorter events, 0.0 us)
Async XLA Ops:
  0.6 1.2 copy-start
  0.7 227.4 %copy-start.8 = (s32[2]{0:T(128)S(1)}, s32[2]{0:T(128)}, u32[]{:S(2)}) copy-start(s32[2]{0:T(128)} %param.18) | copy-start | bytes 28
  0.7 228.0 %copy-start.9 = (s32[46]{0:T(128)S(1)}, s32[46]{0:T(128)}, u32[]{:S(2)}) copy-start(s32[46]{0:T(128)} %param.19) | copy-start | bytes 556
  0.7 230.0 %copy-start.7 = (bf16[2,256,1024]{2,1,0:T(8,128)(2,1)S(1)}, bf16[2,256,1024]{2,1,0:T(8,128)(2,1)}, u32[]{:S(2)}) copy-start(bf16[2,256,1024]{2,1,0:T(8,128)(2,1)} %param.17) | copy-start | bytes 3145732
  328.9 152.0 %copy-start.2 = (bf16[2,256,1024]{2,1,0:T(8,128)(2,1)S(1)}, bf16[2,256,1024]{2,1,0:T(8,128)(2,1)}, u32[]{:S(2)}) copy-start(bf16[2,256,1024]{2,1,0:T(8,128)(2,1)} %get-tuple-element.69) | copy-start | bytes 3145732
  480.3 1.6 copy-start.1
  481.9 1.7 copy-start.5
  481.9 2.6 copy-start.6
  483.6 1.6 copy-start.4
  483.6 2.6 copy-start.3

commit v6 on v5

--- a/solution.py
+++ b/solution.py
@@ -771,7 +771,8 @@
     pl.semaphore_wait(barrier, 3 + jnp.where(place > 0, 1, 0) + jnp.where(place + 1 < count, 1, 0))
 
 
-PUMP_POINTS = ({3: 4, 6: 5, 9: 6, 11: 7, 12: 8, 13: 9, 14: 10}, {})
+AHEAD = 5
+PUMP_POINTS = ({3: 6, 6: 7, 9: 8, 11: 9, 12: 10}, {})
 
 
 class Pump:
@@ -800,7 +801,7 @@
         self.until(PUMP_POINTS[layer].get(point, -1))
 
     def have(self, piece):
-        self.until(piece + self.hops - 1)
+        self.until(max(piece + self.hops - 1, AHEAD))
         crossing, i = self.pieces[piece]
         crossing.finish(i)
 
@@ -1148,8 +1149,8 @@
 
 
 D_, U_, O_, Q_, R_ = range(5)
-HIGH_PLAN = {4: ((D_, 0),), 7: ((U_, 0),), 8: ((D_, 1),), 9: ((D_, 2),), 10: ((O_, 0),), 12: ((D_, 3),), 14: ((U_, 1),), 15: ((D_, 4),), 17: ((U_, 2),), 18: ((U_, 3), (O_, 1)), 19: ((D_, 5), (U_, 4), (O_, 2)), 20: ((U_, 5), (O_, 3))}
-LOW_PLAN = {4: ((R_, 1), (D_, 0)), 5: ((R_, 2),), 6: ((R_, 3),), 7: ((R_, 4), (U_, 0)), 8: ((D_, 1),), 9: ((R_, 5), (D_, 2)), 10: ((O_, 0),), 12: ((D_, 3),), 14: ((U_, 1),), 15: ((D_, 4),), 17: ((U_, 2),), 18: ((U_, 3), (O_, 1), (Q_, 0)), 19: ((D_, 5), (U_, 4), (O_, 2)), 20: ((U_, 5), (O_, 3), (Q_, 1))}
+HIGH_PLAN = {4: ((D_, 0),), 7: ((U_, 0),), 8: ((D_, 1),), 9: ((D_, 2),), 10: ((O_, 0),), 12: ((D_, 3),), 14: ((U_, 1),), 15: ((D_, 4),), 17: ((U_, 2),), 18: ((U_, 3), (O_, 1)), 19: ((U_, 4), (O_, 2)), 20: ((O_, 3),)}
+LOW_PLAN = {4: ((R_, 1), (D_, 0)), 5: ((R_, 2),), 6: ((R_, 3),), 7: ((R_, 4), (U_, 0)), 8: ((D_, 1),), 9: ((D_, 2),), 12: ((D_, 3),), 14: ((U_, 1),), 15: ((D_, 4), (O_, 0)), 17: ((U_, 2),), 18: ((U_, 3), (Q_, 0)), 19: ((U_, 4), (O_, 1)), 20: ((O_, 2), (Q_, 1))}
 
 
 def fold_shapes(kind, count, width, local, units):
@@ -1234,10 +1235,6 @@
         r.rounded[...] = r.grads_out[1].astype(BF16)
         incoming = r.rounded
 
-        @pl.when(section == 0)
-        def _():
-            passing(r.rounded, r.grads_land, 0).start()
-
         for number, (src, dst) in enumerate(((r.gu_in, r.gu), (r.gd_in, r.gd), (r.go_in, r.go))):
             copy = pltpu.make_async_copy(src, dst, r.keep_sems.at[number])
             kept.append(copy)
@@ -1333,6 +1330,7 @@
     def _():
         r.small_go[0] = r.small_in[...]
         r.small_keep[...] = r.small[...]
+        passing(r.rounded, r.grads_land, 0).start()
 
     @pl.when(section == 1)
     def _():

time: 496 us -> 489 us (0.986)
  no operation moved by 1% of the time
where the time goes in v6:
time: 489 us; the launch traced here: 484 us
  Pallas kernels  464 us (95%)
  local copies, waits for them, and re-layouts  15.6 us (3%)
    pallas_call x2, Pallas kernels, backward_call(): pl.pallas_call(functools.partial(backward_kernel, layer, top, names, None...  241 us
    pallas_call x1, Pallas kernels, forward_call(): pl.pallas_call(functools.partial(forward_kernel, layers), out_shape=[jax....  224 us

profile of v6, /device:TPU:0, one launch (start us, length us, event | category | flops | bytes accessed | tf_op | source)
XLA Modules:
  0.0 483.9 jit_solution(4502555488249229234)
XLA Ops:
  0.6 0.0 copy-start
  0.7 0.0 copy-start.8
  0.7 0.0 copy-start.9
  0.7 0.0 copy-start.7
  0.7 1.2 copy-done
  1.9 0.8 dynamic-slice_bitcast_fusion.refs_0_.refs_1_
  2.7 0.7 broadcast_in_dim.32.refs_6_.refs_4_
  3.4 0.7 copy.30
  4.1 1.4 stack.7.refs_1_
  5.5 223.7 %forward.1 = (bf16[1024,1024]{1,0:T(8,128)(2,1)}, bf16[3,1024,256]{2,1,0:T(8,128)(2,1)}, bf16[1024,256]{1,0:T(8,128)(2,1)}, bf16[1024,1024]{1,0:T(8,128)(2,1)}, ...) custom-call(bf16[256,1024]{1,0:T(8,128)(2,1)} %dynamic-slice_bitcast, ...), custom_call_target="tpu_custom_call" | custom-call | tf_op jit(solution)/shard_map/forward/pallas_call | solution.py:937
  229.2 0.0 copy-done.8
  229.2 0.6 dynamic_slice.22
  229.8 0.0 copy-done.9
  229.8 1.3 fusion.1
  231.7 0.0 copy-done.7
  231.7 1.1 multiply_bitcast_fusion.refs_5_
  232.8 98.5 %backward_1.1 = (f32[256,1024]{1,0:T(8,128)}, f32[8,1024]{1,0:T(8,128)}, f32[256,1024]{1,0:T(8,128)}, f32[1024,256]{1,0:T(8,128)}, f32[256,256]{1,0:T(8,128)}, /...) custom-call(f32[256,1024]{1,0:T(8,128)} %get-tuple-element.54.refs_0_, ...), custom_call_target="tpu_custom_call" | custom-call | tf_op jit(solution)/shard_map/backward_1/pallas_call | solution.py:1486
  331.3 0.0 copy-start.2
  331.3 142.2 %backward_0.1 = (f32[256,1024]{1,0:T(8,128)}, f32[8,1024]{1,0:T(8,128)}, f32[256,1024]{1,0:T(8,128)}, f32[1024,256]{1,0:T(8,128)}, f32[256,256]{1,0:T(8,128)}, /...) custom-call(f32[256,1024]{1,0:T(8,128)} %get-tuple-element.70.refs_0_, ...), custom_call_target="tpu_custom_call" | custom-call | tf_op jit(solution)/shard_map/backward_0/pallas_call | solution.py:1486
  473.5 0.8 constant_dynamic-slice_fusion.2
  474.3 0.5 fusion.2
  474.8 0.8 slice.34
  475.6 0.6 constant_dynamic-slice_fusion
  476.1 0.7 slice_reduce_fusion
  476.9 0.0 copy-start.1
  476.9 0.6 fusion
  477.5 0.0 copy-done.2
  477.5 1.0 copy.37
  478.5 0.0 copy-done.1
  478.5 0.0 copy-start.5
  478.5 0.0 copy-start.6
  478.5 1.3 copy.38
  479.8 0.4 copy-done.5
  480.2 0.0 copy-start.4
  480.2 0.0 copy-start.3
  480.2 0.9 copy.39
  481.1 0.0 copy-done.6
  481.1 0.7 copy.40
  481.8 0.0 copy-done.4
  481.8 1.0 copy.41
  482.7 0.0 copy-done.3
  482.7 1.0 copy.42
  (3 shorter events, 0.0 us)
Async XLA Ops:
  0.6 1.2 copy-start
  0.7 228.5 %copy-start.8 = (s32[2]{0:T(128)S(1)}, s32[2]{0:T(128)}, u32[]{:S(2)}) copy-start(s32[2]{0:T(128)} %param.18) | copy-start | bytes 28
  0.7 229.1 %copy-start.9 = (s32[46]{0:T(128)S(1)}, s32[46]{0:T(128)}, u32[]{:S(2)}) copy-start(s32[46]{0:T(128)} %param.19) | copy-start | bytes 556
  0.7 231.1 %copy-start.7 = (bf16[2,256,1024]{2,1,0:T(8,128)(2,1)S(1)}, bf16[2,256,1024]{2,1,0:T(8,128)(2,1)}, u32[]{:S(2)}) copy-start(bf16[2,256,1024]{2,1,0:T(8,128)(2,1)} %param.17) | copy-start | bytes 3145732
  331.3 146.2 %copy-start.2 = (bf16[2,256,1024]{2,1,0:T(8,128)(2,1)S(1)}, bf16[2,256,1024]{2,1,0:T(8,128)(2,1)}, u32[]{:S(2)}) copy-start(bf16[2,256,1024]{2,1,0:T(8,128)(2,1)} %get-tuple-element.69) | copy-start | bytes 3145732
  476.9 1.6 copy-start.1
  478.5 1.7 copy-start.5
  478.5 2.6 copy-start.6
  480.2 1.6 copy-start.4
  480.2 2.6 copy-start.3

commit v7 on v6

--- a/solution.py
+++ b/solution.py
@@ -285,7 +285,7 @@
 def mlp_forward_body(
     ring, gather, scatter, middle, gain, shift, w_up, b_up, w_down, b_down,
     second, activated, slope_of, leaving, own,
-    ready=nothing, tick=nothing,
+    ready=nothing, tick=nothing, late=nothing,
 ):
     block, chunk = ring.block, ring.chunk
     for c in range(CHUNKS):
@@ -294,7 +294,7 @@
         second[ring.rows(ring.me, c)] = (unit * gain() + shift()).astype(BF16)
         gather.start(c)
 
-    def expand(at):
+    def widen(at):
         upward = mm(second[at], w_up[...]) + b_up()
         inner = jnp.tanh(GELU_SCALE * (upward + 0.044715 * upward * upward * upward))
         half = 0.5 * (1.0 + inner)
@@ -305,22 +305,42 @@
         value = value.astype(BF16)
         activated[at] = value
         slope_of[at] = slope.astype(BF16)
-        return mm(value, w_down[...])
+
+    def narrow(at):
+        return mm(activated[at], w_down[...])
+
+    def expand(at):
+        widen(at)
+        return narrow(at)
 
     tick(11)
     ready()
+    if late is not nothing:
+        widen(rows_at(ring.me * block, block))
+        for c in range(CHUNKS):
+            gather.arrived_mate(c)
+        widen(rows_at(ring.mate * block, block))
+        for c in range(CHUNKS):
+            gather.arrived_peer(c)
+            widen(ring.rows(ring.peer, c))
+            gather.arrived_far(c)
+            widen(ring.rows(ring.far, c))
+        late()
+        expand = narrow
     own[...] = expand(rows_at(ring.me * block, block))
     tick(12)
-    for c in range(CHUNKS):
+    for c in range(CHUNKS if late is nothing else 0):
         gather.arrived_mate(c)
     part = expand(rows_at(ring.mate * block, block))
     for c in range(CHUNKS):
         scatter.put(2, c, part[c * chunk : (c + 1) * chunk])
     tick(13)
     for c in range(CHUNKS):
-        gather.arrived_peer(c)
+        if late is nothing:
+            gather.arrived_peer(c)
         peer_part = expand(ring.rows(ring.peer, c))
-        gather.arrived_far(c)
+        if late is nothing:
+            gather.arrived_far(c)
         scatter.put(0, c, expand(ring.rows(ring.far, c)))
         scatter.put(1, c, peer_part + scatter.take(0, c))
         tick(14 + c)
@@ -894,12 +914,14 @@
 
         def ready():
             have(2)
-            have(3)
+            if l > 0:
+                have(3)
 
         mlp_forward_body(
             ring, gather, scatter, middle, row(3), row(4), wu, row(5), wd, row(6),
             second, activated, slope_of, leaving, own,
             ready=ready, tick=lambda point, l=l: pump.tick(l, point),
+            late=nothing if l > 0 else lambda: have(3),
         )
         save(l, 3, second)
         save(l, 4, activated)

time: 489 us -> 491 us (level)
  no operation moved by 1% of the time
where the time goes in v7:
time: 491 us; the launch traced here: 483 us
  Pallas kernels  463 us (94%)
  local copies, waits for them, and re-layouts  15.6 us (3%)
    pallas_call x2, Pallas kernels, backward_call(): pl.pallas_call(functools.partial(backward_kernel, layer, top, names, None...  243 us
    pallas_call x1, Pallas kernels, forward_call(): pl.pallas_call(functools.partial(forward_kernel, layers), out_shape=[jax....  220 us

profile of v7, /device:TPU:0, one launch (start us, length us, event | category | flops | bytes accessed | tf_op | source)
XLA Modules:
  0.0 483.1 jit_solution(2749273205049472223)
XLA Ops:
  0.6 0.0 copy-start
  0.7 0.0 copy-start.8
  0.7 0.0 copy-start.9
  0.7 0.0 copy-start.7
  0.7 1.2 copy-done
  1.9 0.8 dynamic-slice_bitcast_fusion.refs_0_.refs_1_
  2.7 0.7 broadcast_in_dim.32.refs_6_.refs_4_
  3.4 0.7 copy.30
  4.1 1.4 stack.7.refs_1_
  5.5 220.4 %forward.1 = (bf16[1024,1024]{1,0:T(8,128)(2,1)}, bf16[3,1024,256]{2,1,0:T(8,128)(2,1)}, bf16[1024,256]{1,0:T(8,128)(2,1)}, bf16[1024,1024]{1,0:T(8,128)(2,1)}, ...) custom-call(bf16[256,1024]{1,0:T(8,128)(2,1)} %dynamic-slice_bitcast, ...), custom_call_target="tpu_custom_call" | custom-call | tf_op jit(solution)/shard_map/forward/pallas_call | solution.py:959
  226.0 0.0 copy-done.8
  226.0 0.6 dynamic_slice.22
  226.6 0.0 copy-done.9
  226.6 1.3 fusion.1
  228.5 0.0 copy-done.7
  228.5 1.1 multiply_bitcast_fusion.refs_5_
  229.6 100.5 %backward_1.1 = (f32[256,1024]{1,0:T(8,128)}, f32[8,1024]{1,0:T(8,128)}, f32[256,1024]{1,0:T(8,128)}, f32[1024,256]{1,0:T(8,128)}, f32[256,256]{1,0:T(8,128)}, /...) custom-call(f32[256,1024]{1,0:T(8,128)} %get-tuple-element.54.refs_0_, ...), custom_call_target="tpu_custom_call" | custom-call | tf_op jit(solution)/shard_map/backward_1/pallas_call | solution.py:1508
  330.2 0.0 copy-start.2
  330.2 142.3 %backward_0.1 = (f32[256,1024]{1,0:T(8,128)}, f32[8,1024]{1,0:T(8,128)}, f32[256,1024]{1,0:T(8,128)}, f32[1024,256]{1,0:T(8,128)}, f32[256,256]{1,0:T(8,128)}, /...) custom-call(f32[256,1024]{1,0:T(8,128)} %get-tuple-element.70.refs_0_, ...), custom_call_target="tpu_custom_call" | custom-call | tf_op jit(solution)/shard_map/backward_0/pallas_call | solution.py:1508
  472.5 0.8 constant_dynamic-slice_fusion.2
  473.2 0.5 fusion.2
  473.8 0.8 slice.34
  474.5 0.6 constant_dynamic-slice_fusion
  475.1 0.7 slice_reduce_fusion
  475.8 0.0 copy-start.1
  475.9 0.6 fusion
  476.5 0.0 copy-done.2
  476.5 1.0 copy.37
  477.5 0.0 copy-done.1
  477.5 0.0 copy-start.5
  477.5 0.0 copy-start.6
  477.5 1.3 copy.38
  478.8 0.4 copy-done.5
  479.1 0.0 copy-start.4
  479.1 0.0 copy-start.3
  479.2 0.9 copy.39
  480.0 0.0 copy-done.6
  480.0 0.7 copy.40
  480.7 0.0 copy-done.4
  480.7 1.0 copy.41
  481.7 0.0 copy-done.3
  481.7 1.0 copy.42
  (3 shorter events, 0.0 us)
Async XLA Ops:
  0.6 1.2 copy-start
  0.7 225.3 %copy-start.8 = (s32[2]{0:T(128)S(1)}, s32[2]{0:T(128)}, u32[]{:S(2)}) copy-start(s32[2]{0:T(128)} %param.18) | copy-start | bytes 28
  0.7 225.9 %copy-start.9 = (s32[46]{0:T(128)S(1)}, s32[46]{0:T(128)}, u32[]{:S(2)}) copy-start(s32[46]{0:T(128)} %param.19) | copy-start | bytes 556
  0.7 227.8 %copy-start.7 = (bf16[2,256,1024]{2,1,0:T(8,128)(2,1)S(1)}, bf16[2,256,1024]{2,1,0:T(8,128)(2,1)}, u32[]{:S(2)}) copy-start(bf16[2,256,1024]{2,1,0:T(8,128)(2,1)} %param.17) | copy-start | bytes 3145732
  330.2 146.3 %copy-start.2 = (bf16[2,256,1024]{2,1,0:T(8,128)(2,1)S(1)}, bf16[2,256,1024]{2,1,0:T(8,128)(2,1)}, u32[]{:S(2)}) copy-start(bf16[2,256,1024]{2,1,0:T(8,128)(2,1)} %get-tuple-element.69) | copy-start | bytes 3145732
  475.8 1.6 copy-start.1
  477.5 1.7 copy-start.5
  477.5 2.6 copy-start.6
  479.1 1.6 copy-start.4
  479.1 2.6 copy-start.3
